TPU v7x, 256 devices: a whole 4x4x8 slice. The times are simulated.
256 devices in a mesh: grp: 2 (over core), zon: 16 (over z, y_hi), mer: 8 (over x, y_lo).
Axes of the slice: x: 4, y: 4 (y_hi: 2, y_lo: 2; y = y_hi * 2 + y_lo), z: 8, core: 2. Of those that a mesh axis runs over, the one named last changes fastest.
Arguments:
- model_state: float32 [4, 6, 512, 2048], P(None, 'grp', 'mer', 'zon'), may hold values from -4 to 4
- control: float32 [4, 6, 512, 2048], P('grp', None, 'mer', 'zon'), may hold values from -6 to 6
- error_std: float32 [4, 6, 512, 2048], P('grp', None, 'mer', 'zon'), may hold values from 0.3 to 3
- bottom_level: int32 [512, 2048], P('mer', 'zon'), may hold values from 0 to 6
- obs_count: int32 [2, 8, 16], P('grp', 'mer', 'zon'), may hold values from 1 to 256, as said below
- obs_corner: int32 [2, 8, 16, 256], P('grp', 'mer', 'zon'), may hold values from 0 to 98174, as said below
- obs_weight: float32 [2, 8, 16, 4, 256], P('grp', 'mer', 'zon'), may hold values from 0 to 1, as said below
- obs_value: float32 [2, 8, 16, 256], P('grp', 'mer', 'zon'), may hold values from -5 to 5
- obs_precision: float32 [2, 8, 16, 256], P('grp', 'mer', 'zon'), may hold values from 0.25 to 4
Outputs:
- gradient: float32 [4, 6, 512, 2048], P('grp', None, 'mer', 'zon')
Inputs may be any that keep to these rules, and one draw needn't show every extreme that they name: `obs_count`: at least one live observation in every block, exactly 256 in some block. `obs_corner`: each slot's four interpolation cells lie in its own tile; padded slots also hold valid indices. `obs_weight`: the four weights of a slot are nonnegative and sum to one.
All inputs are finite; a program needn't handle non-finite values.
Results may differ from a plain program's by a relative error of at most 0.0003.
Values may be sent and summed in bfloat16 or wider, within the bound.
No kernel may reach another device: no remote copies, remote signals or barrier semaphores. Data moves between devices by JAX's collectives and lax.ppermute only.
A program may use at most 64 MiB of HBM per device.

v0:
```python
import jax
import jax.numpy as jnp
from jax import lax
from jax.sharding import PartitionSpec as P

SWEEPS = 10


SMOOTHING = 0.2
ADVECTION = 0.1
MIXING = 0.15


def extended(value, sides, width):
    for axis, dim in sides:
        size, length = (lax.axis_size(axis), value.shape[dim])
        up = [(i, (i + 1) % size) for i in range(size)]
        down = [(j, i) for i, j in up]
        last = lax.slice_in_dim(value, length - width, length, axis=dim)
        first = lax.slice_in_dim(value, 0, width, axis=dim)
        before = lax.ppermute(last, axis, up)
        after = lax.ppermute(first, axis, down)
        value = jnp.concatenate([before, value, after], axis=dim)
    return value


def flux_sum(padded, mask_pad):
    centre = padded[..., 1:-1, 1:-1]
    summed = mask_pad[..., 1:-1, 2:] * (padded[..., 1:-1, 2:] - centre)
    summed = summed + mask_pad[..., 1:-1, :-2] * (padded[..., 1:-1, :-2] - centre)
    summed = summed + mask_pad[..., 2:, 1:-1] * (padded[..., 2:, 1:-1] - centre)
    summed = summed + mask_pad[..., :-2, 1:-1] * (padded[..., :-2, 1:-1] - centre)
    return mask_pad[..., 1:-1, 1:-1] * summed


def one_sweep(padded, mask_pad):
    return padded[..., 1:-1, 1:-1] + SMOOTHING * flux_sum(padded, mask_pad)


def smooth(field_stack, mask_one):

    def single(sweep_index, current):
        padded = extended(current, (("zon", 3), ("mer", 2)), 1)
        return one_sweep(padded, mask_one)

    return lax.fori_loop(0, SWEEPS, single, field_stack)


def body(
    model_state,
    control,
    error_std,
    bottom_level,
    obs_count,
    obs_corner,
    obs_weight,
    obs_value,
    obs_precision,
):
    level_count = control.shape[1]
    total_row_count = control.shape[2]
    column_count = control.shape[3]
    wet_mask = (lax.iota(jnp.int32, level_count)[:, None, None] < bottom_level[None]).astype(
        jnp.float32
    )
    land_ext = extended(wet_mask.astype(jnp.bfloat16), (("zon", 2), ("mer", 1)), 2).astype(
        jnp.float32
    )
    mer_index = lax.axis_index("mer")
    mer_count = lax.axis_size("mer")
    row_ids = lax.iota(jnp.int32, total_row_count + 4)
    cut_rows = (mer_index == 0) & (row_ids < 2) | (mer_index == mer_count - 1) & (
        row_ids >= total_row_count + 2
    )
    mask_two = land_ext * jnp.logical_not(cut_rows).astype(jnp.float32)[None, :, None]
    mask_one = mask_two[:, 1:-1, 1:-1]
    half_levels = model_state.shape[1]
    group_index = lax.axis_index("grp")
    depth_level_mask = lax.dynamic_slice_in_dim(mask_one, group_index * half_levels, half_levels, 0)
    padded = extended(model_state, (("zon", 3), ("mer", 2)), 1)
    masked = padded * depth_level_mask
    centre = padded[..., 1:-1, 1:-1]
    grad_x = 0.5 * (masked[..., 1:-1, 2:] - masked[..., 1:-1, :-2])
    grad_y = 0.5 * (masked[..., 2:, 1:-1] - masked[..., :-2, 1:-1])
    shifted_values = (
        centre
        - ADVECTION * (centre[2] * grad_x + centre[3] * grad_y)
        + MIXING * flux_sum(padded, depth_level_mask)
    )
    predicted_state = depth_level_mask[:, 1:-1, 1:-1] * shifted_values
    offsets = jnp.array([0, 1, column_count, column_count + 1], jnp.int32)
    corners = obs_corner.reshape(1, -1) + offsets[:, None]
    weights = obs_weight.reshape(4, -1)
    live_slot = (lax.iota(jnp.int32, weights.shape[1]) < obs_count.reshape(())).astype(jnp.float32)
    values_seen = obs_value.reshape(-1)
    precision = obs_precision.reshape(-1)

    def observe(field_stack):
        return jnp.sum(weights * field_stack.reshape(-1)[corners], axis=0)

    prior_estimate = lax.all_to_all(predicted_state, "grp", split_axis=0, concat_axis=1, tiled=True)
    seen_background = observe(prior_estimate)
    innovation = live_slot * (values_seen - seen_background)
    increment = wet_mask * error_std * smooth(control, mask_one)
    misfit = live_slot * precision * (observe(increment) - innovation)
    adjoint_obs = (
        jnp.zeros((control.size,), jnp.float32)
        .at[corners.reshape(-1)]
        .add((weights * misfit[None, :]).reshape(-1))
    )
    adjoint_obs = adjoint_obs.reshape(control.shape)
    return control + smooth(wet_mask * error_std * adjoint_obs, mask_one)


def solution(mesh):
    return jax.shard_map(
        body,
        mesh=mesh,
        in_specs=(
            P(None, "grp", "mer", "zon"),
            P("grp", None, "mer", "zon"),
            P("grp", None, "mer", "zon"),
            P("mer", "zon"),
            P("grp", "mer", "zon"),
            P("grp", "mer", "zon", None),
            P("grp", "mer", "zon", None, None),
            P("grp", "mer", "zon", None),
            P("grp", "mer", "zon", None),
        ),
        out_specs=P("grp", None, "mer", "zon"),
        check_vma=False,
    )
```

profile of v0, /device:TPU:1, one launch (start us, length us, event | category | flops | bytes accessed | tf_op | source)
XLA Modules:
  0.0 604.0 jit_solution(13794020824772804791)
XLA Ops:
  5.4 5.4 collective-permute-start.9
  11.1 5.1 collective-permute-start.13
  22.3 5.4 collective-permute-done.12
  36.6 267.5 %while.20 = (s32[]{:T(128)}, f32[2,6,64,128]{3,2,1,0:T(8,128)S(1)}, f32[6,66,130]{2,1,0:T(8,128)S(1)}, s32[]{:T(128)}) while((s32[]{:T(128)}, f32[2,6,64,128]{3,2,1,0:T(8,128)S(1)}, f32[6,66,130]{2,1,0:T(8,128)S(1)}, s32[]{:T(128)}) %tuple.73), condition=%wide.region_1.0_spmd, body=%wide.region_0.0_spmd.sunk | while | flops 2168930 | bytes 5039445 | solution.py:46
  41.6 6.7 %collective-permute-done = f32[2,6,64,1]{3,2,1,0:T(8,128)S(1)} collective-permute-done((f32[2,6,64,1]{3,2,1,0:T(8,128)S(1)}, f32[2,6,64,1]{3,2,1,0:T(8,128)S(1)}, u32[]{:S(2)}, u32[]{:S(2)}) %collective-permute-start) | collective-permute-done | bytes 3104 | tf_op jit(solution)/shard_map/while/body/eval_jaxpr/ppermute | solution.py:22
  48.3 7.2 %collective-permute-done.1 = f32[2,6,64,1]{3,2,1,0:T(8,128)S(1)} collective-permute-done((f32[2,6,64,1]{3,2,1,0:T(8,128)S(1)}, f32[2,6,64,1]{3,2,1,0:T(8,128)S(1)}, u32[]{:S(2)}, u32[]{:S(2)}) %collective-permute-start.1) | collective-permute-done | bytes 3104 | tf_op jit(solution)/shard_map/while/body/eval_jaxpr/ppermute | solution.py:21
  61.3 8.3 %collective-permute-start = (f32[2,6,64,1]{3,2,1,0:T(8,128)S(1)}, f32[2,6,64,1]{3,2,1,0:T(8,128)S(1)}, u32[]{:S(2)}, u32[]{:S(2)}) collective-permute-start(f32[2,6,64,1]{3,2,1,0:T(8,128)S(1)} %get-tuple-element.143), channel_id=1, source_target_pairs={{8,0},{16,8},{24,16},{32,24},{40,32},{48,40},{56,48},{64,56},{72,6... | collective-permute-start | bytes 9224 | tf_op jit(solution)/shard_map/while/body/eval_jaxpr/ppermute | solution.py:22
  69.6 6.4 %collective-permute-done = f32[2,6,64,1]{3,2,1,0:T(8,128)S(1)} collective-permute-done((f32[2,6,64,1]{3,2,1,0:T(8,128)S(1)}, f32[2,6,64,1]{3,2,1,0:T(8,128)S(1)}, u32[]{:S(2)}, u32[]{:S(2)}) %collective-permute-start) | collective-permute-done | bytes 3104 | tf_op jit(solution)/shard_map/while/body/eval_jaxpr/ppermute | solution.py:22
  75.9 7.3 %collective-permute-done.1 = f32[2,6,64,1]{3,2,1,0:T(8,128)S(1)} collective-permute-done((f32[2,6,64,1]{3,2,1,0:T(8,128)S(1)}, f32[2,6,64,1]{3,2,1,0:T(8,128)S(1)}, u32[]{:S(2)}, u32[]{:S(2)}) %collective-permute-start.1) | collective-permute-done | bytes 3104 | tf_op jit(solution)/shard_map/while/body/eval_jaxpr/ppermute | solution.py:21
  89.0 5.7 collective-permute-start
  94.7 5.5 collective-permute-done
  100.2 10.8 %collective-permute-done.1 = f32[2,6,64,1]{3,2,1,0:T(8,128)S(1)} collective-permute-done((f32[2,6,64,1]{3,2,1,0:T(8,128)S(1)}, f32[2,6,64,1]{3,2,1,0:T(8,128)S(1)}, u32[]{:S(2)}, u32[]{:S(2)}) %collective-permute-start.1) | collective-permute-done | bytes 3104 | tf_op jit(solution)/shard_map/while/body/eval_jaxpr/ppermute | solution.py:21
  116.7 6.5 %collective-permute-start = (f32[2,6,64,1]{3,2,1,0:T(8,128)S(1)}, f32[2,6,64,1]{3,2,1,0:T(8,128)S(1)}, u32[]{:S(2)}, u32[]{:S(2)}) collective-permute-start(f32[2,6,64,1]{3,2,1,0:T(8,128)S(1)} %get-tuple-element.143), channel_id=1, source_target_pairs={{8,0},{16,8},{24,16},{32,24},{40,32},{48,40},{56,48},{64,56},{72,6... | collective-permute-start | bytes 9224 | tf_op jit(solution)/shard_map/while/body/eval_jaxpr/ppermute | solution.py:22
  123.2 6.7 %collective-permute-done = f32[2,6,64,1]{3,2,1,0:T(8,128)S(1)} collective-permute-done((f32[2,6,64,1]{3,2,1,0:T(8,128)S(1)}, f32[2,6,64,1]{3,2,1,0:T(8,128)S(1)}, u32[]{:S(2)}, u32[]{:S(2)}) %collective-permute-start) | collective-permute-done | bytes 3104 | tf_op jit(solution)/shard_map/while/body/eval_jaxpr/ppermute | solution.py:22
  129.9 8.8 %collective-permute-done.1 = f32[2,6,64,1]{3,2,1,0:T(8,128)S(1)} collective-permute-done((f32[2,6,64,1]{3,2,1,0:T(8,128)S(1)}, f32[2,6,64,1]{3,2,1,0:T(8,128)S(1)}, u32[]{:S(2)}, u32[]{:S(2)}) %collective-permute-start.1) | collective-permute-done | bytes 3104 | tf_op jit(solution)/shard_map/while/body/eval_jaxpr/ppermute | solution.py:21
  148.5 16.2 %collective-permute-done = f32[2,6,64,1]{3,2,1,0:T(8,128)S(1)} collective-permute-done((f32[2,6,64,1]{3,2,1,0:T(8,128)S(1)}, f32[2,6,64,1]{3,2,1,0:T(8,128)S(1)}, u32[]{:S(2)}, u32[]{:S(2)}) %collective-permute-start) | collective-permute-done | bytes 3104 | tf_op jit(solution)/shard_map/while/body/eval_jaxpr/ppermute | solution.py:22
  175.5 5.6 collective-permute-done
  181.1 11.5 %collective-permute-done.1 = f32[2,6,64,1]{3,2,1,0:T(8,128)S(1)} collective-permute-done((f32[2,6,64,1]{3,2,1,0:T(8,128)S(1)}, f32[2,6,64,1]{3,2,1,0:T(8,128)S(1)}, u32[]{:S(2)}, u32[]{:S(2)}) %collective-permute-start.1) | collective-permute-done | bytes 3104 | tf_op jit(solution)/shard_map/while/body/eval_jaxpr/ppermute | solution.py:21
  202.4 16.1 %collective-permute-done = f32[2,6,64,1]{3,2,1,0:T(8,128)S(1)} collective-permute-done((f32[2,6,64,1]{3,2,1,0:T(8,128)S(1)}, f32[2,6,64,1]{3,2,1,0:T(8,128)S(1)}, u32[]{:S(2)}, u32[]{:S(2)}) %collective-permute-start) | collective-permute-done | bytes 3104 | tf_op jit(solution)/shard_map/while/body/eval_jaxpr/ppermute | solution.py:22
  228.4 14.9 %collective-permute-done = f32[2,6,64,1]{3,2,1,0:T(8,128)S(1)} collective-permute-done((f32[2,6,64,1]{3,2,1,0:T(8,128)S(1)}, f32[2,6,64,1]{3,2,1,0:T(8,128)S(1)}, u32[]{:S(2)}, u32[]{:S(2)}) %collective-permute-start) | collective-permute-done | bytes 3104 | tf_op jit(solution)/shard_map/while/body/eval_jaxpr/ppermute | solution.py:22
  254.4 15.0 %collective-permute-done = f32[2,6,64,1]{3,2,1,0:T(8,128)S(1)} collective-permute-done((f32[2,6,64,1]{3,2,1,0:T(8,128)S(1)}, f32[2,6,64,1]{3,2,1,0:T(8,128)S(1)}, u32[]{:S(2)}, u32[]{:S(2)}) %collective-permute-start) | collective-permute-done | bytes 3104 | tf_op jit(solution)/shard_map/while/body/eval_jaxpr/ppermute | solution.py:22
  276.5 5.0 collective-permute-start
  281.5 6.9 %collective-permute-done = f32[2,6,64,1]{3,2,1,0:T(8,128)S(1)} collective-permute-done((f32[2,6,64,1]{3,2,1,0:T(8,128)S(1)}, f32[2,6,64,1]{3,2,1,0:T(8,128)S(1)}, u32[]{:S(2)}, u32[]{:S(2)}) %collective-permute-start) | collective-permute-done | bytes 3104 | tf_op jit(solution)/shard_map/while/body/eval_jaxpr/ppermute | solution.py:22
  288.4 10.1 %collective-permute-done.1 = f32[2,6,64,1]{3,2,1,0:T(8,128)S(1)} collective-permute-done((f32[2,6,64,1]{3,2,1,0:T(8,128)S(1)}, f32[2,6,64,1]{3,2,1,0:T(8,128)S(1)}, u32[]{:S(2)}, u32[]{:S(2)}) %collective-permute-start.1) | collective-permute-done | bytes 3104 | tf_op jit(solution)/shard_map/while/body/eval_jaxpr/ppermute | solution.py:21
  305.2 6.2 %gather_fusion = f32[1024]{0:T(1024)S(1)} fusion(f32[98304]{0:T(1024)S(1)} %bitcast.37, s32[1024]{0:T(1024)S(1)} %broadcast_clamp_fusion), kind=kCustom, calls=%fused_computation | custom fusion | bytes 12288 | tf_op jit(solution)/shard_map/gather | solution.py:99
  313.4 5.3 all_to_all.15
  318.8 6.2 %gather_fusion.1 = f32[1024]{0:T(1024)S(1)} fusion(f32[98304]{0:T(1024)S(1)} %bitcast.38, s32[1024]{0:T(1024)S(1)} %broadcast_clamp_fusion), kind=kCustom, calls=%fused_computation.1 | custom fusion | bytes 12288 | tf_op jit(solution)/shard_map/gather | solution.py:99
  325.7 6.2 %scatter_custom_fusion = f32[98304]{0:T(1024)S(1)} fusion(s32[1024]{0:T(1024)S(1)} %bitcast.46, f32[1024]{0:T(1024)S(1)} %mul.278, f32[]{:T(128)} %constant.27.clone.1), kind=kCustom, calls=%fused_computation.91 | custom fusion | flops 1024 | bytes 393220 | tf_op jit(solution)/shard_map/scatter-add | solution.py:109
  332.1 271.1 %while.21 = (s32[]{:T(128)}, f32[2,6,64,128]{3,2,1,0:T(8,128)S(1)}, f32[6,66,130]{2,1,0:T(8,128)S(1)}, s32[]{:T(128)}) while((s32[]{:T(128)}, f32[2,6,64,128]{3,2,1,0:T(8,128)S(1)}, f32[6,66,130]{2,1,0:T(8,128)S(1)}, s32[]{:T(128)}) %tuple.72), condition=%wide.region_6.0_spmd, body=%wide.region_5.0_spmd.sunk | while | flops 2168930 | bytes 5039445 | solution.py:46
  332.3 5.7 collective-permute-start.4
  338.0 15.7 %collective-permute-done.4 = f32[2,6,64,1]{3,2,1,0:T(8,128)S(1)} collective-permute-done((f32[2,6,64,1]{3,2,1,0:T(8,128)S(1)}, f32[2,6,64,1]{3,2,1,0:T(8,128)S(1)}, u32[]{:S(2)}, u32[]{:S(2)}) %collective-permute-start.4) | collective-permute-done | bytes 3104 | tf_op jit(solution)/shard_map/while/body/eval_jaxpr/ppermute | solution.py:22
  360.0 5.2 collective-permute-start.4
  365.2 15.3 %collective-permute-done.4 = f32[2,6,64,1]{3,2,1,0:T(8,128)S(1)} collective-permute-done((f32[2,6,64,1]{3,2,1,0:T(8,128)S(1)}, f32[2,6,64,1]{3,2,1,0:T(8,128)S(1)}, u32[]{:S(2)}, u32[]{:S(2)}) %collective-permute-start.4) | collective-permute-done | bytes 3104 | tf_op jit(solution)/shard_map/while/body/eval_jaxpr/ppermute | solution.py:22
  388.0 5.4 collective-permute-start.4
  393.3 6.3 %collective-permute-done.4 = f32[2,6,64,1]{3,2,1,0:T(8,128)S(1)} collective-permute-done((f32[2,6,64,1]{3,2,1,0:T(8,128)S(1)}, f32[2,6,64,1]{3,2,1,0:T(8,128)S(1)}, u32[]{:S(2)}, u32[]{:S(2)}) %collective-permute-start.4) | collective-permute-done | bytes 3104 | tf_op jit(solution)/shard_map/while/body/eval_jaxpr/ppermute | solution.py:22
  399.6 10.3 %collective-permute-done.5 = f32[2,6,64,1]{3,2,1,0:T(8,128)S(1)} collective-permute-done((f32[2,6,64,1]{3,2,1,0:T(8,128)S(1)}, f32[2,6,64,1]{3,2,1,0:T(8,128)S(1)}, u32[]{:S(2)}, u32[]{:S(2)}) %collective-permute-start.5) | collective-permute-done | bytes 3104 | tf_op jit(solution)/shard_map/while/body/eval_jaxpr/ppermute | solution.py:21
  419.8 16.1 %collective-permute-done.4 = f32[2,6,64,1]{3,2,1,0:T(8,128)S(1)} collective-permute-done((f32[2,6,64,1]{3,2,1,0:T(8,128)S(1)}, f32[2,6,64,1]{3,2,1,0:T(8,128)S(1)}, u32[]{:S(2)}, u32[]{:S(2)}) %collective-permute-start.4) | collective-permute-done | bytes 3104 | tf_op jit(solution)/shard_map/while/body/eval_jaxpr/ppermute | solution.py:22
  441.9 5.0 collective-permute-start.4
  447.0 6.7 %collective-permute-done.4 = f32[2,6,64,1]{3,2,1,0:T(8,128)S(1)} collective-permute-done((f32[2,6,64,1]{3,2,1,0:T(8,128)S(1)}, f32[2,6,64,1]{3,2,1,0:T(8,128)S(1)}, u32[]{:S(2)}, u32[]{:S(2)}) %collective-permute-start.4) | collective-permute-done | bytes 3104 | tf_op jit(solution)/shard_map/while/body/eval_jaxpr/ppermute | solution.py:22
  453.7 10.2 %collective-permute-done.5 = f32[2,6,64,1]{3,2,1,0:T(8,128)S(1)} collective-permute-done((f32[2,6,64,1]{3,2,1,0:T(8,128)S(1)}, f32[2,6,64,1]{3,2,1,0:T(8,128)S(1)}, u32[]{:S(2)}, u32[]{:S(2)}) %collective-permute-start.5) | collective-permute-done | bytes 3104 | tf_op jit(solution)/shard_map/while/body/eval_jaxpr/ppermute | solution.py:21
  473.5 16.0 %collective-permute-done.4 = f32[2,6,64,1]{3,2,1,0:T(8,128)S(1)} collective-permute-done((f32[2,6,64,1]{3,2,1,0:T(8,128)S(1)}, f32[2,6,64,1]{3,2,1,0:T(8,128)S(1)}, u32[]{:S(2)}, u32[]{:S(2)}) %collective-permute-start.4) | collective-permute-done | bytes 3104 | tf_op jit(solution)/shard_map/while/body/eval_jaxpr/ppermute | solution.py:22
  499.6 15.1 %collective-permute-done.4 = f32[2,6,64,1]{3,2,1,0:T(8,128)S(1)} collective-permute-done((f32[2,6,64,1]{3,2,1,0:T(8,128)S(1)}, f32[2,6,64,1]{3,2,1,0:T(8,128)S(1)}, u32[]{:S(2)}, u32[]{:S(2)}) %collective-permute-start.4) | collective-permute-done | bytes 3104 | tf_op jit(solution)/shard_map/while/body/eval_jaxpr/ppermute | solution.py:22
  525.7 15.1 %collective-permute-done.4 = f32[2,6,64,1]{3,2,1,0:T(8,128)S(1)} collective-permute-done((f32[2,6,64,1]{3,2,1,0:T(8,128)S(1)}, f32[2,6,64,1]{3,2,1,0:T(8,128)S(1)}, u32[]{:S(2)}, u32[]{:S(2)}) %collective-permute-start.4) | collective-permute-done | bytes 3104 | tf_op jit(solution)/shard_map/while/body/eval_jaxpr/ppermute | solution.py:22
  547.9 5.2 collective-permute-start.4
  553.0 6.9 %collective-permute-done.4 = f32[2,6,64,1]{3,2,1,0:T(8,128)S(1)} collective-permute-done((f32[2,6,64,1]{3,2,1,0:T(8,128)S(1)}, f32[2,6,64,1]{3,2,1,0:T(8,128)S(1)}, u32[]{:S(2)}, u32[]{:S(2)}) %collective-permute-start.4) | collective-permute-done | bytes 3104 | tf_op jit(solution)/shard_map/while/body/eval_jaxpr/ppermute | solution.py:22
  559.9 9.9 %collective-permute-done.5 = f32[2,6,64,1]{3,2,1,0:T(8,128)S(1)} collective-permute-done((f32[2,6,64,1]{3,2,1,0:T(8,128)S(1)}, f32[2,6,64,1]{3,2,1,0:T(8,128)S(1)}, u32[]{:S(2)}, u32[]{:S(2)}) %collective-permute-start.5) | collective-permute-done | bytes 3104 | tf_op jit(solution)/shard_map/while/body/eval_jaxpr/ppermute | solution.py:21
  575.5 5.0 collective-permute-start.4
  580.5 15.3 %collective-permute-done.4 = f32[2,6,64,1]{3,2,1,0:T(8,128)S(1)} collective-permute-done((f32[2,6,64,1]{3,2,1,0:T(8,128)S(1)}, f32[2,6,64,1]{3,2,1,0:T(8,128)S(1)}, u32[]{:S(2)}, u32[]{:S(2)}) %collective-permute-start.4) | collective-permute-done | bytes 3104 | tf_op jit(solution)/shard_map/while/body/eval_jaxpr/ppermute | solution.py:22
  (305 shorter events, 190.7 us)
Async XLA Ops:
  1.6 16.9 %collective-permute-start.8 = (bf16[6,64,2]{2,1,0:T(8,128)(2,1)S(1)}, bf16[6,64,2]{2,1,0:T(8,128)(2,1)S(1)}, u32[]{:S(2)}, u32[]{:S(2)}) collective-permute-start(bf16[6,64,2]{2,1,0:T(8,128)(2,1)S(1)} %get-tuple-element.86), channel_id=1, source_target_pairs={{0,8},{8,16},{16,24},{24,32},{32,40},{40,48},{48,56},{56,64},{64,7... | collective-permute-start | bytes 4616 | tf_op jit(solution)/shard_map/ppermute | solution.py:21
  5.4 13.1 %collective-permute-start.9 = (bf16[6,64,2]{2,1,0:T(8,128)(2,1)S(1)}, bf16[6,64,2]{2,1,0:T(8,128)(2,1)S(1)}, u32[]{:S(2)}, u32[]{:S(2)}) collective-permute-start(bf16[6,64,2]{2,1,0:T(8,128)(2,1)S(1)} %get-tuple-element.87), channel_id=1, source_target_pairs={{8,0},{16,8},{24,16},{32,24},{40,32},{48,40},{56,48},{64,56},{72,6... | collective-permute-start | bytes 4616 | tf_op jit(solution)/shard_map/ppermute | solution.py:22
  11.0 16.7 %collective-permute-start.12 = (f32[4,3,64,1]{3,2,1,0:T(8,128)S(1)}, f32[4,3,64,1]{3,2,1,0:T(8,128)S(1)}, u32[]{:S(2)}, u32[]{:S(2)}) collective-permute-start(f32[4,3,64,1]{3,2,1,0:T(8,128)S(1)} %get-tuple-element.82), channel_id=1, source_target_pairs={{0,8},{8,16},{16,24},{24,32},{32,40},{40,48},{48,56},{56,64},{64,7... | collective-permute-start | bytes 9224 | tf_op jit(solution)/shard_map/ppermute | solution.py:21
  11.1 19.8 %collective-permute-start.13 = (f32[4,3,64,1]{3,2,1,0:T(8,128)S(1)}, f32[4,3,64,1]{3,2,1,0:T(8,128)S(1)}, u32[]{:S(2)}, u32[]{:S(2)}) collective-permute-start(f32[4,3,64,1]{3,2,1,0:T(8,128)S(1)} %get-tuple-element.83), channel_id=1, source_target_pairs={{8,0},{16,8},{24,16},{32,24},{40,32},{48,40},{56,48},{64,56},{72,6... | collective-permute-start | bytes 9224 | tf_op jit(solution)/shard_map/ppermute | solution.py:22
  18.6 16.7 %collective-permute-start.10 = (bf16[6,2,132]{2,1,0:T(2,128)(2,1)S(1)}, bf16[6,2,132]{2,1,0:T(2,128)(2,1)S(1)}, u32[]{:S(2)}, u32[]{:S(2)}) collective-permute-start(bf16[6,2,132]{2,1,0:T(2,128)(2,1)S(1)} %get-tuple-element.84), channel_id=1, source_target_pairs={{0,1},{1,2},{2,3},{3,4},{4,5},{5,6},{6,7},{7,0},{8,9},{9,10},{10,1... | collective-permute-start | bytes 9512 | tf_op jit(solution)/shard_map/ppermute | solution.py:21
  19.1 16.2 %collective-permute-start.11 = (bf16[6,2,132]{2,1,0:T(2,128)(2,1)S(1)}, bf16[6,2,132]{2,1,0:T(2,128)(2,1)S(1)}, u32[]{:S(2)}, u32[]{:S(2)}) collective-permute-start(bf16[6,2,132]{2,1,0:T(2,128)(2,1)S(1)} %get-tuple-element.85), channel_id=1, source_target_pairs={{1,0},{2,1},{3,2},{4,3},{5,4},{6,5},{7,6},{0,7},{9,8},{10,9},{11,1... | collective-permute-start | bytes 9512 | tf_op jit(solution)/shard_map/ppermute | solution.py:22
  31.7 279.7 %collective-permute-start.14 = (f32[4,3,1,130]{3,2,1,0:T(1,128)}, f32[4,3,1,130]{3,2,1,0:T(1,128)S(1)}, u32[]{:S(2)}, u32[]{:S(2)}) collective-permute-start(f32[4,3,1,130]{3,2,1,0:T(1,128)} %get-tuple-element.74), channel_id=1, source_target_pairs={{0,1},{1,2},{2,3},{3,4},{4,5},{5,6},{6,7},{7,0},{8,9},{9,10},{10,1... | collective-permute-start | bytes 18728 | tf_op jit(solution)/shard_map/ppermute | solution.py:21
  32.1 279.4 %collective-permute-start.15 = (f32[4,3,1,130]{3,2,1,0:T(1,128)}, f32[4,3,1,130]{3,2,1,0:T(1,128)S(1)}, u32[]{:S(2)}, u32[]{:S(2)}) collective-permute-start(f32[4,3,1,130]{3,2,1,0:T(1,128)} %get-tuple-element.73), channel_id=1, source_target_pairs={{1,0},{2,1},{3,2},{4,3},{5,4},{6,5},{7,6},{0,7},{9,8},{10,9},{11,1... | collective-permute-start | bytes 18728 | tf_op jit(solution)/shard_map/ppermute | solution.py:22
  36.8 11.5 %collective-permute-start = (f32[2,6,64,1]{3,2,1,0:T(8,128)S(1)}, f32[2,6,64,1]{3,2,1,0:T(8,128)S(1)}, u32[]{:S(2)}, u32[]{:S(2)}) collective-permute-start(f32[2,6,64,1]{3,2,1,0:T(8,128)S(1)} %get-tuple-element.143), channel_id=1, source_target_pairs={{8,0},{16,8},{24,16},{32,24},{40,32},{48,40},{56,48},{64,56},{72,6... | collective-permute-start | bytes 9224 | tf_op jit(solution)/shard_map/while/body/eval_jaxpr/ppermute | solution.py:22
  41.6 14.0 %collective-permute-start.1 = (f32[2,6,64,1]{3,2,1,0:T(8,128)S(1)}, f32[2,6,64,1]{3,2,1,0:T(8,128)S(1)}, u32[]{:S(2)}, u32[]{:S(2)}) collective-permute-start(f32[2,6,64,1]{3,2,1,0:T(8,128)S(1)} %get-tuple-element.144), channel_id=1, source_target_pairs={{0,8},{8,16},{16,24},{24,32},{32,40},{40,48},{48,56},{56,64},{64,7... | collective-permute-start | bytes 9224 | tf_op jit(solution)/shard_map/while/body/eval_jaxpr/ppermute | solution.py:21
  61.3 14.7 %collective-permute-start = (f32[2,6,64,1]{3,2,1,0:T(8,128)S(1)}, f32[2,6,64,1]{3,2,1,0:T(8,128)S(1)}, u32[]{:S(2)}, u32[]{:S(2)}) collective-permute-start(f32[2,6,64,1]{3,2,1,0:T(8,128)S(1)} %get-tuple-element.143), channel_id=1, source_target_pairs={{8,0},{16,8},{24,16},{32,24},{40,32},{48,40},{56,48},{64,56},{72,6... | collective-permute-start | bytes 9224 | tf_op jit(solution)/shard_map/while/body/eval_jaxpr/ppermute | solution.py:22
  69.6 13.7 %collective-permute-start.1 = (f32[2,6,64,1]{3,2,1,0:T(8,128)S(1)}, f32[2,6,64,1]{3,2,1,0:T(8,128)S(1)}, u32[]{:S(2)}, u32[]{:S(2)}) collective-permute-start(f32[2,6,64,1]{3,2,1,0:T(8,128)S(1)} %get-tuple-element.144), channel_id=1, source_target_pairs={{0,8},{8,16},{16,24},{24,32},{32,40},{40,48},{48,56},{56,64},{64,7... | collective-permute-start | bytes 9224 | tf_op jit(solution)/shard_map/while/body/eval_jaxpr/ppermute | solution.py:21
  89.0 11.2 %collective-permute-start = (f32[2,6,64,1]{3,2,1,0:T(8,128)S(1)}, f32[2,6,64,1]{3,2,1,0:T(8,128)S(1)}, u32[]{:S(2)}, u32[]{:S(2)}) collective-permute-start(f32[2,6,64,1]{3,2,1,0:T(8,128)S(1)} %get-tuple-element.143), channel_id=1, source_target_pairs={{8,0},{16,8},{24,16},{32,24},{40,32},{48,40},{56,48},{64,56},{72,6... | collective-permute-start | bytes 9224 | tf_op jit(solution)/shard_map/while/body/eval_jaxpr/ppermute | solution.py:22
  94.7 16.3 %collective-permute-start.1 = (f32[2,6,64,1]{3,2,1,0:T(8,128)S(1)}, f32[2,6,64,1]{3,2,1,0:T(8,128)S(1)}, u32[]{:S(2)}, u32[]{:S(2)}) collective-permute-start(f32[2,6,64,1]{3,2,1,0:T(8,128)S(1)} %get-tuple-element.144), channel_id=1, source_target_pairs={{0,8},{8,16},{16,24},{24,32},{32,40},{40,48},{48,56},{56,64},{64,7... | collective-permute-start | bytes 9224 | tf_op jit(solution)/shard_map/while/body/eval_jaxpr/ppermute | solution.py:21
  116.7 13.2 %collective-permute-start = (f32[2,6,64,1]{3,2,1,0:T(8,128)S(1)}, f32[2,6,64,1]{3,2,1,0:T(8,128)S(1)}, u32[]{:S(2)}, u32[]{:S(2)}) collective-permute-start(f32[2,6,64,1]{3,2,1,0:T(8,128)S(1)} %get-tuple-element.143), channel_id=1, source_target_pairs={{8,0},{16,8},{24,16},{32,24},{40,32},{48,40},{56,48},{64,56},{72,6... | collective-permute-start | bytes 9224 | tf_op jit(solution)/shard_map/while/body/eval_jaxpr/ppermute | solution.py:22
  123.2 15.5 %collective-permute-start.1 = (f32[2,6,64,1]{3,2,1,0:T(8,128)S(1)}, f32[2,6,64,1]{3,2,1,0:T(8,128)S(1)}, u32[]{:S(2)}, u32[]{:S(2)}) collective-permute-start(f32[2,6,64,1]{3,2,1,0:T(8,128)S(1)} %get-tuple-element.144), channel_id=1, source_target_pairs={{0,8},{8,16},{16,24},{24,32},{32,40},{40,48},{48,56},{56,64},{64,7... | collective-permute-start | bytes 9224 | tf_op jit(solution)/shard_map/while/body/eval_jaxpr/ppermute | solution.py:21
  144.5 20.3 %collective-permute-start = (f32[2,6,64,1]{3,2,1,0:T(8,128)S(1)}, f32[2,6,64,1]{3,2,1,0:T(8,128)S(1)}, u32[]{:S(2)}, u32[]{:S(2)}) collective-permute-start(f32[2,6,64,1]{3,2,1,0:T(8,128)S(1)} %get-tuple-element.143), channel_id=1, source_target_pairs={{8,0},{16,8},{24,16},{32,24},{40,32},{48,40},{56,48},{64,56},{72,6... | collective-permute-start | bytes 9224 | tf_op jit(solution)/shard_map/while/body/eval_jaxpr/ppermute | solution.py:22
  148.2 16.7 %collective-permute-start.1 = (f32[2,6,64,1]{3,2,1,0:T(8,128)S(1)}, f32[2,6,64,1]{3,2,1,0:T(8,128)S(1)}, u32[]{:S(2)}, u32[]{:S(2)}) collective-permute-start(f32[2,6,64,1]{3,2,1,0:T(8,128)S(1)} %get-tuple-element.144), channel_id=1, source_target_pairs={{0,8},{8,16},{16,24},{24,32},{32,40},{40,48},{48,56},{56,64},{64,7... | collective-permute-start | bytes 9224 | tf_op jit(solution)/shard_map/while/body/eval_jaxpr/ppermute | solution.py:21
  170.6 10.5 %collective-permute-start = (f32[2,6,64,1]{3,2,1,0:T(8,128)S(1)}, f32[2,6,64,1]{3,2,1,0:T(8,128)S(1)}, u32[]{:S(2)}, u32[]{:S(2)}) collective-permute-start(f32[2,6,64,1]{3,2,1,0:T(8,128)S(1)} %get-tuple-element.143), channel_id=1, source_target_pairs={{8,0},{16,8},{24,16},{32,24},{40,32},{48,40},{56,48},{64,56},{72,6... | collective-permute-start | bytes 9224 | tf_op jit(solution)/shard_map/while/body/eval_jaxpr/ppermute | solution.py:22
  175.5 17.1 %collective-permute-start.1 = (f32[2,6,64,1]{3,2,1,0:T(8,128)S(1)}, f32[2,6,64,1]{3,2,1,0:T(8,128)S(1)}, u32[]{:S(2)}, u32[]{:S(2)}) collective-permute-start(f32[2,6,64,1]{3,2,1,0:T(8,128)S(1)} %get-tuple-element.144), channel_id=1, source_target_pairs={{0,8},{8,16},{16,24},{24,32},{32,40},{40,48},{48,56},{56,64},{64,7... | collective-permute-start | bytes 9224 | tf_op jit(solution)/shard_map/while/body/eval_jaxpr/ppermute | solution.py:21
  198.3 20.1 %collective-permute-start = (f32[2,6,64,1]{3,2,1,0:T(8,128)S(1)}, f32[2,6,64,1]{3,2,1,0:T(8,128)S(1)}, u32[]{:S(2)}, u32[]{:S(2)}) collective-permute-start(f32[2,6,64,1]{3,2,1,0:T(8,128)S(1)} %get-tuple-element.143), channel_id=1, source_target_pairs={{8,0},{16,8},{24,16},{32,24},{40,32},{48,40},{56,48},{64,56},{72,6... | collective-permute-start | bytes 9224 | tf_op jit(solution)/shard_map/while/body/eval_jaxpr/ppermute | solution.py:22
  200.3 18.4 %collective-permute-start.1 = (f32[2,6,64,1]{3,2,1,0:T(8,128)S(1)}, f32[2,6,64,1]{3,2,1,0:T(8,128)S(1)}, u32[]{:S(2)}, u32[]{:S(2)}) collective-permute-start(f32[2,6,64,1]{3,2,1,0:T(8,128)S(1)} %get-tuple-element.144), channel_id=1, source_target_pairs={{0,8},{8,16},{16,24},{24,32},{32,40},{40,48},{48,56},{56,64},{64,7... | collective-permute-start | bytes 9224 | tf_op jit(solution)/shard_map/while/body/eval_jaxpr/ppermute | solution.py:21
  224.5 18.8 %collective-permute-start = (f32[2,6,64,1]{3,2,1,0:T(8,128)S(1)}, f32[2,6,64,1]{3,2,1,0:T(8,128)S(1)}, u32[]{:S(2)}, u32[]{:S(2)}) collective-permute-start(f32[2,6,64,1]{3,2,1,0:T(8,128)S(1)} %get-tuple-element.143), channel_id=1, source_target_pairs={{8,0},{16,8},{24,16},{32,24},{40,32},{48,40},{56,48},{64,56},{72,6... | collective-permute-start | bytes 9224 | tf_op jit(solution)/shard_map/while/body/eval_jaxpr/ppermute | solution.py:22
  227.6 17.2 %collective-permute-start.1 = (f32[2,6,64,1]{3,2,1,0:T(8,128)S(1)}, f32[2,6,64,1]{3,2,1,0:T(8,128)S(1)}, u32[]{:S(2)}, u32[]{:S(2)}) collective-permute-start(f32[2,6,64,1]{3,2,1,0:T(8,128)S(1)} %get-tuple-element.144), channel_id=1, source_target_pairs={{0,8},{8,16},{16,24},{24,32},{32,40},{40,48},{48,56},{56,64},{64,7... | collective-permute-start | bytes 9224 | tf_op jit(solution)/shard_map/while/body/eval_jaxpr/ppermute | solution.py:21
  250.5 18.9 %collective-permute-start = (f32[2,6,64,1]{3,2,1,0:T(8,128)S(1)}, f32[2,6,64,1]{3,2,1,0:T(8,128)S(1)}, u32[]{:S(2)}, u32[]{:S(2)}) collective-permute-start(f32[2,6,64,1]{3,2,1,0:T(8,128)S(1)} %get-tuple-element.143), channel_id=1, source_target_pairs={{8,0},{16,8},{24,16},{32,24},{40,32},{48,40},{56,48},{64,56},{72,6... | collective-permute-start | bytes 9224 | tf_op jit(solution)/shard_map/while/body/eval_jaxpr/ppermute | solution.py:22
  252.5 18.3 %collective-permute-start.1 = (f32[2,6,64,1]{3,2,1,0:T(8,128)S(1)}, f32[2,6,64,1]{3,2,1,0:T(8,128)S(1)}, u32[]{:S(2)}, u32[]{:S(2)}) collective-permute-start(f32[2,6,64,1]{3,2,1,0:T(8,128)S(1)} %get-tuple-element.144), channel_id=1, source_target_pairs={{0,8},{8,16},{16,24},{24,32},{32,40},{40,48},{48,56},{56,64},{64,7... | collective-permute-start | bytes 9224 | tf_op jit(solution)/shard_map/while/body/eval_jaxpr/ppermute | solution.py:21
  276.5 11.9 %collective-permute-start = (f32[2,6,64,1]{3,2,1,0:T(8,128)S(1)}, f32[2,6,64,1]{3,2,1,0:T(8,128)S(1)}, u32[]{:S(2)}, u32[]{:S(2)}) collective-permute-start(f32[2,6,64,1]{3,2,1,0:T(8,128)S(1)} %get-tuple-element.143), channel_id=1, source_target_pairs={{8,0},{16,8},{24,16},{32,24},{40,32},{48,40},{56,48},{64,56},{72,6... | collective-permute-start | bytes 9224 | tf_op jit(solution)/shard_map/while/body/eval_jaxpr/ppermute | solution.py:22
  281.5 17.0 %collective-permute-start.1 = (f32[2,6,64,1]{3,2,1,0:T(8,128)S(1)}, f32[2,6,64,1]{3,2,1,0:T(8,128)S(1)}, u32[]{:S(2)}, u32[]{:S(2)}) collective-permute-start(f32[2,6,64,1]{3,2,1,0:T(8,128)S(1)} %get-tuple-element.144), channel_id=1, source_target_pairs={{0,8},{8,16},{16,24},{24,32},{32,40},{40,48},{48,56},{56,64},{64,7... | collective-permute-start | bytes 9224 | tf_op jit(solution)/shard_map/while/body/eval_jaxpr/ppermute | solution.py:21
  332.3 21.4 %collective-permute-start.4 = (f32[2,6,64,1]{3,2,1,0:T(8,128)S(1)}, f32[2,6,64,1]{3,2,1,0:T(8,128)S(1)}, u32[]{:S(2)}, u32[]{:S(2)}) collective-permute-start(f32[2,6,64,1]{3,2,1,0:T(8,128)S(1)} %get-tuple-element.155), channel_id=1, source_target_pairs={{8,0},{16,8},{24,16},{32,24},{40,32},{48,40},{56,48},{64,56},{72,6... | collective-permute-start | bytes 9224 | tf_op jit(solution)/shard_map/while/body/eval_jaxpr/ppermute | solution.py:22
  338.0 16.3 %collective-permute-start.5 = (f32[2,6,64,1]{3,2,1,0:T(8,128)S(1)}, f32[2,6,64,1]{3,2,1,0:T(8,128)S(1)}, u32[]{:S(2)}, u32[]{:S(2)}) collective-permute-start(f32[2,6,64,1]{3,2,1,0:T(8,128)S(1)} %get-tuple-element.156), channel_id=1, source_target_pairs={{0,8},{8,16},{16,24},{24,32},{32,40},{40,48},{48,56},{56,64},{64,7... | collective-permute-start | bytes 9224 | tf_op jit(solution)/shard_map/while/body/eval_jaxpr/ppermute | solution.py:21
  360.0 20.5 %collective-permute-start.4 = (f32[2,6,64,1]{3,2,1,0:T(8,128)S(1)}, f32[2,6,64,1]{3,2,1,0:T(8,128)S(1)}, u32[]{:S(2)}, u32[]{:S(2)}) collective-permute-start(f32[2,6,64,1]{3,2,1,0:T(8,128)S(1)} %get-tuple-element.155), channel_id=1, source_target_pairs={{8,0},{16,8},{24,16},{32,24},{40,32},{48,40},{56,48},{64,56},{72,6... | collective-permute-start | bytes 9224 | tf_op jit(solution)/shard_map/while/body/eval_jaxpr/ppermute | solution.py:22
  365.2 17.0 %collective-permute-start.5 = (f32[2,6,64,1]{3,2,1,0:T(8,128)S(1)}, f32[2,6,64,1]{3,2,1,0:T(8,128)S(1)}, u32[]{:S(2)}, u32[]{:S(2)}) collective-permute-start(f32[2,6,64,1]{3,2,1,0:T(8,128)S(1)} %get-tuple-element.156), channel_id=1, source_target_pairs={{0,8},{8,16},{16,24},{24,32},{32,40},{40,48},{48,56},{56,64},{64,7... | collective-permute-start | bytes 9224 | tf_op jit(solution)/shard_map/while/body/eval_jaxpr/ppermute | solution.py:21
  388.0 11.7 %collective-permute-start.4 = (f32[2,6,64,1]{3,2,1,0:T(8,128)S(1)}, f32[2,6,64,1]{3,2,1,0:T(8,128)S(1)}, u32[]{:S(2)}, u32[]{:S(2)}) collective-permute-start(f32[2,6,64,1]{3,2,1,0:T(8,128)S(1)} %get-tuple-element.155), channel_id=1, source_target_pairs={{8,0},{16,8},{24,16},{32,24},{40,32},{48,40},{56,48},{64,56},{72,6... | collective-permute-start | bytes 9224 | tf_op jit(solution)/shard_map/while/body/eval_jaxpr/ppermute | solution.py:22
  393.3 16.7 %collective-permute-start.5 = (f32[2,6,64,1]{3,2,1,0:T(8,128)S(1)}, f32[2,6,64,1]{3,2,1,0:T(8,128)S(1)}, u32[]{:S(2)}, u32[]{:S(2)}) collective-permute-start(f32[2,6,64,1]{3,2,1,0:T(8,128)S(1)} %get-tuple-element.156), channel_id=1, source_target_pairs={{0,8},{8,16},{16,24},{24,32},{32,40},{40,48},{48,56},{56,64},{64,7... | collective-permute-start | bytes 9224 | tf_op jit(solution)/shard_map/while/body/eval_jaxpr/ppermute | solution.py:21
  415.7 20.2 %collective-permute-start.4 = (f32[2,6,64,1]{3,2,1,0:T(8,128)S(1)}, f32[2,6,64,1]{3,2,1,0:T(8,128)S(1)}, u32[]{:S(2)}, u32[]{:S(2)}) collective-permute-start(f32[2,6,64,1]{3,2,1,0:T(8,128)S(1)} %get-tuple-element.155), channel_id=1, source_target_pairs={{8,0},{16,8},{24,16},{32,24},{40,32},{48,40},{56,48},{64,56},{72,6... | collective-permute-start | bytes 9224 | tf_op jit(solution)/shard_map/while/body/eval_jaxpr/ppermute | solution.py:22
  418.1 18.1 %collective-permute-start.5 = (f32[2,6,64,1]{3,2,1,0:T(8,128)S(1)}, f32[2,6,64,1]{3,2,1,0:T(8,128)S(1)}, u32[]{:S(2)}, u32[]{:S(2)}) collective-permute-start(f32[2,6,64,1]{3,2,1,0:T(8,128)S(1)} %get-tuple-element.156), channel_id=1, source_target_pairs={{0,8},{8,16},{16,24},{24,32},{32,40},{40,48},{48,56},{56,64},{64,7... | collective-permute-start | bytes 9224 | tf_op jit(solution)/shard_map/while/body/eval_jaxpr/ppermute | solution.py:21
  441.9 11.8 %collective-permute-start.4 = (f32[2,6,64,1]{3,2,1,0:T(8,128)S(1)}, f32[2,6,64,1]{3,2,1,0:T(8,128)S(1)}, u32[]{:S(2)}, u32[]{:S(2)}) collective-permute-start(f32[2,6,64,1]{3,2,1,0:T(8,128)S(1)} %get-tuple-element.155), channel_id=1, source_target_pairs={{8,0},{16,8},{24,16},{32,24},{40,32},{48,40},{56,48},{64,56},{72,6... | collective-permute-start | bytes 9224 | tf_op jit(solution)/shard_map/while/body/eval_jaxpr/ppermute | solution.py:22
  447.0 16.9 %collective-permute-start.5 = (f32[2,6,64,1]{3,2,1,0:T(8,128)S(1)}, f32[2,6,64,1]{3,2,1,0:T(8,128)S(1)}, u32[]{:S(2)}, u32[]{:S(2)}) collective-permute-start(f32[2,6,64,1]{3,2,1,0:T(8,128)S(1)} %get-tuple-element.156), channel_id=1, source_target_pairs={{0,8},{8,16},{16,24},{24,32},{32,40},{40,48},{48,56},{56,64},{64,7... | collective-permute-start | bytes 9224 | tf_op jit(solution)/shard_map/while/body/eval_jaxpr/ppermute | solution.py:21
  469.6 19.9 %collective-permute-start.4 = (f32[2,6,64,1]{3,2,1,0:T(8,128)S(1)}, f32[2,6,64,1]{3,2,1,0:T(8,128)S(1)}, u32[]{:S(2)}, u32[]{:S(2)}) collective-permute-start(f32[2,6,64,1]{3,2,1,0:T(8,128)S(1)} %get-tuple-element.155), channel_id=1, source_target_pairs={{8,0},{16,8},{24,16},{32,24},{40,32},{48,40},{56,48},{64,56},{72,6... | collective-permute-start | bytes 9224 | tf_op jit(solution)/shard_map/while/body/eval_jaxpr/ppermute | solution.py:22
  471.8 18.1 %collective-permute-start.5 = (f32[2,6,64,1]{3,2,1,0:T(8,128)S(1)}, f32[2,6,64,1]{3,2,1,0:T(8,128)S(1)}, u32[]{:S(2)}, u32[]{:S(2)}) collective-permute-start(f32[2,6,64,1]{3,2,1,0:T(8,128)S(1)} %get-tuple-element.156), channel_id=1, source_target_pairs={{0,8},{8,16},{16,24},{24,32},{32,40},{40,48},{48,56},{56,64},{64,7... | collective-permute-start | bytes 9224 | tf_op jit(solution)/shard_map/while/body/eval_jaxpr/ppermute | solution.py:21
  495.6 19.1 %collective-permute-start.4 = (f32[2,6,64,1]{3,2,1,0:T(8,128)S(1)}, f32[2,6,64,1]{3,2,1,0:T(8,128)S(1)}, u32[]{:S(2)}, u32[]{:S(2)}) collective-permute-start(f32[2,6,64,1]{3,2,1,0:T(8,128)S(1)} %get-tuple-element.155), channel_id=1, source_target_pairs={{8,0},{16,8},{24,16},{32,24},{40,32},{48,40},{56,48},{64,56},{72,6... | collective-permute-start | bytes 9224 | tf_op jit(solution)/shard_map/while/body/eval_jaxpr/ppermute | solution.py:22
  498.3 17.7 %collective-permute-start.5 = (f32[2,6,64,1]{3,2,1,0:T(8,128)S(1)}, f32[2,6,64,1]{3,2,1,0:T(8,128)S(1)}, u32[]{:S(2)}, u32[]{:S(2)}) collective-permute-start(f32[2,6,64,1]{3,2,1,0:T(8,128)S(1)} %get-tuple-element.156), channel_id=1, source_target_pairs={{0,8},{8,16},{16,24},{24,32},{32,40},{40,48},{48,56},{56,64},{64,7... | collective-permute-start | bytes 9224 | tf_op jit(solution)/shard_map/while/body/eval_jaxpr/ppermute | solution.py:21
  521.7 19.1 %collective-permute-start.4 = (f32[2,6,64,1]{3,2,1,0:T(8,128)S(1)}, f32[2,6,64,1]{3,2,1,0:T(8,128)S(1)}, u32[]{:S(2)}, u32[]{:S(2)}) collective-permute-start(f32[2,6,64,1]{3,2,1,0:T(8,128)S(1)} %get-tuple-element.155), channel_id=1, source_target_pairs={{8,0},{16,8},{24,16},{32,24},{40,32},{48,40},{56,48},{64,56},{72,6... | collective-permute-start | bytes 9224 | tf_op jit(solution)/shard_map/while/body/eval_jaxpr/ppermute | solution.py:22
  524.0 18.2 %collective-permute-start.5 = (f32[2,6,64,1]{3,2,1,0:T(8,128)S(1)}, f32[2,6,64,1]{3,2,1,0:T(8,128)S(1)}, u32[]{:S(2)}, u32[]{:S(2)}) collective-permute-start(f32[2,6,64,1]{3,2,1,0:T(8,128)S(1)} %get-tuple-element.156), channel_id=1, source_target_pairs={{0,8},{8,16},{16,24},{24,32},{32,40},{40,48},{48,56},{56,64},{64,7... | collective-permute-start | bytes 9224 | tf_op jit(solution)/shard_map/while/body/eval_jaxpr/ppermute | solution.py:21
  547.9 12.1 %collective-permute-start.4 = (f32[2,6,64,1]{3,2,1,0:T(8,128)S(1)}, f32[2,6,64,1]{3,2,1,0:T(8,128)S(1)}, u32[]{:S(2)}, u32[]{:S(2)}) collective-permute-start(f32[2,6,64,1]{3,2,1,0:T(8,128)S(1)} %get-tuple-element.155), channel_id=1, source_target_pairs={{8,0},{16,8},{24,16},{32,24},{40,32},{48,40},{56,48},{64,56},{72,6... | collective-permute-start | bytes 9224 | tf_op jit(solution)/shard_map/while/body/eval_jaxpr/ppermute | solution.py:22
  553.0 16.8 %collective-permute-start.5 = (f32[2,6,64,1]{3,2,1,0:T(8,128)S(1)}, f32[2,6,64,1]{3,2,1,0:T(8,128)S(1)}, u32[]{:S(2)}, u32[]{:S(2)}) collective-permute-start(f32[2,6,64,1]{3,2,1,0:T(8,128)S(1)} %get-tuple-element.156), channel_id=1, source_target_pairs={{0,8},{8,16},{16,24},{24,32},{32,40},{40,48},{48,56},{56,64},{64,7... | collective-permute-start | bytes 9224 | tf_op jit(solution)/shard_map/while/body/eval_jaxpr/ppermute | solution.py:21
  575.5 20.2 %collective-permute-start.4 = (f32[2,6,64,1]{3,2,1,0:T(8,128)S(1)}, f32[2,6,64,1]{3,2,1,0:T(8,128)S(1)}, u32[]{:S(2)}, u32[]{:S(2)}) collective-permute-start(f32[2,6,64,1]{3,2,1,0:T(8,128)S(1)} %get-tuple-element.155), channel_id=1, source_target_pairs={{8,0},{16,8},{24,16},{32,24},{40,32},{48,40},{56,48},{64,56},{72,6... | collective-permute-start | bytes 9224 | tf_op jit(solution)/shard_map/while/body/eval_jaxpr/ppermute | solution.py:22
  580.5 17.1 %collective-permute-start.5 = (f32[2,6,64,1]{3,2,1,0:T(8,128)S(1)}, f32[2,6,64,1]{3,2,1,0:T(8,128)S(1)}, u32[]{:S(2)}, u32[]{:S(2)}) collective-permute-start(f32[2,6,64,1]{3,2,1,0:T(8,128)S(1)} %get-tuple-element.156), channel_id=1, source_target_pairs={{0,8},{8,16},{16,24},{24,32},{32,40},{40,48},{48,56},{56,64},{64,7... | collective-permute-start | bytes 9224 | tf_op jit(solution)/shard_map/while/body/eval_jaxpr/ppermute | solution.py:21
  (60 other events, 522.3 us)
where the time goes:
time: 606 us; the launch traced here: 604 us
  waiting for transfers between devices  350 us (58%)
  starting transfers between devices  193 us (32%)
  other arithmetic  28 us (5%)
  local copies, waits for them, and re-layouts  25.3 us (4%)
    ppermute x44, waiting for transfers between devices, extended(): after = lax.ppermute(first, axis, down)  232 us
    ppermute x44, starting transfers between devices, extended(): after = lax.ppermute(first, axis, down)  175 us
    ppermute x44, waiting for transfers between devices, extended(): before = lax.ppermute(last, axis, up)  119 us
    ppermute x44, starting transfers between devices, extended(): before = lax.ppermute(last, axis, up)  18 us
    gather x4, local copies, waits for them, and re-layouts, observe(): return jnp.sum(weights * field_stack.reshape(-1)[corners], axis=0)  12.3 us
  transfers between devices with their start and end apart: 88, of which 62 were waited for; matrix products, arithmetic and copies ran while one was open for 4% of the time, Pallas kernels for 0%

commit v1 on v0

v1 whole, which is shorter than its diff:
```python
import functools

import jax
import jax.numpy as jnp
from jax import lax
from jax.experimental import pallas as pl
from jax.experimental.pallas import tpu as pltpu
from jax.sharding import PartitionSpec as P

SWEEPS = 10
SMOOTHING = 0.2
ADVECTION = 0.1
MIXING = 0.15

PAIR = 2
LEVELS = 6
HALF = 3
PLANES = PAIR * LEVELS
ROWS = 64
COLS = 128
HALO = SWEEPS
EDGE = 16
GAP = 2 * HALO
PITCH = COLS + GAP
TILES = -(-PLANES * PITCH // COLS)
BOTTOM_LANE = 240
TALL = ROWS + 2 * EDGE
PAD = 8
DEEP = TALL + 2 * PAD
TRAVEL = jnp.bfloat16
F32 = jnp.float32


def lanes(rows):
    return lax.broadcasted_iota(jnp.int32, (rows, COLS), 1)


def between(lane, low, high):
    if low <= 0:
        return lane < high
    if high >= COLS:
        return lane >= low
    return (lane >= low) & (lane < high)


def roll(value, shift):
    shift %= COLS
    return value if shift == 0 else pltpu.roll(value, shift, 1)


def runs(tile, source):
    found = []
    for lane in range(COLS):
        where = source(tile * COLS + lane)
        if found and found[-1][0] == where:
            found[-1][2] = lane + 1
        else:
            found.append([where, lane, lane + 1])
    return found


def value_source(at):
    plane, inside = divmod(at, PITCH)
    if plane >= PLANES:
        return None
    if inside < HALO:
        return ("halo", (GAP * plane + inside) // COLS)
    if inside >= HALO + COLS:
        return ("halo", (GAP * plane + inside - COLS) // COLS)
    return ("core", plane)


def depth_source(at):
    plane, inside = divmod(at, PITCH)
    return None if plane >= PLANES else (plane, inside // COLS)


def core_place(plane):
    return divmod(plane * PITCH + HALO, COLS)


def strips(read, lane, east, west):
    for plane in range(PLANES):
        turned = roll(read(plane), GAP * plane + HALO)
        for half, start in ((east, GAP * plane), (west, GAP * plane + HALO)):
            for part in range(2):
                low = max(start - part * COLS, 0)
                high = min(start + HALO - part * COLS, COLS)
                if low < high:
                    half[part] = jnp.where(between(lane, low, high), turned, half[part])
    return east, west


def send_strips(east, west, even, first_ref, second_ref):
    for part in range(2):
        here = slice(part * COLS, (part + 1) * COLS)
        first_ref[:, here] = jnp.where(even, east[part], west[part]).astype(TRAVEL)
        second_ref[:, here] = jnp.where(even, west[part], east[part]).astype(TRAVEL)


def zonal_even():
    return lax.axis_index("zon") % 2 == 0


def meridional_even():
    return lax.axis_index("mer") % 2 == 0


def sides(first, second, even):
    first, second = first.astype(F32), second.astype(F32)
    return jnp.where(even, second, first), jnp.where(even, first, second)


def pack_kernel(model_ref, control_ref, bottom_ref, first_ref, second_ref):
    lane = lanes(ROWS)
    blank = jnp.zeros((ROWS, COLS), F32)
    east, west = strips(
        lambda p: control_ref[p // LEVELS, p % LEVELS], lane, [blank, blank], [blank, blank]
    )
    depth = bottom_ref[...].astype(F32)
    low = BOTTOM_LANE - COLS
    mark = between(lane, low, low + HALO)
    east[1] = jnp.where(mark, roll(depth, low - (COLS - HALO)), east[1])
    west[1] = jnp.where(mark, roll(depth, low), west[1])
    for q in range(4 * HALF):
        value = model_ref[q // HALF, q % HALF]
        for half, column, start in (
            (east, value[:, COLS - 1 :], GAP * q + 15),
            (west, value[:, :1], GAP * q + 5),
        ):
            part, at = divmod(start, COLS)
            coarse = column.astype(TRAVEL).astype(F32)
            half[part] = jnp.where(lane == at, coarse, half[part])
            half[part] = jnp.where(lane == at + 1, column - coarse, half[part])
    send_strips(east, west, zonal_even(), first_ref, second_ref)


def place(read, first_ref, second_ref, even, lane, x_ref):
    before, after, both = [], [], []
    for part in range(2):
        here = slice(part * COLS, (part + 1) * COLS)
        low, high = sides(first_ref[:, here], second_ref[:, here], even)
        before.append(low)
        after.append(high)
        both.append(jnp.where((lane + part * COLS) % GAP < HALO, low, high))
    turned = {}
    for tile in range(TILES):
        value = jnp.zeros((ROWS, COLS), F32)
        for source, low, high in runs(tile, value_source):
            if source is None:
                continue
            kind, index = source
            if kind == "core":
                if index not in turned:
                    turned[index] = roll(read(index), GAP * index + HALO)
                piece = turned[index]
            else:
                piece = both[index]
            whole = low == 0 and high == COLS
            value = piece if whole else jnp.where(between(lane, low, high), piece, value)
        x_ref[tile] = value
    return before, after


def edge_rows(even):
    return (
        pl.multiple_of(jnp.where(even, ROWS - EDGE, 0), EDGE),
        pl.multiple_of(jnp.where(even, 0, ROWS - EDGE), EDGE),
    )


def widen_kernel(
    model_ref, control_ref, bottom_ref, first_ref, second_ref, x_ref, depth_ref, a_ref, b_ref, rows_ref
):
    lane = lanes(ROWS)
    before, after = place(
        lambda p: control_ref[p // LEVELS, p % LEVELS], first_ref, second_ref, zonal_even(), lane, x_ref
    )
    depth = roll(bottom_ref[...].astype(F32), HALO)
    low = BOTTOM_LANE - COLS
    depth_ref[0] = jnp.where(lane < HALO, roll(before[1], -low), depth)
    depth_ref[1] = jnp.where(
        lane < HALO, depth, jnp.where(lane < GAP, roll(after[1], HALO - low), 0.0)
    )
    even = meridional_even()
    for start, row, out_ref in zip(
        edge_rows(even), (jnp.where(even, ROWS - 1, 0), jnp.where(even, 0, ROWS - 1)), (a_ref, b_ref)
    ):
        for tile in range(TILES):
            out_ref[tile] = x_ref[tile, pl.ds(start, EDGE), :].astype(TRAVEL)
        for part in range(2):
            out_ref[TILES + part] = depth_ref[part, pl.ds(start, EDGE), :].astype(TRAVEL)
        rows_ref[...] = jnp.zeros((EDGE, COLS), F32)
        for q in range(4 * HALF):
            rows_ref[q : q + 1, :] = model_ref[q // HALF, q % HALF, pl.ds(row, 1), :]
        value = rows_ref[...]
        coarse = value.astype(TRAVEL)
        out_ref[TILES + 2] = coarse
        out_ref[TILES + 3] = (value - coarse.astype(F32)).astype(TRAVEL)


def rewiden_kernel(field_ref, first_ref, second_ref, x_ref, a_ref, b_ref):
    place(lambda p: field_ref[p], first_ref, second_ref, zonal_even(), lanes(ROWS), x_ref)
    for start, out_ref in zip(edge_rows(meridional_even()), (a_ref, b_ref)):
        for tile in range(TILES):
            out_ref[tile] = x_ref[tile, pl.ds(start, EDGE), :].astype(TRAVEL)


def background_kernel(
    model_ref, bottom_ref, first_ref, second_ref, depth_ref, a_ref, b_ref, keep_ref, send_ref, tall_ref
):
    lane = lanes(ROWS)
    group = lax.axis_index("grp")
    even_zon, even_mer = zonal_even(), meridional_even()
    before, after = [], []
    for part in range(2):
        here = slice(part * COLS, (part + 1) * COLS)
        low, high = sides(first_ref[:, here], second_ref[:, here], even_zon)
        before.append(low)
        after.append(high)

    def halo_rows(index):
        return sides(a_ref[index], b_ref[index], even_mer)

    def stand(value, above, below):
        tall_ref[8 : 8 + ROWS, :] = value
        tall_ref[7:8, :] = above
        tall_ref[8 + ROWS : 9 + ROWS, :] = below
        return tall_ref[7 : 7 + ROWS, :], tall_ref[9 : 9 + ROWS, :]

    depth = bottom_ref[...].astype(F32)
    depth_east = jnp.where(lane == COLS - 1, roll(depth_ref[1], COLS - 1 - HALO), roll(depth, -1))
    depth_west = jnp.where(lane == 0, roll(depth_ref[0], 1 - HALO), roll(depth, 1))
    edge_lane = lanes(EDGE)
    flat = [
        jnp.where(edge_lane < COLS - HALO, roll(main, -HALO), roll(rest, -HALO))
        for main, rest in zip(halo_rows(TILES), halo_rows(TILES + 1))
    ]
    depth_below, depth_above = stand(depth, flat[0][EDGE - 1 :], flat[1][:1])
    coarse, fine = halo_rows(TILES + 2), halo_rows(TILES + 3)
    low_rows, high_rows = coarse[0] + fine[0], coarse[1] + fine[1]
    for level in range(HALF):
        here = (group * HALF + level).astype(F32)
        wet, wet_e, wet_w, wet_n, wet_s = (
            jnp.where(value > here, 1.0, 0.0)
            for value in (depth, depth_east, depth_west, depth_above, depth_below)
        )
        flow_x, flow_y = model_ref[2, level], model_ref[3, level]
        for field in range(4):
            q = field * HALF + level
            value = model_ref[field, level]
            part, at = divmod(GAP * q + 5, COLS)
            column = after[part][:, at : at + 1] + after[part][:, at + 1 : at + 2]
            east = jnp.where(lane == COLS - 1, column, roll(value, -1))
            part, at = divmod(GAP * q + 15, COLS)
            column = before[part][:, at : at + 1] + before[part][:, at + 1 : at + 2]
            west = jnp.where(lane == 0, column, roll(value, 1))
            south, north = stand(value, low_rows[q : q + 1], high_rows[q : q + 1])
            grad_x = 0.5 * (wet_e * east - wet_w * west)
            grad_y = 0.5 * (wet_n * north - wet_s * south)
            flux = (
                wet_e * (east - value)
                + wet_w * (west - value)
                + wet_n * (north - value)
                + wet_s * (south - value)
            )
            result = wet * (
                value - ADVECTION * (flow_x * grad_x + flow_y * grad_y) + MIXING * (wet * flux)
            )
            own = group == field // 2

            @pl.when(own)
            def _():
                keep_ref[field % 2, level] = result

            @pl.when(jnp.logical_not(own))
            def _():
                send_ref[field % 2, level] = result


def neighbour_sums(read, start, rows, use):
    lane = lanes(rows)
    first, last = lane == 0, lane == COLS - 1
    turned = {}

    def turn(tile, shift):
        tile %= TILES
        if (tile, shift) not in turned:
            turned[tile, shift] = roll(read(tile, start, rows), shift)
        return turned[tile, shift]

    for tile in range(TILES):
        centre = read(tile, start, rows)
        east = jnp.where(last, turn(tile + 1, -1), turn(tile, -1))
        west = jnp.where(first, turn(tile - 1, 1), turn(tile, 1))
        total = (east + west) + (read(tile, start - 1, rows) + read(tile, start + 1, rows))
        use(tile, centre, total)


def sweep_all(wide_ref, keep_ref, give_ref):
    def sweep(source, target, start, rows):
        def read(tile, at, count):
            return wide_ref[source, tile, pl.ds(at, count), :]

        def use(tile, centre, total):
            here = pl.ds(start, rows)
            wide_ref[target, tile, here, :] = (
                keep_ref[tile, here, :] * centre + give_ref[tile, here, :] * total
            )

        neighbour_sums(read, start, rows, use)

    sweep(0, 1, PAD, TALL)

    def step(index, carry):
        source = (index + 1) % 2
        sweep(source, 1 - source, 2 * PAD, TALL - 2 * PAD)
        return carry

    lax.fori_loop(0, SWEEPS - 1, step, 0)


def fill_wide(x_ref, a_ref, b_ref, wide_ref, mask_ref):
    even = meridional_even()
    for tile in range(TILES):
        low, high = sides(a_ref[tile], b_ref[tile], even)
        value = jnp.concatenate([low, x_ref[tile], high], axis=0)
        if mask_ref is not None:
            value = value * mask_ref[tile, PAD : PAD + TALL, :]
        wide_ref[0, tile, PAD : PAD + TALL, :] = value


def plane_of(wide_ref, plane, lane):
    tile, offset = core_place(plane)
    here = slice(PAD + EDGE, PAD + EDGE + ROWS)
    value = wide_ref[0, tile, here, :]
    if offset:
        value = jnp.where(lane >= offset, value, wide_ref[0, tile + 1, here, :])
    return roll(value, -offset)


def smooth_kernel(x_ref, depth_ref, a_ref, b_ref, out_ref, keep_ref, give_ref, wide_ref, mask_ref):
    even = meridional_even()
    tall_lane = lanes(TALL)
    low = [sides(a_ref[TILES + part], b_ref[TILES + part], even) for part in range(2)]
    depth = [jnp.concatenate([low[p][0], depth_ref[p], low[p][1]], axis=0) for p in range(2)]
    for tile in range(TILES):
        value = jnp.zeros((TALL, COLS), F32)
        for source, start, stop in runs(tile, depth_source):
            if source is None:
                continue
            plane, part = source
            wet = jnp.where(roll(depth[part], GAP * plane) > (plane % LEVELS), 1.0, 0.0)
            value = jnp.where(between(tall_lane, start, stop), wet, value)
        mask_ref[tile, :PAD, :] = jnp.zeros((PAD, COLS), F32)
        mask_ref[tile, PAD + TALL :, :] = jnp.zeros((PAD, COLS), F32)
        mask_ref[tile, PAD : PAD + TALL, :] = value

    def use(tile, centre, total):
        here = slice(PAD, PAD + TALL)
        keep_ref[tile, here, :] = centre * (1.0 - SMOOTHING * total)
        give_ref[tile, here, :] = SMOOTHING * centre

    neighbour_sums(lambda t, at, n: mask_ref[t, at : at + n, :], PAD, TALL, use)
    fill_wide(x_ref, a_ref, b_ref, wide_ref, mask_ref)
    sweep_all(wide_ref, keep_ref, give_ref)
    lane = lanes(ROWS)
    for plane in range(PLANES):
        out_ref[plane] = plane_of(wide_ref, plane, lane)


def gradient_kernel(x_ref, a_ref, b_ref, keep_ref, give_ref, control_ref, out_ref, wide_ref):
    fill_wide(x_ref, a_ref, b_ref, wide_ref, None)
    sweep_all(wide_ref, keep_ref, give_ref)
    lane = lanes(ROWS)
    for plane in range(PLANES):
        f, k = divmod(plane, LEVELS)
        out_ref[f, k] = control_ref[f, k] + plane_of(wide_ref, plane, lane)


def split(value):
    coarse = value.astype(jnp.bfloat16)
    return jnp.concatenate([coarse, (value - coarse.astype(F32)).astype(jnp.bfloat16)], axis=1)


def join(value):
    return value[:, :COLS] + value[:, COLS:]


def observe_kernel(
    count_ref,
    smooth_ref,
    error_ref,
    bottom_ref,
    keep_ref,
    other_ref,
    corner_ref,
    weight_ref,
    value_ref,
    precision_ref,
    field_ref,
    first_ref,
    second_ref,
    total_ref,
):
    group = lax.axis_index("grp")
    slots = corner_ref.shape[-1]
    depth = bottom_ref[...]
    for plane in range(PLANES):
        f, k = divmod(plane, LEVELS)
        scale = jnp.where(depth > k, error_ref[f, k], 0.0)
        held = group == k // HALF
        prior = jnp.where(held, keep_ref[f, k % HALF], other_ref[f, k % HALF])
        total_ref[plane * ROWS : (plane + 1) * ROWS, :] = scale * smooth_ref[plane] + prior
    corner = corner_ref[0, 0]
    row = (corner >> 7).astype(F32)
    column = (corner & (COLS - 1)).astype(F32)
    stacked = jnp.concatenate(
        [weight_ref[0, 0, 0], value_ref[0, 0], precision_ref[0, 0], row, column], axis=0
    )
    tall = jnp.transpose(stacked)
    row_tall = jnp.concatenate([tall[:, 6:7], tall[:, 6:7] + 1.0], axis=0)
    cells = PLANES * ROWS
    wide_row = lax.broadcasted_iota(jnp.int32, (2 * slots, cells), 1).astype(F32)
    pick = jnp.where(wide_row == row_tall, 1.0, 0.0).astype(jnp.bfloat16)
    seen = join(jnp.dot(pick, split(total_ref[...]), preferred_element_type=F32))
    lane = lanes(slots).astype(F32)
    at, beside = lane == tall[:, 7:8], lane == tall[:, 7:8] + 1.0
    lower = jnp.where(at, tall[:, 0:1], jnp.where(beside, tall[:, 1:2], 0.0))
    upper = jnp.where(at, tall[:, 2:3], jnp.where(beside, tall[:, 3:4], 0.0))
    observed = jnp.sum(lower * seen[:slots] + upper * seen[slots:], axis=1, keepdims=True)
    live = lax.broadcasted_iota(jnp.int32, (slots, 1), 0) < count_ref[0, 0, 0]
    misfit = jnp.where(live, tall[:, 5:6] * (observed - tall[:, 4:5]), 0.0)
    spread = jnp.concatenate([lower * misfit, upper * misfit], axis=0)
    tall_row = lax.broadcasted_iota(jnp.int32, (cells, slots), 0).astype(F32)
    back = jnp.concatenate(
        [
            jnp.where(tall_row == row, 1.0, 0.0).astype(jnp.bfloat16),
            jnp.where(tall_row == row + 1.0, 1.0, 0.0).astype(jnp.bfloat16),
        ],
        axis=1,
    )
    total_ref[...] = join(jnp.dot(back, split(spread), preferred_element_type=F32))
    for plane in range(PLANES):
        f, k = divmod(plane, LEVELS)
        scale = jnp.where(depth > k, error_ref[f, k], 0.0)
        field_ref[plane] = scale * total_ref[plane * ROWS : (plane + 1) * ROWS, :]
    blank = jnp.zeros((ROWS, COLS), F32)
    east, west = strips(
        lambda p: field_ref[p], lanes(ROWS), [blank, blank], [blank, blank]
    )
    send_strips(east, west, zonal_even(), first_ref, second_ref)


def call(kernel, outs, scratch=(), scalars=0, name=None):
    def run(*args):
        return pl.pallas_call(
            kernel,
            out_shape=[jax.ShapeDtypeStruct(shape, kind) for shape, kind in outs],
            in_specs=[
                pl.BlockSpec(memory_space=pltpu.SMEM if i < scalars else pltpu.VMEM)
                for i in range(len(args))
            ],
            out_specs=[pl.BlockSpec(memory_space=pltpu.VMEM) for _ in outs],
            scratch_shapes=[pltpu.VMEM(shape, kind) for shape, kind in scratch],
            compiler_params=pltpu.CompilerParams(vmem_limit_bytes=24 * 2**20),
            name=name,
        )(*args)

    return run


def swap(value, axis, shift, wrap):
    size = lax.axis_size(axis)
    pairs = []
    for i in range(shift, size + shift - 1, 2):
        j = i + 1
        if j < size or wrap:
            pairs += [(i, j % size), (j % size, i)]
    return lax.ppermute(value, axis, pairs)


def exchange(first, second, axis, wrap):
    return swap(first, axis, 0, wrap), swap(second, axis, 1, wrap)


ZONAL = ((ROWS, 2 * COLS), TRAVEL)
WIDE = ((TILES, ROWS, COLS), F32)


def body(
    model_state,
    control,
    error_std,
    bottom_level,
    obs_count,
    obs_corner,
    obs_weight,
    obs_value,
    obs_precision,
):
    first, second = call(pack_kernel, [ZONAL, ZONAL], name="pack")(
        model_state, control, bottom_level
    )
    zon = exchange(first, second, "zon", True)
    message = ((TILES + 4, EDGE, COLS), TRAVEL)
    x, depth, first, second = call(
        widen_kernel,
        [WIDE, ((2, ROWS, COLS), F32), message, message],
        [((EDGE, COLS), F32)],
        name="widen",
    )(model_state, control, bottom_level, *zon)
    mer = exchange(first, second, "mer", False)
    part = ((PAIR, HALF, ROWS, COLS), F32)
    keep, send = call(
        background_kernel, [part, part], [((ROWS + 16, COLS), F32)], name="background"
    )(model_state, bottom_level, *zon, depth, *mer)
    other = lax.ppermute(send, "grp", [(0, 1), (1, 0)])
    deep = ((TILES, DEEP, COLS), F32)
    smoothed, keep_coef, give_coef = call(
        smooth_kernel,
        [((PLANES, ROWS, COLS), F32), deep, deep],
        [((2, TILES, DEEP, COLS), F32), deep],
        name="smooth",
    )(x, depth, *mer)
    field, first, second = call(
        observe_kernel,
        [((PLANES, ROWS, COLS), F32), ZONAL, ZONAL],
        [((PLANES * ROWS, COLS), F32)],
        scalars=1,
        name="observe",
    )(
        obs_count,
        smoothed,
        error_std,
        bottom_level,
        keep,
        other,
        obs_corner,
        obs_weight,
        obs_value,
        obs_precision,
    )
    zon = exchange(first, second, "zon", True)
    message = ((TILES, EDGE, COLS), TRAVEL)
    x, first, second = call(rewiden_kernel, [WIDE, message, message], name="rewiden")(field, *zon)
    mer = exchange(first, second, "mer", False)
    return call(
        gradient_kernel,
        [(control.shape, F32)],
        [((2, TILES, DEEP, COLS), F32)],
        name="gradient",
    )(x, *mer, keep_coef, give_coef, control)[0]


def solution(mesh):
    return jax.shard_map(
        body,
        mesh=mesh,
        in_specs=(
            P(None, "grp", "mer", "zon"),
            P("grp", None, "mer", "zon"),
            P("grp", None, "mer", "zon"),
            P("mer", "zon"),
            P("grp", "mer", "zon"),
            P("grp", "mer", "zon", None),
            P("grp", "mer", "zon", None, None),
            P("grp", "mer", "zon", None),
            P("grp", "mer", "zon", None),
        ),
        out_specs=P("grp", None, "mer", "zon"),
        check_vma=False,
    )
```

time: 606 us -> 56.4 us (0.09)
  the two profiles are of different devices: /device:TPU:1 before, /device:TPU:2 now
where the time goes in v1:
time: 56.4 us; the launch traced here: 56.1 us
  starting transfers between devices  23.1 us (41%)
  Pallas kernels  15.1 us (27%)
  waiting for transfers between devices  13.6 us (24%)
  local copies, waits for them, and re-layouts  3.42 us (6%)
  between operations  0.85 us (2%)
    ppermute x8, starting transfers between devices, swap(): return lax.ppermute(value, axis, pairs)  23 us
    pallas_call x7, Pallas kernels, run(): pl.pallas_call(kernel, out_shape=[jax.ShapeDtypeStruct(shape, kind) for s...  15.1 us
    ppermute x8, waiting for transfers between devices, swap(): return lax.ppermute(value, axis, pairs)  13.6 us
    unnamed x20, local copies, waits for them, and re-layouts  3.42 us
  transfers between devices with their start and end apart: 9, of which 6 were waited for; matrix products, arithmetic and copies ran while one was open for 0% of the time, Pallas kernels for 10%

profile of v1, /device:TPU:2, one launch (start us, length us, event | category | flops | bytes accessed | tf_op | source)
XLA Modules:
  0.0 56.1 jit_solution(2034116047676209557)
XLA Ops:
  0.0 0.0 copy-start
  0.0 1.0 %copy-done = f32[4,3,64,128]{3,2,1,0:T(8,128)S(1)} copy-done((f32[4,3,64,128]{3,2,1,0:T(8,128)S(1)}, f32[4,3,64,128]{3,2,1,0:T(8,128)}, u32[]{:S(2)}) %copy-start) | copy-done | bytes 393240
  1.0 0.0 copy-start.1
  1.0 1.0 %copy-done.1 = f32[2,6,64,128]{3,2,1,0:T(8,128)S(1)} copy-done((f32[2,6,64,128]{3,2,1,0:T(8,128)S(1)}, f32[2,6,64,128]{3,2,1,0:T(8,128)}, u32[]{:S(2)}) %copy-start.1) | copy-done | bytes 393240
  2.0 0.0 copy-start.3
  2.0 0.8 %copy-done.3 = s32[64,128]{1,0:T(8,128)S(1)} copy-done((s32[64,128]{1,0:T(8,128)S(1)}, s32[64,128]{1,0:T(8,128)}, u32[]{:S(2)}) %copy-start.3) | copy-done | bytes 32792
  2.8 0.4 pack.1
  3.1 3.3 %collective-permute-start = (bf16[64,256]{1,0:T(8,128)(2,1)S(1)}, bf16[64,256]{1,0:T(8,128)(2,1)S(1)}, u32[]{:S(2)}, u32[]{:S(2)}) collective-permute-start(bf16[64,256]{1,0:T(8,128)(2,1)S(1)} %get-tuple-element.22), channel_id=1, source_target_pairs={{0,8},{8,0},{16,24},{24,16},{32,40},{40,32},{48,56},{56,48},{64,72... | collective-permute-start | bytes 98312 | tf_op jit(solution)/shard_map/ppermute | solution.py:480
  6.4 0.0 copy-start.4
  6.4 5.6 %collective-permute-start.1 = (bf16[64,256]{1,0:T(8,128)(2,1)S(1)}, bf16[64,256]{1,0:T(8,128)(2,1)S(1)}, u32[]{:S(2)}, u32[]{:S(2)}) collective-permute-start(bf16[64,256]{1,0:T(8,128)(2,1)S(1)} %get-tuple-element.23), channel_id=1, source_target_pairs={{8,16},{16,8},{24,32},{32,24},{40,48},{48,40},{56,64},{64,56},{72,... | collective-permute-start | bytes 98312 | tf_op jit(solution)/shard_map/ppermute | solution.py:480
  12.0 0.0 collective-permute-done.first_ref
  12.0 1.9 %collective-permute-done.1.second_ref = bf16[64,256]{1,0:T(8,128)(2,1)S(1)} collective-permute-done((bf16[64,256]{1,0:T(8,128)(2,1)S(1)}, bf16[64,256]{1,0:T(8,128)(2,1)S(1)}, u32[]{:S(2)}, u32[]{:S(2)}) %collective-permute-start.1) | collective-permute-done | bytes 32800 | tf_op jit(solution)/shard_map/ppermute | solution.py:480
  13.9 0.2 widen.1
  14.1 1.7 %collective-permute-start.2 = (bf16[18,16,128]{2,1,0:T(8,128)(2,1)S(1)}, bf16[18,16,128]{2,1,0:T(8,128)(2,1)S(1)}, u32[]{:S(2)}, u32[]{:S(2)}) collective-permute-start(bf16[18,16,128]{2,1,0:T(8,128)(2,1)S(1)} %get-tuple-element.26), channel_id=1, source_target_pairs={{0,1},{1,0},{2,3},{3,2},{4,5},{5,4},{6,7},{7,6},{8,9},{9,8},{10,11... | collective-permute-start | bytes 221192 | tf_op jit(solution)/shard_map/ppermute | solution.py:480
  15.8 2.3 %collective-permute-start.3 = (bf16[18,16,128]{2,1,0:T(8,128)(2,1)S(1)}, bf16[18,16,128]{2,1,0:T(8,128)(2,1)S(1)}, u32[]{:S(2)}, u32[]{:S(2)}) collective-permute-start(bf16[18,16,128]{2,1,0:T(8,128)(2,1)S(1)} %get-tuple-element.27), channel_id=1, source_target_pairs={{1,2},{2,1},{3,4},{4,3},{5,6},{6,5},{9,10},{10,9},{11,12},{12,11},... | collective-permute-start | bytes 221192 | tf_op jit(solution)/shard_map/ppermute | solution.py:480
  18.1 0.5 collective-permute-done.2.a_ref
  18.6 4.3 %collective-permute-done.3.b_ref = bf16[18,16,128]{2,1,0:T(8,128)(2,1)S(1)} collective-permute-done((bf16[18,16,128]{2,1,0:T(8,128)(2,1)S(1)}, bf16[18,16,128]{2,1,0:T(8,128)(2,1)S(1)}, u32[]{:S(2)}, u32[]{:S(2)}) %collective-permute-start.3) | collective-permute-done | bytes 73760 | tf_op jit(solution)/shard_map/ppermute | solution.py:480
  22.9 0.0 copy-done.4
  22.9 1.6 %background.1 = (f32[2,3,64,128]{3,2,1,0:T(8,128)S(1)}, f32[2,3,64,128]{3,2,1,0:T(8,128)S(1)}) custom-call(f32[4,3,64,128]{3,2,1,0:T(8,128)S(1)} %copy-done, s32[64,128]{1,0:T(8,128)S(1)} %copy-done.4, bf16[64,256]{1,0:T(8,128)(2,1)S(1)} %collective-permute-done.first_ref, bf16[64,256]{1,0:T(8,128)(2,1)S(1)} %collective-permute-done.1.second_ref, ...), custom_call_target="tpu_custom_call" | custom-call | tf_op jit(solution)/shard_map/background/pallas_call | solution.py:457
  24.6 0.0 copy-start.5
  24.6 0.1 collective-permute-start.4
  25.4 0.0 copy-start.6
  25.4 0.0 copy-start.8
  25.4 0.0 copy-start.9
  25.4 5.5 %smooth.1 = (f32[12,64,128]{2,1,0:T(8,128)S(1)}, f32[14,112,128]{2,1,0:T(8,128)S(1)}, f32[14,112,128]{2,1,0:T(8,128)S(1)}) custom-call(f32[14,64,128]{2,1,0:T(8,128)S(1)} %get-tuple-element.24.x_ref, f32[2,64,128]{2,1,0:T(8,128)S(1)} %get-tuple-element.25.depth_ref, bf16[18,16,128]{2,1,0:T(8,128)(2,1)S(1)} %collective-permute-done.2.a_ref, ...), custom_call_target="tpu_custom_call" | custom-call | tf_op jit(solution)/shard_map/smooth/pallas_call | solution.py:457
  30.9 0.0 collective-permute-done.4.other_ref
  31.0 0.0 copy-start.7
  31.0 0.0 copy-done.5
  31.0 0.0 copy-done.6
  31.0 0.0 copy-done.8
  31.0 0.0 copy-done.9
  31.0 0.6 %copy-done.7 = s32[1,1,1,256]{3,2,1,0:T(1,128)S(1)} copy-done((s32[1,1,1,256]{3,2,1,0:T(1,128)S(1)}, s32[1,1,1,256]{3,2,1,0:T(1,128)}, u32[]{:S(2)}) %copy-start.7) | copy-done | bytes 1048
  31.6 1.6 %observe.1 = (f32[12,64,128]{2,1,0:T(8,128)S(1)}, bf16[64,256]{1,0:T(8,128)(2,1)S(1)}, bf16[64,256]{1,0:T(8,128)(2,1)S(1)}) custom-call(s32[1,1,1]{2,1,0:T(1,128)S(6)} %copy.10.count_ref, f32[12,64,128]{2,1,0:T(8,128)S(1)} %get-tuple-element.28.smooth_ref, f32[2,6,64,128]{3,2,1,0:T(8,128)S(1)} %copy-done.5, s32[64,128]{1,0:T(8,128)S(1)} %copy-done.4, ...), custom_call_target="tpu_custom_call" | custom-call | tf_op jit(solution)/shard_map/observe/pallas_call | solution.py:457
  33.2 0.0 copy-start.2
  33.3 0.1 collective-permute-start.5
  33.4 6.7 %collective-permute-start.6 = (bf16[64,256]{1,0:T(8,128)(2,1)S(1)}, bf16[64,256]{1,0:T(8,128)(2,1)S(1)}, u32[]{:S(2)}, u32[]{:S(2)}) collective-permute-start(bf16[64,256]{1,0:T(8,128)(2,1)S(1)} %get-tuple-element.33), channel_id=1, source_target_pairs={{8,16},{16,8},{24,32},{32,24},{40,48},{48,40},{56,64},{64,56},{72,... | collective-permute-start | bytes 98312 | tf_op jit(solution)/shard_map/ppermute | solution.py:480
  40.1 0.0 collective-permute-done.5.first_ref
  40.1 1.9 %collective-permute-done.6.second_ref = bf16[64,256]{1,0:T(8,128)(2,1)S(1)} collective-permute-done((bf16[64,256]{1,0:T(8,128)(2,1)S(1)}, bf16[64,256]{1,0:T(8,128)(2,1)S(1)}, u32[]{:S(2)}, u32[]{:S(2)}) %collective-permute-start.6) | collective-permute-done | bytes 32800 | tf_op jit(solution)/shard_map/ppermute | solution.py:480
  42.0 0.2 rewiden.1
  42.1 1.4 %collective-permute-start.7 = (bf16[14,16,128]{2,1,0:T(8,128)(2,1)S(1)}, bf16[14,16,128]{2,1,0:T(8,128)(2,1)S(1)}, u32[]{:S(2)}, u32[]{:S(2)}) collective-permute-start(bf16[14,16,128]{2,1,0:T(8,128)(2,1)S(1)} %get-tuple-element.35), channel_id=1, source_target_pairs={{0,1},{1,0},{2,3},{3,2},{4,5},{5,4},{6,7},{7,6},{8,9},{9,8},{10,11... | collective-permute-start | bytes 172040 | tf_op jit(solution)/shard_map/ppermute | solution.py:480
  43.6 1.9 %collective-permute-start.8 = (bf16[14,16,128]{2,1,0:T(8,128)(2,1)S(1)}, bf16[14,16,128]{2,1,0:T(8,128)(2,1)S(1)}, u32[]{:S(2)}, u32[]{:S(2)}) collective-permute-start(bf16[14,16,128]{2,1,0:T(8,128)(2,1)S(1)} %get-tuple-element.36), channel_id=1, source_target_pairs={{1,2},{2,1},{3,4},{4,3},{5,6},{6,5},{9,10},{10,9},{11,12},{12,11},... | collective-permute-start | bytes 172040 | tf_op jit(solution)/shard_map/ppermute | solution.py:480
  45.5 0.9 %collective-permute-done.7.a_ref = bf16[14,16,128]{2,1,0:T(8,128)(2,1)S(1)} collective-permute-done((bf16[14,16,128]{2,1,0:T(8,128)(2,1)S(1)}, bf16[14,16,128]{2,1,0:T(8,128)(2,1)S(1)}, u32[]{:S(2)}, u32[]{:S(2)}) %collective-permute-start.7) | collective-permute-done | bytes 57376 | tf_op jit(solution)/shard_map/ppermute | solution.py:480
  46.4 4.1 %collective-permute-done.8.b_ref = bf16[14,16,128]{2,1,0:T(8,128)(2,1)S(1)} collective-permute-done((bf16[14,16,128]{2,1,0:T(8,128)(2,1)S(1)}, bf16[14,16,128]{2,1,0:T(8,128)(2,1)S(1)}, u32[]{:S(2)}, u32[]{:S(2)}) %collective-permute-start.8) | collective-permute-done | bytes 57376 | tf_op jit(solution)/shard_map/ppermute | solution.py:480
  50.5 0.0 copy-done.2
  50.5 5.6 %gradient.1 = f32[2,6,64,128]{3,2,1,0:T(8,128)} custom-call(f32[14,64,128]{2,1,0:T(8,128)S(1)} %get-tuple-element.34.x_ref, bf16[14,16,128]{2,1,0:T(8,128)(2,1)S(1)} %collective-permute-done.7.a_ref, bf16[14,16,128]{2,1,0:T(8,128)(2,1)S(1)} %collective-permute-done.8.b_ref, f32[14,112,128]{2,1,0:T(8,128)S(1)} %get-tuple-element.37.keep_ref, ...), custom_call_target="tpu_custom_call" | custom-call | tf_op jit(solution)/shard_map/gradient/pallas_call | solution.py:457
Async XLA Ops:
  0.0 1.0 %copy-start = (f32[4,3,64,128]{3,2,1,0:T(8,128)S(1)}, f32[4,3,64,128]{3,2,1,0:T(8,128)}, u32[]{:S(2)}) copy-start(f32[4,3,64,128]{3,2,1,0:T(8,128)} %model_ref.5) | copy-start | bytes 1179652
  1.0 1.0 %copy-start.1 = (f32[2,6,64,128]{3,2,1,0:T(8,128)S(1)}, f32[2,6,64,128]{3,2,1,0:T(8,128)}, u32[]{:S(2)}) copy-start(f32[2,6,64,128]{3,2,1,0:T(8,128)} %control_ref.5) | copy-start | bytes 1179652
  2.0 0.8 %copy-start.3 = (s32[64,128]{1,0:T(8,128)S(1)}, s32[64,128]{1,0:T(8,128)}, u32[]{:S(2)}) copy-start(s32[64,128]{1,0:T(8,128)} %bottom_ref.7) | copy-start | bytes 98308
  3.1 8.9 %collective-permute-start = (bf16[64,256]{1,0:T(8,128)(2,1)S(1)}, bf16[64,256]{1,0:T(8,128)(2,1)S(1)}, u32[]{:S(2)}, u32[]{:S(2)}) collective-permute-start(bf16[64,256]{1,0:T(8,128)(2,1)S(1)} %get-tuple-element.22), channel_id=1, source_target_pairs={{0,8},{8,0},{16,24},{24,16},{32,40},{40,32},{48,56},{56,48},{64,72... | collective-permute-start | bytes 98312 | tf_op jit(solution)/shard_map/ppermute | solution.py:480
  6.4 16.5 %copy-start.4 = (s32[64,128]{1,0:T(8,128)S(1)}, s32[64,128]{1,0:T(8,128)}, u32[]{:S(2)}) copy-start(s32[64,128]{1,0:T(8,128)} %bottom_ref.7) | copy-start | bytes 98308
  6.4 7.5 %collective-permute-start.1 = (bf16[64,256]{1,0:T(8,128)(2,1)S(1)}, bf16[64,256]{1,0:T(8,128)(2,1)S(1)}, u32[]{:S(2)}, u32[]{:S(2)}) collective-permute-start(bf16[64,256]{1,0:T(8,128)(2,1)S(1)} %get-tuple-element.23), channel_id=1, source_target_pairs={{8,16},{16,8},{24,32},{32,24},{40,48},{48,40},{56,64},{64,56},{72,... | collective-permute-start | bytes 98312 | tf_op jit(solution)/shard_map/ppermute | solution.py:480
  14.1 4.4 %collective-permute-start.2 = (bf16[18,16,128]{2,1,0:T(8,128)(2,1)S(1)}, bf16[18,16,128]{2,1,0:T(8,128)(2,1)S(1)}, u32[]{:S(2)}, u32[]{:S(2)}) collective-permute-start(bf16[18,16,128]{2,1,0:T(8,128)(2,1)S(1)} %get-tuple-element.26), channel_id=1, source_target_pairs={{0,1},{1,0},{2,3},{3,2},{4,5},{5,4},{6,7},{7,6},{8,9},{9,8},{10,11... | collective-permute-start | bytes 221192 | tf_op jit(solution)/shard_map/ppermute | solution.py:480
  15.8 7.1 %collective-permute-start.3 = (bf16[18,16,128]{2,1,0:T(8,128)(2,1)S(1)}, bf16[18,16,128]{2,1,0:T(8,128)(2,1)S(1)}, u32[]{:S(2)}, u32[]{:S(2)}) collective-permute-start(bf16[18,16,128]{2,1,0:T(8,128)(2,1)S(1)} %get-tuple-element.27), channel_id=1, source_target_pairs={{1,2},{2,1},{3,4},{4,3},{5,6},{6,5},{9,10},{10,9},{11,12},{12,11},... | collective-permute-start | bytes 221192 | tf_op jit(solution)/shard_map/ppermute | solution.py:480
  24.6 6.4 %copy-start.5 = (f32[2,6,64,128]{3,2,1,0:T(8,128)S(1)}, f32[2,6,64,128]{3,2,1,0:T(8,128)}, u32[]{:S(2)}) copy-start(f32[2,6,64,128]{3,2,1,0:T(8,128)} %error_ref.1) | copy-start | bytes 1179652
  24.6 6.4 %collective-permute-start.4 = (f32[2,3,64,128]{3,2,1,0:T(8,128)S(1)}, f32[2,3,64,128]{3,2,1,0:T(8,128)S(1)}, u32[]{:S(2)}, u32[]{:S(2)}) collective-permute-start(f32[2,3,64,128]{3,2,1,0:T(8,128)S(1)} %get-tuple-element.30), channel_id=1, source_target_pairs={{0,128},{128,0},{1,129},{129,1},{2,130},{130,2},{3,131},{131,3},{4... | collective-permute-start | bytes 589832 | tf_op jit(solution)/shard_map/ppermute | solution.py:518
  25.4 5.6 %copy-start.6 = (f32[1,1,1,4,256]{4,3,2,1,0:T(4,128)S(1)}, f32[1,1,1,4,256]{4,3,2,1,0:T(4,128)}, u32[]{:S(2)}) copy-start(f32[1,1,1,4,256]{4,3,2,1,0:T(4,128)} %weight_ref.1) | copy-start | bytes 12292
  25.4 5.6 %copy-start.8 = (f32[1,1,1,256]{3,2,1,0:T(1,128)S(1)}, f32[1,1,1,256]{3,2,1,0:T(1,128)}, u32[]{:S(2)}) copy-start(f32[1,1,1,256]{3,2,1,0:T(1,128)} %value_ref.1) | copy-start | bytes 3076
  25.4 5.6 %copy-start.9 = (f32[1,1,1,256]{3,2,1,0:T(1,128)S(1)}, f32[1,1,1,256]{3,2,1,0:T(1,128)}, u32[]{:S(2)}) copy-start(f32[1,1,1,256]{3,2,1,0:T(1,128)} %precision_ref.1) | copy-start | bytes 3076
  31.0 0.7 %copy-start.7 = (s32[1,1,1,256]{3,2,1,0:T(1,128)S(1)}, s32[1,1,1,256]{3,2,1,0:T(1,128)}, u32[]{:S(2)}) copy-start(s32[1,1,1,256]{3,2,1,0:T(1,128)} %corner_ref.1) | copy-start | bytes 3076
  33.2 17.3 %copy-start.2 = (f32[2,6,64,128]{3,2,1,0:T(8,128)S(1)}, f32[2,6,64,128]{3,2,1,0:T(8,128)}, u32[]{:S(2)}) copy-start(f32[2,6,64,128]{3,2,1,0:T(8,128)} %control_ref.5) | copy-start | bytes 1179652
  33.3 6.8 %collective-permute-start.5 = (bf16[64,256]{1,0:T(8,128)(2,1)S(1)}, bf16[64,256]{1,0:T(8,128)(2,1)S(1)}, u32[]{:S(2)}, u32[]{:S(2)}) collective-permute-start(bf16[64,256]{1,0:T(8,128)(2,1)S(1)} %get-tuple-element.32), channel_id=1, source_target_pairs={{0,8},{8,0},{16,24},{24,16},{32,40},{40,32},{48,56},{56,48},{64,72... | collective-permute-start | bytes 98312 | tf_op jit(solution)/shard_map/ppermute | solution.py:480
  33.4 8.6 %collective-permute-start.6 = (bf16[64,256]{1,0:T(8,128)(2,1)S(1)}, bf16[64,256]{1,0:T(8,128)(2,1)S(1)}, u32[]{:S(2)}, u32[]{:S(2)}) collective-permute-start(bf16[64,256]{1,0:T(8,128)(2,1)S(1)} %get-tuple-element.33), channel_id=1, source_target_pairs={{8,16},{16,8},{24,32},{32,24},{40,48},{48,40},{56,64},{64,56},{72,... | collective-permute-start | bytes 98312 | tf_op jit(solution)/shard_map/ppermute | solution.py:480
  42.1 4.3 %collective-permute-start.7 = (bf16[14,16,128]{2,1,0:T(8,128)(2,1)S(1)}, bf16[14,16,128]{2,1,0:T(8,128)(2,1)S(1)}, u32[]{:S(2)}, u32[]{:S(2)}) collective-permute-start(bf16[14,16,128]{2,1,0:T(8,128)(2,1)S(1)} %get-tuple-element.35), channel_id=1, source_target_pairs={{0,1},{1,0},{2,3},{3,2},{4,5},{5,4},{6,7},{7,6},{8,9},{9,8},{10,11... | collective-permute-start | bytes 172040 | tf_op jit(solution)/shard_map/ppermute | solution.py:480
  43.6 7.0 %collective-permute-start.8 = (bf16[14,16,128]{2,1,0:T(8,128)(2,1)S(1)}, bf16[14,16,128]{2,1,0:T(8,128)(2,1)S(1)}, u32[]{:S(2)}, u32[]{:S(2)}) collective-permute-start(bf16[14,16,128]{2,1,0:T(8,128)(2,1)S(1)} %get-tuple-element.36), channel_id=1, source_target_pairs={{1,2},{2,1},{3,4},{4,3},{5,6},{6,5},{9,10},{10,9},{11,12},{12,11},... | collective-permute-start | bytes 172040 | tf_op jit(solution)/shard_map/ppermute | solution.py:480

commit v2 on v0

v2 whole, which is shorter than its diff:
```python
import jax
import jax.numpy as jnp
from jax import lax
from jax.experimental import pallas as pl
from jax.experimental.pallas import tpu as pltpu
from jax.sharding import PartitionSpec as P

SWEEPS = 10
SMOOTHING = 0.2
ADVECTION = 0.1
MIXING = 0.15

PAIR = 2
LEVELS = 6
HALF = 3
FIELDS = 4
PLANES = PAIR * LEVELS
STEPPED = FIELDS * HALF
ROWS = 64
COLS = 128
HALO = SWEEPS
EDGE = 16
TALL = ROWS + 2 * EDGE
PAD = 8
DEEP = TALL + 2 * PAD
BAND = 3 * HALO
LANES = COLS // BAND
BANDS = PLANES // LANES
DEPTH_ROW = PLANES * HALO
MODEL_ROW = DEPTH_ROW + HALO
LONG = 160
SHORT = 128
MODEL_LANE = 16
TRAVEL = jnp.bfloat16
F32 = jnp.float32
VMEM = pltpu.VMEM


def lanes(rows):
    return lax.broadcasted_iota(jnp.int32, (rows, COLS), 1)


def window(lane, start, width):
    start %= COLS
    stop = start + width
    if stop > COLS:
        return (lane >= start) | (lane < stop - COLS)
    return (lane >= start) & (lane < stop)


def roll(value, shift):
    shift %= COLS
    return value if shift == 0 else pltpu.roll(value, shift, 1)


def even_on(axis):
    return lax.axis_index(axis) % 2 == 0


def sides(first, second, even):
    first, second = first.astype(F32), second.astype(F32)
    return jnp.where(even, second, first), jnp.where(even, first, second)


def turn(plane):
    return BAND * (plane % LANES) + 2 * HALO


def stage(low_ref, high_ref, low, high):
    for plane in range(PLANES):
        here = slice(plane * HALO, (plane + 1) * HALO)
        low_ref[here, :] = low(plane)
        high_ref[here, :] = high(plane)


def send_rows(low_ref, high_ref, first_ref, second_ref):
    even = even_on("mer")
    low, high = low_ref[...], high_ref[...]
    first_ref[...] = jnp.where(even, high, low).astype(TRAVEL)
    second_ref[...] = jnp.where(even, low, high).astype(TRAVEL)


def start_kernel(
    model_ref,
    control_ref,
    bottom_ref,
    first_ref,
    second_ref,
    control_low,
    control_high,
    model_low,
    model_high,
    bottom_low,
    bottom_high,
    low_ref,
    high_ref,
    sems,
):
    ends = pl.ds(0, EDGE), pl.ds(ROWS - EDGE, EDGE)
    tips = pl.ds(0, 8), pl.ds(ROWS - 8, 8)
    copies = [
        pltpu.make_async_copy(control_ref.at[:, :, ends[0], :], control_low, sems.at[0]),
        pltpu.make_async_copy(control_ref.at[:, :, ends[1], :], control_high, sems.at[1]),
        pltpu.make_async_copy(model_ref.at[:, :, tips[0], :], model_low, sems.at[2]),
        pltpu.make_async_copy(model_ref.at[:, :, tips[1], :], model_high, sems.at[3]),
        pltpu.make_async_copy(bottom_ref.at[ends[0], :], bottom_low, sems.at[4]),
        pltpu.make_async_copy(bottom_ref.at[ends[1], :], bottom_high, sems.at[5]),
    ]
    for copy in copies:
        copy.start()
    for copy in copies:
        copy.wait()
    stage(
        low_ref,
        high_ref,
        lambda p: control_low[p // LEVELS, p % LEVELS, :HALO, :],
        lambda p: control_high[p // LEVELS, p % LEVELS, EDGE - HALO :, :],
    )
    low_ref[DEPTH_ROW:MODEL_ROW, :] = bottom_low[:HALO, :].astype(F32)
    high_ref[DEPTH_ROW:MODEL_ROW, :] = bottom_high[EDGE - HALO :, :].astype(F32)
    for q in range(STEPPED):
        for ref, value in (
            (low_ref, model_low[q // HALF, q % HALF, :1, :]),
            (high_ref, model_high[q // HALF, q % HALF, 7:, :]),
        ):
            coarse = value.astype(TRAVEL).astype(F32)
            at = MODEL_ROW + q
            ref[at : at + 1, :] = coarse
            ref[at + STEPPED : at + STEPPED + 1, :] = value - coarse
    rest = MODEL_ROW + 2 * STEPPED
    low_ref[rest:, :] = jnp.zeros((LONG - rest, COLS), F32)
    high_ref[rest:, :] = jnp.zeros((LONG - rest, COLS), F32)
    send_rows(low_ref, high_ref, first_ref, second_ref)


def stand(value, low, high):
    blank = jnp.zeros((EDGE - HALO, COLS), F32)
    return jnp.concatenate([blank, low, value, high, blank], axis=0)


def raise_planes(read, first_ref, second_ref, low_ref, high_ref, tall_ref):
    low, high = sides(first_ref[...], second_ref[...], even_on("mer"))
    low_ref[...] = low
    high_ref[...] = high
    blank = jnp.zeros((EDGE - HALO, COLS), F32)
    for plane in range(PLANES):
        here = slice(plane * HALO, (plane + 1) * HALO)
        tall_ref[plane, : EDGE - HALO, :] = blank
        tall_ref[plane, EDGE - HALO : EDGE, :] = low_ref[here, :]
        tall_ref[plane, EDGE : EDGE + ROWS, :] = read(plane)
        tall_ref[plane, EDGE + ROWS : EDGE + ROWS + HALO, :] = high_ref[here, :]
        tall_ref[plane, EDGE + ROWS + HALO :, :] = blank


def cut_bands(tall_ref, west_ref, east_ref):
    lane = lanes(TALL)
    blank = jnp.zeros((TALL, COLS), F32)
    to_east, to_west = blank, blank
    for group in range(BANDS):
        west = east = go_east = go_west = blank
        for j in range(LANES):
            plane = group * LANES + j
            turned = roll(tall_ref[plane], turn(plane))
            at = BAND * j
            west = jnp.where(window(lane, at + 2 * HALO, 2 * HALO), turned, west)
            east = jnp.where(window(lane, at, 2 * HALO), turned, east)
            go_east = jnp.where(window(lane, at + HALO, HALO), turned, go_east)
            go_west = jnp.where(window(lane, at + 2 * HALO, HALO), turned, go_west)
        west_ref[group] = west
        east_ref[group] = east
        to_east = to_east + roll(go_east, HALO * group)
        to_west = to_west + roll(go_west, HALO * group)
    return to_east, to_west


def send_columns(part, to_east, to_west, first_ref, second_ref):
    even = even_on("zon")
    here = slice(part * COLS, (part + 1) * COLS)
    first_ref[:, here] = jnp.where(even, to_east, to_west).astype(TRAVEL)
    second_ref[:, here] = jnp.where(even, to_west, to_east).astype(TRAVEL)


def first_columns_kernel(
    model_ref,
    control_ref,
    bottom_ref,
    a_ref,
    b_ref,
    tall_ref,
    depth_ref,
    west_ref,
    east_ref,
    first_ref,
    second_ref,
    low_ref,
    high_ref,
):
    raise_planes(
        lambda p: control_ref[p // LEVELS, p % LEVELS], a_ref, b_ref, low_ref, high_ref, tall_ref
    )
    send_columns(0, *cut_bands(tall_ref, west_ref, east_ref), first_ref, second_ref)
    depth = stand(
        bottom_ref[...].astype(F32),
        low_ref[DEPTH_ROW:MODEL_ROW, :],
        high_ref[DEPTH_ROW:MODEL_ROW, :],
    )
    depth_ref[...] = depth
    tall_lane = lanes(TALL)
    lane = lanes(ROWS)
    to_east = to_west = jnp.zeros((ROWS, COLS), F32)
    for q in range(STEPPED):
        value = model_ref[q // HALF, q % HALF]
        at = MODEL_LANE + 2 * q
        column = value[:, COLS - 1 :]
        coarse = column.astype(TRAVEL).astype(F32)
        to_east = jnp.where(lane == at, coarse, to_east)
        to_east = jnp.where(lane == at + 1, column - coarse, to_east)
        column = value[:, :1]
        coarse = column.astype(TRAVEL).astype(F32)
        to_west = jnp.where(lane == at - 1, coarse, to_west)
        to_west = jnp.where(lane == at - 2, column - coarse, to_west)
    blank = jnp.zeros((EDGE, COLS), F32)
    mark = tall_lane < HALO
    send_columns(
        1,
        jnp.where(mark, roll(depth, HALO), jnp.concatenate([blank, to_east, blank], axis=0)),
        jnp.where(mark, depth, jnp.concatenate([blank, to_west, blank], axis=0)),
        first_ref,
        second_ref,
    )


def next_columns_kernel(
    field_ref, a_ref, b_ref, tall_ref, west_ref, east_ref, first_ref, second_ref, low_ref, high_ref
):
    raise_planes(lambda p: field_ref[p], a_ref, b_ref, low_ref, high_ref, tall_ref)
    send_columns(0, *cut_bands(tall_ref, west_ref, east_ref), first_ref, second_ref)


def base_step(model_ref, depth_ref, a_ref, b_ref, base_ref, low_ref, high_ref, tall_ref):
    lane = lanes(ROWS)
    group = lax.axis_index("grp")
    low, high = sides(a_ref[...], b_ref[...], even_on("mer"))
    low_ref[...] = low
    high_ref[...] = high
    core = slice(EDGE, EDGE + ROWS)
    south, north = slice(EDGE - 1, EDGE + ROWS - 1), slice(EDGE + 1, EDGE + ROWS + 1)
    depth = depth_ref[core, :]
    around = (
        depth,
        jnp.where(lane == COLS - 1, 0.0, roll(depth, -1)),
        jnp.where(lane == 0, 0.0, roll(depth, 1)),
        depth_ref[north, :],
        depth_ref[south, :],
    )
    for level in range(HALF):
        here = (group * HALF + level).astype(F32)
        wet, wet_e, wet_w, wet_n, wet_s = (jnp.where(v > here, 1.0, 0.0) for v in around)
        count = MIXING * (wet_e + wet_w + wet_n + wet_s)
        flow_x = 0.5 * ADVECTION * model_ref[2, level]
        flow_y = 0.5 * ADVECTION * model_ref[3, level]
        give_e, give_w = wet_e * (MIXING - flow_x), wet_w * (MIXING + flow_x)
        give_n, give_s = wet_n * (MIXING - flow_y), wet_s * (MIXING + flow_y)
        for field in range(FIELDS):
            at = MODEL_ROW + field * HALF + level
            value = model_ref[field, level]
            tall_ref[8 : 8 + ROWS, :] = value
            tall_ref[7:8, :] = low_ref[at : at + 1, :] + low_ref[at + STEPPED : at + STEPPED + 1, :]
            tall_ref[8 + ROWS : 9 + ROWS, :] = (
                high_ref[at : at + 1, :] + high_ref[at + STEPPED : at + STEPPED + 1, :]
            )
            base_ref[field, level] = wet * (
                value * (1.0 - count)
                + give_e * roll(value, -1)
                + give_w * roll(value, 1)
                + give_n * tall_ref[9 : 9 + ROWS, :]
                + give_s * tall_ref[7 : 7 + ROWS, :]
            )


def background_kernel(model_ref, depth_ref, base_ref, first_ref, second_ref, keep_ref, send_ref):
    lane = lanes(ROWS)
    group = lax.axis_index("grp")
    core = slice(EDGE, EDGE + ROWS)
    before, after = sides(first_ref[core, COLS:], second_ref[core, COLS:], even_on("zon"))
    at_west, at_east = lane == 0, lane == COLS - 1
    beside = jnp.where(at_west, roll(before, 1 - HALO), jnp.where(at_east, roll(after, -1), 0.0))
    depth = jnp.minimum(depth_ref[core, :], beside)
    columns = jnp.where(lane % 2 == 0, before + roll(before, -1), after + roll(after, 1))
    sign = jnp.where(at_west, 0.5 * ADVECTION, -0.5 * ADVECTION)
    for level in range(HALF):
        wet = depth > (group * HALF + level).astype(F32)
        gain = jnp.where(wet, MIXING + sign * model_ref[2, level], 0.0)
        loss = jnp.where(wet, MIXING, 0.0)
        for field in range(FIELDS):
            halo = roll(columns, -(MODEL_LANE + 2 * (field * HALF + level)))
            result = base_ref[field, level] + (gain * halo - loss * model_ref[field, level])
            own = group == field // 2

            @pl.when(own)
            def _():
                keep_ref[field % 2, level] = result

            @pl.when(jnp.logical_not(own))
            def _():
                send_ref[field % 2, level] = result


def neighbour_sum(ref, index, start, rows):
    here = ref[index, pl.ds(start, rows), :]
    return here, (roll(here, -1) + roll(here, 1)) + (
        ref[index, pl.ds(start - 1, rows), :] + ref[index, pl.ds(start + 1, rows), :]
    )


def coefficients(mask_ref, count, keep_ref, give_ref):
    for index in range(count):
        wet, total = neighbour_sum(mask_ref, index, PAD, TALL)
        keep_ref[index, PAD : PAD + TALL, :] = wet * (1.0 - SMOOTHING * total)
        give_ref[index, PAD : PAD + TALL, :] = SMOOTHING * wet


def sweep_all(count, masks, keep_ref, give_ref, one_ref, two_ref):
    def sweep(source_ref, target_ref, start, rows):
        for index in range(count):
            here, total = neighbour_sum(source_ref, index, start, rows)
            at = pl.ds(start, rows)
            target_ref[index, at, :] = (
                keep_ref[index % masks, at, :] * here + give_ref[index % masks, at, :] * total
            )

    sweep(one_ref, two_ref, PAD, TALL)
    sweep(two_ref, one_ref, 2 * PAD, TALL - 2 * PAD)

    def step(index, carry):
        sweep(one_ref, two_ref, 2 * PAD, TALL - 2 * PAD)
        sweep(two_ref, one_ref, 2 * PAD, TALL - 2 * PAD)
        return carry

    lax.fori_loop(0, SWEEPS // 2 - 1, step, 0)


def clear_pads(ref, count):
    for index in range(count):
        ref[index, :PAD, :] = jnp.zeros((PAD, COLS), F32)
        ref[index, PAD + TALL :, :] = jnp.zeros((PAD, COLS), F32)


CORE = slice(PAD + EDGE, PAD + EDGE + ROWS)
BODY = slice(PAD, PAD + TALL)


def first_interior_kernel(
    tall_ref,
    depth_ref,
    model_ref,
    a_ref,
    b_ref,
    inner_ref,
    keep_ref,
    give_ref,
    base_ref,
    mask_ref,
    one_ref,
    two_ref,
    low_ref,
    high_ref,
    stand_ref,
):
    base_step(model_ref, depth_ref, a_ref, b_ref, base_ref, low_ref, high_ref, stand_ref)
    clear_pads(mask_ref, LEVELS)
    clear_pads(one_ref, PLANES)
    depth = depth_ref[...]
    for level in range(LEVELS):
        wet = jnp.where(depth > level, 1.0, 0.0)
        mask_ref[level, BODY, :] = wet
        for field in range(PAIR):
            plane = field * LEVELS + level
            one_ref[plane, BODY, :] = wet * tall_ref[plane]
    coefficients(mask_ref, LEVELS, keep_ref, give_ref)
    sweep_all(PLANES, LEVELS, keep_ref, give_ref, one_ref, two_ref)
    for plane in range(PLANES):
        inner_ref[plane] = one_ref[plane, CORE, :]


def next_interior_kernel(tall_ref, keep_ref, give_ref, inner_ref, one_ref, two_ref):
    clear_pads(one_ref, PLANES)
    for plane in range(PLANES):
        one_ref[plane, BODY, :] = tall_ref[plane]
    sweep_all(PLANES, LEVELS, keep_ref, give_ref, one_ref, two_ref)
    for plane in range(PLANES):
        inner_ref[plane] = one_ref[plane, CORE, :]


def fill_bands(first_ref, second_ref, west_ref, east_ref, one_ref, mask_ref):
    lane = lanes(TALL)
    before, after = sides(first_ref[:, :COLS], second_ref[:, :COLS], even_on("zon"))
    clear_pads(one_ref, 2 * BANDS)
    in_west = (lane >= HALO) & ((lane - HALO) % BAND < HALO)
    in_east = (lane >= 2 * HALO) & ((lane - 2 * HALO) % BAND < HALO)
    for group in range(BANDS):
        west = jnp.where(in_west, roll(before, -HALO * group), west_ref[group])
        east = jnp.where(in_east, roll(after, -HALO * group), east_ref[group])
        for index, value in ((group, west), (BANDS + group, east)):
            if mask_ref is not None:
                value = value * mask_ref[index, BODY, :]
            one_ref[index, BODY, :] = value


def join_bands(one_ref, plane, inner, lane):
    group, j = divmod(plane, LANES)
    value = jnp.where(
        window(lane, BAND * j + 2 * HALO, HALO),
        one_ref[group, CORE, :],
        one_ref[BANDS + group, CORE, :],
    )
    edge = (lane < HALO) | (lane >= COLS - HALO)
    return jnp.where(edge, roll(value, -turn(plane)), inner)


def first_bands_kernel(
    first_ref,
    second_ref,
    west_ref,
    east_ref,
    depth_ref,
    inner_ref,
    out_ref,
    keep_ref,
    give_ref,
    mask_ref,
    one_ref,
    two_ref,
):
    tall_lane = lanes(TALL)
    clear_pads(mask_ref, 2 * BANDS)
    before, after = sides(first_ref[:, COLS:], second_ref[:, COLS:], even_on("zon"))
    depth = depth_ref[...]
    blank = jnp.zeros((TALL, COLS), F32)
    west, east = [blank] * BANDS, [blank] * BANDS
    for j in range(LANES):
        at = BAND * j
        turned = roll(depth, turn(j))
        low = jnp.where(window(tall_lane, at + HALO, HALO), roll(before, at + HALO), turned)
        high = jnp.where(window(tall_lane, at + 2 * HALO, HALO), roll(after, at + 2 * HALO), turned)
        for group in range(BANDS):
            level = (group * LANES + j) % LEVELS
            west[group] = jnp.where(
                window(tall_lane, at + HALO, BAND), jnp.where(low > level, 1.0, 0.0), west[group]
            )
            east[group] = jnp.where(
                window(tall_lane, at, BAND), jnp.where(high > level, 1.0, 0.0), east[group]
            )
    for group in range(BANDS):
        mask_ref[group, BODY, :] = west[group]
        mask_ref[BANDS + group, BODY, :] = east[group]
    coefficients(mask_ref, 2 * BANDS, keep_ref, give_ref)
    fill_bands(first_ref, second_ref, west_ref, east_ref, one_ref, mask_ref)
    sweep_all(2 * BANDS, 2 * BANDS, keep_ref, give_ref, one_ref, two_ref)
    lane = lanes(ROWS)
    for plane in range(PLANES):
        out_ref[plane] = join_bands(one_ref, plane, inner_ref[plane], lane)


def gradient_kernel(
    first_ref,
    second_ref,
    west_ref,
    east_ref,
    inner_ref,
    keep_ref,
    give_ref,
    control_ref,
    out_ref,
    one_ref,
    two_ref,
):
    fill_bands(first_ref, second_ref, west_ref, east_ref, one_ref, None)
    sweep_all(2 * BANDS, 2 * BANDS, keep_ref, give_ref, one_ref, two_ref)
    lane = lanes(ROWS)
    for plane in range(PLANES):
        f, k = divmod(plane, LEVELS)
        out_ref[f, k] = control_ref[f, k] + join_bands(one_ref, plane, inner_ref[plane], lane)


def split(value):
    coarse = value.astype(jnp.bfloat16)
    return jnp.concatenate([coarse, (value - coarse.astype(F32)).astype(jnp.bfloat16)], axis=1)


def join(value):
    return value[:, :COLS] + value[:, COLS:]


def observe_kernel(
    count_ref,
    smooth_ref,
    error_ref,
    bottom_ref,
    keep_ref,
    other_ref,
    corner_ref,
    weight_ref,
    value_ref,
    precision_ref,
    field_ref,
    first_ref,
    second_ref,
    total_ref,
    low_ref,
    high_ref,
):
    group = lax.axis_index("grp")
    slots = corner_ref.shape[-1]
    depth = bottom_ref[...]
    for plane in range(PLANES):
        f, k = divmod(plane, LEVELS)
        scale = jnp.where(depth > k, error_ref[f, k], 0.0)
        held = group == k // HALF
        prior = jnp.where(held, keep_ref[f, k % HALF], other_ref[f, k % HALF])
        total_ref[plane * ROWS : (plane + 1) * ROWS, :] = scale * smooth_ref[plane] + prior
    corner = corner_ref[0, 0]
    row = (corner >> 7).astype(F32)
    column = (corner & (COLS - 1)).astype(F32)
    stacked = jnp.concatenate(
        [weight_ref[0, 0, 0], value_ref[0, 0], precision_ref[0, 0], row, column], axis=0
    )
    tall = jnp.transpose(stacked)
    row_tall = jnp.concatenate([tall[:, 6:7], tall[:, 6:7] + 1.0], axis=0)
    cells = PLANES * ROWS
    wide_row = lax.broadcasted_iota(jnp.int32, (2 * slots, cells), 1).astype(F32)
    pick = jnp.where(wide_row == row_tall, 1.0, 0.0).astype(jnp.bfloat16)
    seen = join(jnp.dot(pick, split(total_ref[...]), preferred_element_type=F32))
    lane = lanes(slots).astype(F32)
    at, beside = lane == tall[:, 7:8], lane == tall[:, 7:8] + 1.0
    lower = jnp.where(at, tall[:, 0:1], jnp.where(beside, tall[:, 1:2], 0.0))
    upper = jnp.where(at, tall[:, 2:3], jnp.where(beside, tall[:, 3:4], 0.0))
    observed = jnp.sum(lower * seen[:slots] + upper * seen[slots:], axis=1, keepdims=True)
    live = lax.broadcasted_iota(jnp.int32, (slots, 1), 0) < count_ref[0, 0, 0]
    misfit = jnp.where(live, tall[:, 5:6] * (observed - tall[:, 4:5]), 0.0)
    spread = jnp.concatenate([lower * misfit, upper * misfit], axis=0)
    tall_row = lax.broadcasted_iota(jnp.int32, (cells, slots), 0).astype(F32)
    back = jnp.concatenate(
        [
            jnp.where(tall_row == row, 1.0, 0.0).astype(jnp.bfloat16),
            jnp.where(tall_row == row + 1.0, 1.0, 0.0).astype(jnp.bfloat16),
        ],
        axis=1,
    )
    total_ref[...] = join(jnp.dot(back, split(spread), preferred_element_type=F32))
    for plane in range(PLANES):
        f, k = divmod(plane, LEVELS)
        scale = jnp.where(depth > k, error_ref[f, k], 0.0)
        field_ref[plane] = scale * total_ref[plane * ROWS : (plane + 1) * ROWS, :]
    stage(
        low_ref,
        high_ref,
        lambda p: field_ref[p, :HALO, :],
        lambda p: field_ref[p, ROWS - HALO :, :],
    )
    blank = jnp.zeros((SHORT - DEPTH_ROW, COLS), F32)
    low_ref[DEPTH_ROW:, :] = blank
    high_ref[DEPTH_ROW:, :] = blank
    send_rows(low_ref, high_ref, first_ref, second_ref)


def call(kernel, outs, scratch=(), scalars=0, remote=False, work=0):
    space = pltpu.HBM if remote else VMEM

    def run(*args):
        return pl.pallas_call(
            kernel,
            out_shape=[jax.ShapeDtypeStruct(shape, kind) for shape, kind in outs],
            in_specs=[
                pl.BlockSpec(memory_space=pltpu.SMEM if i < scalars else space)
                for i in range(len(args))
            ],
            out_specs=[pl.BlockSpec(memory_space=VMEM) for _ in outs],
            scratch_shapes=list(scratch),
            compiler_params=pltpu.CompilerParams(vmem_limit_bytes=24 * 2**20),
            cost_estimate=pl.CostEstimate(
                flops=work, bytes_accessed=work // 10, transcendentals=0
            )
            if work
            else None,
            name=kernel.__name__.removesuffix("_kernel"),
        )(*args)

    return run


def swap(value, axis, shift, wrap):
    size = lax.axis_size(axis)
    pairs = []
    for i in range(shift, size + shift - 1, 2):
        j = i + 1
        if j < size or wrap:
            pairs += [(i, j % size), (j % size, i)]
    return lax.ppermute(value, axis, pairs)


def exchange(first, second, axis, wrap):
    return swap(first, axis, 0, wrap), swap(second, axis, 1, wrap)


FULL = ((PLANES, ROWS, COLS), F32)
RAISED = ((PLANES, TALL, COLS), F32)
SIDE = ((BANDS, TALL, COLS), F32)
STEP = ((FIELDS, HALF, ROWS, COLS), F32)
PART = ((PAIR, HALF, ROWS, COLS), F32)
MASKS = ((LEVELS, DEEP, COLS), F32)
STRIP = ((2 * BANDS, DEEP, COLS), F32)


def rows_of(count):
    return ((count, COLS), TRAVEL)


def columns_of(count):
    return ((TALL, count * COLS), TRAVEL)


def body(
    model_state,
    control,
    error_std,
    bottom_level,
    obs_count,
    obs_corner,
    obs_weight,
    obs_value,
    obs_precision,
):
    dma = pltpu.SemaphoreType.DMA
    long, short = VMEM((LONG, COLS), F32), VMEM((SHORT, COLS), F32)
    first, second = call(
        start_kernel,
        [rows_of(LONG)] * 2,
        [VMEM((PAIR, LEVELS, EDGE, COLS), F32)] * 2
        + [VMEM((FIELDS, HALF, 8, COLS), F32)] * 2
        + [VMEM((EDGE, COLS), jnp.int32)] * 2
        + [long, long, dma((6,))],
        remote=True,
    )(model_state, control, bottom_level)
    mer = exchange(first, second, "mer", False)
    tall, depth, west, east, first, second = call(
        first_columns_kernel,
        [RAISED, ((TALL, COLS), F32), SIDE, SIDE, columns_of(2), columns_of(2)],
        [long, long],
    )(model_state, control, bottom_level, *mer)
    zon = exchange(first, second, "zon", True)
    inner, keep_coef, give_coef, base = call(
        first_interior_kernel,
        [FULL, MASKS, MASKS, STEP],
        [VMEM(*MASKS)]
        + [VMEM((PLANES, DEEP, COLS), F32)] * 2
        + [long, long, VMEM((ROWS + 16, COLS), F32)],
        work=10**7,
    )(tall, depth, model_state, *mer)
    keep, send = call(background_kernel, [PART, PART])(model_state, depth, base, *zon)
    other = lax.ppermute(send, "grp", [(0, 1), (1, 0)])
    smoothed, keep_band, give_band = call(
        first_bands_kernel, [FULL, STRIP, STRIP], [VMEM(*STRIP)] * 3, work=10**7
    )(*zon, west, east, depth, inner)
    field, first, second = call(
        observe_kernel,
        [FULL, rows_of(SHORT), rows_of(SHORT)],
        [VMEM((PLANES * ROWS, COLS), F32), short, short],
        scalars=1,
    )(
        obs_count,
        smoothed,
        error_std,
        bottom_level,
        keep,
        other,
        obs_corner,
        obs_weight,
        obs_value,
        obs_precision,
    )
    mer = exchange(first, second, "mer", False)
    tall, west, east, first, second = call(
        next_columns_kernel, [RAISED, SIDE, SIDE, columns_of(1), columns_of(1)], [short, short]
    )(field, *mer)
    zon = exchange(first, second, "zon", True)
    (inner,) = call(
        next_interior_kernel, [FULL], [VMEM((PLANES, DEEP, COLS), F32)] * 2, work=10**7
    )(tall, keep_coef, give_coef)
    return call(gradient_kernel, [(control.shape, F32)], [VMEM(*STRIP)] * 2)(
        *zon, west, east, inner, keep_band, give_band, control
    )[0]


def solution(mesh):
    return jax.shard_map(
        body,
        mesh=mesh,
        in_specs=(
            P(None, "grp", "mer", "zon"),
            P("grp", None, "mer", "zon"),
            P("grp", None, "mer", "zon"),
            P("mer", "zon"),
            P("grp", "mer", "zon"),
            P("grp", "mer", "zon", None),
            P("grp", "mer", "zon", None, None),
            P("grp", "mer", "zon", None),
            P("grp", "mer", "zon", None),
        ),
        out_specs=P("grp", None, "mer", "zon"),
        check_vma=False,
    )
```

time: 606 us -> 50.2 us (0.08)
  the two profiles are of different devices: /device:TPU:1 before, /device:TPU:10 now
where the time goes in v2:
time: 50.2 us; the launch traced here: 50 us
  starting transfers between devices  24.9 us (50%)
  Pallas kernels  15 us (30%)
  waiting for transfers between devices  5.79 us (12%)
  local copies, waits for them, and re-layouts  3.41 us (7%)
  between operations  0.89 us (2%)
    ppermute x8, starting transfers between devices, swap(): return lax.ppermute(value, axis, pairs)  24.8 us
    pallas_call x9, Pallas kernels, run(): pl.pallas_call(kernel, out_shape=[jax.ShapeDtypeStruct(shape, kind) for s...  15 us
    ppermute x8, waiting for transfers between devices, swap(): return lax.ppermute(value, axis, pairs)  5.78 us
    unnamed x20, local copies, waits for them, and re-layouts  3.41 us
  transfers between devices with their start and end apart: 9, of which 2 were waited for; matrix products, arithmetic and copies ran while one was open for 0% of the time, Pallas kernels for 17%

profile of v2, /device:TPU:10, one launch (start us, length us, event | category | flops | bytes accessed | tf_op | source)
XLA Modules:
  0.0 50.0 jit_solution(12515076492053710267)
XLA Ops:
  0.0 0.0 copy-start
  0.0 1.0 %copy-done = f32[4,3,64,128]{3,2,1,0:T(8,128)S(1)} copy-done((f32[4,3,64,128]{3,2,1,0:T(8,128)S(1)}, f32[4,3,64,128]{3,2,1,0:T(8,128)}, u32[]{:S(2)}) %copy-start) | copy-done | bytes 393240
  1.0 0.0 copy-start.1
  1.0 1.0 %copy-done.1 = f32[2,6,64,128]{3,2,1,0:T(8,128)S(1)} copy-done((f32[2,6,64,128]{3,2,1,0:T(8,128)S(1)}, f32[2,6,64,128]{3,2,1,0:T(8,128)}, u32[]{:S(2)}) %copy-start.1) | copy-done | bytes 393240
  2.0 0.0 copy-start.4
  2.0 0.8 %copy-done.4 = s32[64,128]{1,0:T(8,128)S(1)} copy-done((s32[64,128]{1,0:T(8,128)S(1)}, s32[64,128]{1,0:T(8,128)}, u32[]{:S(2)}) %copy-start.4) | copy-done | bytes 32792
  2.8 0.2 start.1
  2.9 0.5 %collective-permute-start = (bf16[160,128]{1,0:T(8,128)(2,1)S(1)}, bf16[160,128]{1,0:T(8,128)(2,1)S(1)}, u32[]{:S(2)}, u32[]{:S(2)}) collective-permute-start(bf16[160,128]{1,0:T(8,128)(2,1)S(1)} %get-tuple-element.30), channel_id=1, source_target_pairs={{0,1},{1,0},{2,3},{3,2},{4,5},{5,4},{6,7},{7,6},{8,9},{9,8},{10,11... | collective-permute-start | bytes 122888 | tf_op jit(solution)/shard_map/ppermute | solution.py:599
  3.5 4.4 %collective-permute-start.1 = (bf16[160,128]{1,0:T(8,128)(2,1)S(1)}, bf16[160,128]{1,0:T(8,128)(2,1)S(1)}, u32[]{:S(2)}, u32[]{:S(2)}) collective-permute-start(bf16[160,128]{1,0:T(8,128)(2,1)S(1)} %get-tuple-element.31), channel_id=1, source_target_pairs={{1,2},{2,1},{3,4},{4,3},{5,6},{6,5},{9,10},{10,9},{11,12},{12,11},... | collective-permute-start | bytes 122888 | tf_op jit(solution)/shard_map/ppermute | solution.py:599
  7.9 0.0 collective-permute-done.a_ref
  7.9 2.4 %collective-permute-done.1.b_ref = bf16[160,128]{1,0:T(8,128)(2,1)S(1)} collective-permute-done((bf16[160,128]{1,0:T(8,128)(2,1)S(1)}, bf16[160,128]{1,0:T(8,128)(2,1)S(1)}, u32[]{:S(2)}, u32[]{:S(2)}) %collective-permute-start.1) | collective-permute-done | bytes 40992 | tf_op jit(solution)/shard_map/ppermute | solution.py:599
  10.2 0.6 %first_columns.1 = (f32[12,96,128]{2,1,0:T(8,128)S(1)}, f32[96,128]{1,0:T(8,128)S(1)}, f32[3,96,128]{2,1,0:T(8,128)S(1)}, f32[3,96,128]{2,1,0:T(8,128)S(1)}, bf1...) custom-call(f32[4,3,64,128]{3,2,1,0:T(8,128)S(1)} %copy-done, f32[2,6,64,128]{3,2,1,0:T(8,128)S(1)} %copy-done.1, ...), custom_call_target="tpu_custom_call" | custom-call | tf_op jit(solution)/shard_map/first_columns/pallas_call | solution.py:571
  10.9 2.7 %collective-permute-start.2 = (bf16[96,256]{1,0:T(8,128)(2,1)S(1)}, bf16[96,256]{1,0:T(8,128)(2,1)S(1)}, u32[]{:S(2)}, u32[]{:S(2)}) collective-permute-start(bf16[96,256]{1,0:T(8,128)(2,1)S(1)} %get-tuple-element.32), channel_id=1, source_target_pairs={{0,8},{8,0},{16,24},{24,16},{32,40},{40,32},{48,56},{56,48},{64,72... | collective-permute-start | bytes 147464 | tf_op jit(solution)/shard_map/ppermute | solution.py:599
  13.6 6.2 %collective-permute-start.3 = (bf16[96,256]{1,0:T(8,128)(2,1)S(1)}, bf16[96,256]{1,0:T(8,128)(2,1)S(1)}, u32[]{:S(2)}, u32[]{:S(2)}) collective-permute-start(bf16[96,256]{1,0:T(8,128)(2,1)S(1)} %get-tuple-element.33), channel_id=1, source_target_pairs={{8,16},{16,8},{24,32},{32,24},{40,48},{48,40},{56,64},{64,56},{72,... | collective-permute-start | bytes 147464 | tf_op jit(solution)/shard_map/ppermute | solution.py:599
  19.8 3.4 %first_interior.1 = (f32[12,64,128]{2,1,0:T(8,128)S(1)}, f32[6,112,128]{2,1,0:T(8,128)S(1)}, f32[6,112,128]{2,1,0:T(8,128)S(1)}, f32[4,3,64,128]{3,2,1,0:T(8,128)S(1)}) custom-call(f32[12,96,128]{2,1,0:T(8,128)S(1)} %get-tuple-element.37.tall_ref, f32[96,128]{1,0:T(8,128)S(1)} %get-tuple-element.36.depth_ref, f32[4,3,64,128]{3,2,1,0:T(8,128)S(1)} %copy-done, ...), custom_call_target="tpu_custom_call" | custom-call | flops 10000000 | bytes 1000000 | tf_op jit(solution)/shard_map/first_interior/pallas_call | solution.py:571
  23.2 0.0 collective-permute-done.2.first_ref
  23.2 0.0 collective-permute-done.3.second_ref
  23.2 1.0 %background.1 = (f32[2,3,64,128]{3,2,1,0:T(8,128)S(1)}, f32[2,3,64,128]{3,2,1,0:T(8,128)S(1)}) custom-call(f32[4,3,64,128]{3,2,1,0:T(8,128)S(1)} %copy-done, f32[96,128]{1,0:T(8,128)S(1)} %get-tuple-element.36.depth_ref, f32[4,3,64,128]{3,2,1,0:T(8,128)S(1)} %get-tuple-element.40.base_ref, bf16[96,256]{1,0:T(8,128)(2,1)S(1)} %collective-permute-done.2.first_ref, ...), custom_call_target="tpu_custom_call" | custom-call | tf_op jit(solution)/shard_map/background/pallas_call | solution.py:571
  24.3 0.1 collective-permute-start.4
  25.0 0.0 copy-start.3
  25.0 0.0 copy-start.5
  25.0 0.0 copy-start.6
  25.0 0.0 copy-start.8
  25.1 0.0 copy-start.9
  25.1 2.2 %first_bands.1 = (f32[12,64,128]{2,1,0:T(8,128)S(1)}, f32[6,112,128]{2,1,0:T(8,128)S(1)}, f32[6,112,128]{2,1,0:T(8,128)S(1)}) custom-call(bf16[96,256]{1,0:T(8,128)(2,1)S(1)} %collective-permute-done.2.first_ref, bf16[96,256]{1,0:T(8,128)(2,1)S(1)} %collective-permute-done.3.second_ref, f32[3,96,128]{2,1,0:T(8,128)S(1)} %get-tuple-element.34.west_ref, ...), custom_call_target="tpu_custom_call" | custom-call | flops 10000000 | bytes 1000000 | tf_op jit(solution)/shard_map/first_bands/pallas_call | solution.py:571
  27.3 0.0 collective-permute-done.4.other_ref
  27.3 0.0 copy-start.7
  27.3 0.0 copy-done.3
  27.3 0.0 copy-done.5
  27.3 0.0 copy-done.6
  27.3 0.0 copy-done.8
  27.3 0.0 copy-done.9
  27.3 0.6 %copy-done.7 = s32[1,1,1,256]{3,2,1,0:T(1,128)S(1)} copy-done((s32[1,1,1,256]{3,2,1,0:T(1,128)S(1)}, s32[1,1,1,256]{3,2,1,0:T(1,128)}, u32[]{:S(2)}) %copy-start.7) | copy-done | bytes 1048
  28.0 1.6 %observe.1 = (f32[12,64,128]{2,1,0:T(8,128)S(1)}, bf16[128,128]{1,0:T(8,128)(2,1)S(1)}, bf16[128,128]{1,0:T(8,128)(2,1)S(1)}) custom-call(s32[1,1,1]{2,1,0:T(1,128)S(6)} %copy.10.count_ref, f32[12,64,128]{2,1,0:T(8,128)S(1)} %get-tuple-element.39.smooth_ref, f32[2,6,64,128]{3,2,1,0:T(8,128)S(1)} %copy-done.3, s32[64,128]{1,0:T(8,128)S(1)} %copy-done.5, ...), custom_call_target="tpu_custom_call" | custom-call | tf_op jit(solution)/shard_map/observe/pallas_call | solution.py:571
  29.5 1.7 %collective-permute-start.5 = (bf16[128,128]{1,0:T(8,128)(2,1)S(1)}, bf16[128,128]{1,0:T(8,128)(2,1)S(1)}, u32[]{:S(2)}, u32[]{:S(2)}) collective-permute-start(bf16[128,128]{1,0:T(8,128)(2,1)S(1)} %get-tuple-element.44), channel_id=1, source_target_pairs={{0,1},{1,0},{2,3},{3,2},{4,5},{5,4},{6,7},{7,6},{8,9},{9,8},{10,11... | collective-permute-start | bytes 98312 | tf_op jit(solution)/shard_map/ppermute | solution.py:599
  31.2 3.3 %collective-permute-start.6 = (bf16[128,128]{1,0:T(8,128)(2,1)S(1)}, bf16[128,128]{1,0:T(8,128)(2,1)S(1)}, u32[]{:S(2)}, u32[]{:S(2)}) collective-permute-start(bf16[128,128]{1,0:T(8,128)(2,1)S(1)} %get-tuple-element.45), channel_id=1, source_target_pairs={{1,2},{2,1},{3,4},{4,3},{5,6},{6,5},{9,10},{10,9},{11,12},{12,11},... | collective-permute-start | bytes 98312 | tf_op jit(solution)/shard_map/ppermute | solution.py:599
  34.5 0.0 collective-permute-done.5.a_ref
  34.5 3.4 %collective-permute-done.6.b_ref = bf16[128,128]{1,0:T(8,128)(2,1)S(1)} collective-permute-done((bf16[128,128]{1,0:T(8,128)(2,1)S(1)}, bf16[128,128]{1,0:T(8,128)(2,1)S(1)}, u32[]{:S(2)}, u32[]{:S(2)}) %collective-permute-start.6) | collective-permute-done | bytes 32800 | tf_op jit(solution)/shard_map/ppermute | solution.py:599
  37.9 0.4 next_columns.1
  38.3 0.1 collective-permute-start.7
  38.4 6.0 %collective-permute-start.8 = (bf16[96,128]{1,0:T(8,128)(2,1)S(1)}, bf16[96,128]{1,0:T(8,128)(2,1)S(1)}, u32[]{:S(2)}, u32[]{:S(2)}) collective-permute-start(bf16[96,128]{1,0:T(8,128)(2,1)S(1)} %get-tuple-element.47), channel_id=1, source_target_pairs={{8,16},{16,8},{24,32},{32,24},{40,48},{48,40},{56,64},{64,56},{72,... | collective-permute-start | bytes 73736 | tf_op jit(solution)/shard_map/ppermute | solution.py:599
  44.3 0.0 copy-start.2
  44.4 3.0 %next_interior.1.inner_ref = f32[12,64,128]{2,1,0:T(8,128)S(1)} custom-call(f32[12,96,128]{2,1,0:T(8,128)S(1)} %get-tuple-element.50.tall_ref, f32[6,112,128]{2,1,0:T(8,128)S(1)} %get-tuple-element.51.keep_ref, f32[6,112,128]{2,1,0:T(8,128)S(1)} %get-tuple-element.52.give_ref), custom_call_target="tpu_custom_call" | custom-call | flops 10000000 | bytes 1000000 | tf_op jit(solution)/shard_map/next_interior/pallas_call | solution.py:571
  47.3 0.0 collective-permute-done.7.first_ref
  47.3 0.0 collective-permute-done.8.second_ref
  47.3 0.0 copy-done.2
  47.3 2.6 %gradient.1 = f32[2,6,64,128]{3,2,1,0:T(8,128)} custom-call(bf16[96,128]{1,0:T(8,128)(2,1)S(1)} %collective-permute-done.7.first_ref, bf16[96,128]{1,0:T(8,128)(2,1)S(1)} %collective-permute-done.8.second_ref, f32[3,96,128]{2,1,0:T(8,128)S(1)} %get-tuple-element.48.west_ref, f32[3,96,128]{2,1,0:T(8,128)S(1)} %get-tuple-element.49.east_ref, ...), custom_call_target="tpu_custom_call" | custom-call | tf_op jit(solution)/shard_map/gradient/pallas_call | solution.py:571
Async XLA Ops:
  0.0 1.0 %copy-start = (f32[4,3,64,128]{3,2,1,0:T(8,128)S(1)}, f32[4,3,64,128]{3,2,1,0:T(8,128)}, u32[]{:S(2)}) copy-start(f32[4,3,64,128]{3,2,1,0:T(8,128)} %model_ref.7) | copy-start | bytes 1179652
  1.0 1.0 %copy-start.1 = (f32[2,6,64,128]{3,2,1,0:T(8,128)S(1)}, f32[2,6,64,128]{3,2,1,0:T(8,128)}, u32[]{:S(2)}) copy-start(f32[2,6,64,128]{3,2,1,0:T(8,128)} %control_ref.5) | copy-start | bytes 1179652
  2.0 0.8 %copy-start.4 = (s32[64,128]{1,0:T(8,128)S(1)}, s32[64,128]{1,0:T(8,128)}, u32[]{:S(2)}) copy-start(s32[64,128]{1,0:T(8,128)} %bottom_ref.5) | copy-start | bytes 98308
  2.9 4.9 %collective-permute-start = (bf16[160,128]{1,0:T(8,128)(2,1)S(1)}, bf16[160,128]{1,0:T(8,128)(2,1)S(1)}, u32[]{:S(2)}, u32[]{:S(2)}) collective-permute-start(bf16[160,128]{1,0:T(8,128)(2,1)S(1)} %get-tuple-element.30), channel_id=1, source_target_pairs={{0,1},{1,0},{2,3},{3,2},{4,5},{5,4},{6,7},{7,6},{8,9},{9,8},{10,11... | collective-permute-start | bytes 122888 | tf_op jit(solution)/shard_map/ppermute | solution.py:599
  3.5 6.8 %collective-permute-start.1 = (bf16[160,128]{1,0:T(8,128)(2,1)S(1)}, bf16[160,128]{1,0:T(8,128)(2,1)S(1)}, u32[]{:S(2)}, u32[]{:S(2)}) collective-permute-start(bf16[160,128]{1,0:T(8,128)(2,1)S(1)} %get-tuple-element.31), channel_id=1, source_target_pairs={{1,2},{2,1},{3,4},{4,3},{5,6},{6,5},{9,10},{10,9},{11,12},{12,11},... | collective-permute-start | bytes 122888 | tf_op jit(solution)/shard_map/ppermute | solution.py:599
  10.9 12.3 %collective-permute-start.2 = (bf16[96,256]{1,0:T(8,128)(2,1)S(1)}, bf16[96,256]{1,0:T(8,128)(2,1)S(1)}, u32[]{:S(2)}, u32[]{:S(2)}) collective-permute-start(bf16[96,256]{1,0:T(8,128)(2,1)S(1)} %get-tuple-element.32), channel_id=1, source_target_pairs={{0,8},{8,0},{16,24},{24,16},{32,40},{40,32},{48,56},{56,48},{64,72... | collective-permute-start | bytes 147464 | tf_op jit(solution)/shard_map/ppermute | solution.py:599
  13.6 9.6 %collective-permute-start.3 = (bf16[96,256]{1,0:T(8,128)(2,1)S(1)}, bf16[96,256]{1,0:T(8,128)(2,1)S(1)}, u32[]{:S(2)}, u32[]{:S(2)}) collective-permute-start(bf16[96,256]{1,0:T(8,128)(2,1)S(1)} %get-tuple-element.33), channel_id=1, source_target_pairs={{8,16},{16,8},{24,32},{32,24},{40,48},{48,40},{56,64},{64,56},{72,... | collective-permute-start | bytes 147464 | tf_op jit(solution)/shard_map/ppermute | solution.py:599
  24.3 3.0 %collective-permute-start.4 = (f32[2,3,64,128]{3,2,1,0:T(8,128)S(1)}, f32[2,3,64,128]{3,2,1,0:T(8,128)S(1)}, u32[]{:S(2)}, u32[]{:S(2)}) collective-permute-start(f32[2,3,64,128]{3,2,1,0:T(8,128)S(1)} %get-tuple-element.42), channel_id=1, source_target_pairs={{0,128},{128,0},{1,129},{129,1},{2,130},{130,2},{3,131},{131,3},{4... | collective-permute-start | bytes 589832 | tf_op jit(solution)/shard_map/ppermute | solution.py:661
  25.0 2.3 %copy-start.3 = (f32[2,6,64,128]{3,2,1,0:T(8,128)S(1)}, f32[2,6,64,128]{3,2,1,0:T(8,128)}, u32[]{:S(2)}) copy-start(f32[2,6,64,128]{3,2,1,0:T(8,128)} %error_ref.1) | copy-start | bytes 1179652
  25.0 2.3 %copy-start.5 = (s32[64,128]{1,0:T(8,128)S(1)}, s32[64,128]{1,0:T(8,128)}, u32[]{:S(2)}) copy-start(s32[64,128]{1,0:T(8,128)} %bottom_ref.5) | copy-start | bytes 98308
  25.0 2.3 %copy-start.6 = (f32[1,1,1,4,256]{4,3,2,1,0:T(4,128)S(1)}, f32[1,1,1,4,256]{4,3,2,1,0:T(4,128)}, u32[]{:S(2)}) copy-start(f32[1,1,1,4,256]{4,3,2,1,0:T(4,128)} %weight_ref.1) | copy-start | bytes 12292
  25.0 2.3 %copy-start.8 = (f32[1,1,1,256]{3,2,1,0:T(1,128)S(1)}, f32[1,1,1,256]{3,2,1,0:T(1,128)}, u32[]{:S(2)}) copy-start(f32[1,1,1,256]{3,2,1,0:T(1,128)} %value_ref.1) | copy-start | bytes 3076
  25.1 2.3 %copy-start.9 = (f32[1,1,1,256]{3,2,1,0:T(1,128)S(1)}, f32[1,1,1,256]{3,2,1,0:T(1,128)}, u32[]{:S(2)}) copy-start(f32[1,1,1,256]{3,2,1,0:T(1,128)} %precision_ref.1) | copy-start | bytes 3076
  27.3 0.7 %copy-start.7 = (s32[1,1,1,256]{3,2,1,0:T(1,128)S(1)}, s32[1,1,1,256]{3,2,1,0:T(1,128)}, u32[]{:S(2)}) copy-start(s32[1,1,1,256]{3,2,1,0:T(1,128)} %corner_ref.1) | copy-start | bytes 3076
  29.5 4.9 %collective-permute-start.5 = (bf16[128,128]{1,0:T(8,128)(2,1)S(1)}, bf16[128,128]{1,0:T(8,128)(2,1)S(1)}, u32[]{:S(2)}, u32[]{:S(2)}) collective-permute-start(bf16[128,128]{1,0:T(8,128)(2,1)S(1)} %get-tuple-element.44), channel_id=1, source_target_pairs={{0,1},{1,0},{2,3},{3,2},{4,5},{5,4},{6,7},{7,6},{8,9},{9,8},{10,11... | collective-permute-start | bytes 98312 | tf_op jit(solution)/shard_map/ppermute | solution.py:599
  31.2 6.7 %collective-permute-start.6 = (bf16[128,128]{1,0:T(8,128)(2,1)S(1)}, bf16[128,128]{1,0:T(8,128)(2,1)S(1)}, u32[]{:S(2)}, u32[]{:S(2)}) collective-permute-start(bf16[128,128]{1,0:T(8,128)(2,1)S(1)} %get-tuple-element.45), channel_id=1, source_target_pairs={{1,2},{2,1},{3,4},{4,3},{5,6},{6,5},{9,10},{10,9},{11,12},{12,11},... | collective-permute-start | bytes 98312 | tf_op jit(solution)/shard_map/ppermute | solution.py:599
  38.3 9.0 %collective-permute-start.7 = (bf16[96,128]{1,0:T(8,128)(2,1)S(1)}, bf16[96,128]{1,0:T(8,128)(2,1)S(1)}, u32[]{:S(2)}, u32[]{:S(2)}) collective-permute-start(bf16[96,128]{1,0:T(8,128)(2,1)S(1)} %get-tuple-element.46), channel_id=1, source_target_pairs={{0,8},{8,0},{16,24},{24,16},{32,40},{40,32},{48,56},{56,48},{64,72... | collective-permute-start | bytes 73736 | tf_op jit(solution)/shard_map/ppermute | solution.py:599
  38.4 8.9 %collective-permute-start.8 = (bf16[96,128]{1,0:T(8,128)(2,1)S(1)}, bf16[96,128]{1,0:T(8,128)(2,1)S(1)}, u32[]{:S(2)}, u32[]{:S(2)}) collective-permute-start(bf16[96,128]{1,0:T(8,128)(2,1)S(1)} %get-tuple-element.47), channel_id=1, source_target_pairs={{8,16},{16,8},{24,32},{32,24},{40,48},{48,40},{56,64},{64,56},{72,... | collective-permute-start | bytes 73736 | tf_op jit(solution)/shard_map/ppermute | solution.py:599
  44.3 3.0 %copy-start.2 = (f32[2,6,64,128]{3,2,1,0:T(8,128)S(1)}, f32[2,6,64,128]{3,2,1,0:T(8,128)}, u32[]{:S(2)}) copy-start(f32[2,6,64,128]{3,2,1,0:T(8,128)} %control_ref.5) | copy-start | bytes 1179652

commit v3 on v2

--- a/solution.py
+++ b/solution.py
@@ -34,6 +34,7 @@
 TRAVEL = jnp.bfloat16
 F32 = jnp.float32
 VMEM = pltpu.VMEM
+GRANT, GRANT_MORE, GRANT_MOST = 24, 40, 53.7
 
 
 def lanes(rows):
@@ -51,6 +52,12 @@
 def roll(value, shift):
     shift %= COLS
     return value if shift == 0 else pltpu.roll(value, shift, 1)
+
+
+def mer_sides(first, second):
+    low, high = sides(first, second, even_on("mer"))
+    index = lax.axis_index("mer")
+    return jnp.where(index == 0, 0.0, low), jnp.where(index == lax.axis_size("mer") - 1, 0.0, high)
 
 
 def even_on(axis):
@@ -138,8 +145,31 @@
     return jnp.concatenate([blank, low, value, high, blank], axis=0)
 
 
+def stand_core(value):
+    blank = jnp.zeros((EDGE, COLS), F32)
+    return jnp.concatenate([blank, value, blank], axis=0)
+
+
+def model_columns(model_ref, east_ref, west_ref):
+    lane = lanes(ROWS)
+    to_east = to_west = jnp.zeros((ROWS, COLS), F32)
+    for q in range(STEPPED):
+        value = model_ref[q // HALF, q % HALF]
+        at = MODEL_LANE + 2 * q
+        column = value[:, COLS - 1 :]
+        coarse = column.astype(TRAVEL).astype(F32)
+        to_east = jnp.where(lane == at, coarse, to_east)
+        to_east = jnp.where(lane == at + 1, column - coarse, to_east)
+        column = value[:, :1]
+        coarse = column.astype(TRAVEL).astype(F32)
+        to_west = jnp.where(lane == at - 1, coarse, to_west)
+        to_west = jnp.where(lane == at - 2, column - coarse, to_west)
+    east_ref[...] = to_east
+    west_ref[...] = to_west
+
+
 def raise_planes(read, first_ref, second_ref, low_ref, high_ref, tall_ref):
-    low, high = sides(first_ref[...], second_ref[...], even_on("mer"))
+    low, high = mer_sides(first_ref[...], second_ref[...])
     low_ref[...] = low
     high_ref[...] = high
     blank = jnp.zeros((EDGE - HALO, COLS), F32)
@@ -181,9 +211,10 @@
 
 
 def first_columns_kernel(
-    model_ref,
     control_ref,
     bottom_ref,
+    model_east_ref,
+    model_west_ref,
     a_ref,
     b_ref,
     tall_ref,
@@ -205,26 +236,11 @@
         high_ref[DEPTH_ROW:MODEL_ROW, :],
     )
     depth_ref[...] = depth
-    tall_lane = lanes(TALL)
-    lane = lanes(ROWS)
-    to_east = to_west = jnp.zeros((ROWS, COLS), F32)
-    for q in range(STEPPED):
-        value = model_ref[q // HALF, q % HALF]
-        at = MODEL_LANE + 2 * q
-        column = value[:, COLS - 1 :]
-        coarse = column.astype(TRAVEL).astype(F32)
-        to_east = jnp.where(lane == at, coarse, to_east)
-        to_east = jnp.where(lane == at + 1, column - coarse, to_east)
-        column = value[:, :1]
-        coarse = column.astype(TRAVEL).astype(F32)
-        to_west = jnp.where(lane == at - 1, coarse, to_west)
-        to_west = jnp.where(lane == at - 2, column - coarse, to_west)
-    blank = jnp.zeros((EDGE, COLS), F32)
-    mark = tall_lane < HALO
+    mark = lanes(TALL) < HALO
     send_columns(
         1,
-        jnp.where(mark, roll(depth, HALO), jnp.concatenate([blank, to_east, blank], axis=0)),
-        jnp.where(mark, depth, jnp.concatenate([blank, to_west, blank], axis=0)),
+        jnp.where(mark, roll(depth, HALO), stand_core(model_east_ref[...])),
+        jnp.where(mark, depth, stand_core(model_west_ref[...])),
         first_ref,
         second_ref,
     )
@@ -240,7 +256,7 @@
 def base_step(model_ref, depth_ref, a_ref, b_ref, base_ref, low_ref, high_ref, tall_ref):
     lane = lanes(ROWS)
     group = lax.axis_index("grp")
-    low, high = sides(a_ref[...], b_ref[...], even_on("mer"))
+    low, high = mer_sides(a_ref[...], b_ref[...])
     low_ref[...] = low
     high_ref[...] = high
     core = slice(EDGE, EDGE + ROWS)
@@ -292,18 +308,14 @@
         wet = depth > (group * HALF + level).astype(F32)
         gain = jnp.where(wet, MIXING + sign * model_ref[2, level], 0.0)
         loss = jnp.where(wet, MIXING, 0.0)
-        for field in range(FIELDS):
-            halo = roll(columns, -(MODEL_LANE + 2 * (field * HALF + level)))
-            result = base_ref[field, level] + (gain * halo - loss * model_ref[field, level])
-            own = group == field // 2
-
-            @pl.when(own)
-            def _():
-                keep_ref[field % 2, level] = result
-
-            @pl.when(jnp.logical_not(own))
-            def _():
-                send_ref[field % 2, level] = result
+        for out_ref, pair in ((keep_ref, group), (send_ref, 1 - group)):
+            for f in range(PAIR):
+                field = PAIR * pair + f
+                at = MODEL_LANE + 2 * (field * HALF + level)
+                halo = pltpu.roll(columns, COLS - at, 1)
+                out_ref[f, level] = base_ref[field, level] + (
+                    gain * halo - loss * model_ref[field, level]
+                )
 
 
 def neighbour_sum(ref, index, start, rows):
@@ -492,17 +504,57 @@
     return value[:, :COLS] + value[:, COLS:]
 
 
+def prepare_kernel(*refs):
+    here_refs, out_refs, (*held_refs, sems) = refs[:8], refs[8:16], refs[16:]
+    copies = [
+        pltpu.make_async_copy(source, target, sems.at[i])
+        for i, (source, target) in enumerate(zip(here_refs, held_refs))
+    ]
+    for copy in copies:
+        copy.start()
+    for copy in copies:
+        copy.wait()
+    count_ref, model_ref, error_ref, bottom_ref = held_refs[:4]
+    corner_ref, weight_ref, value_ref, precision_ref = held_refs[4:]
+    east_ref, west_ref, scale_ref, pick_ref, back_ref, lower_ref, upper_ref, want_ref = out_refs
+    model_columns(model_ref, east_ref, west_ref)
+    depth = bottom_ref[...]
+    for plane in range(PLANES):
+        f, k = divmod(plane, LEVELS)
+        scale_ref[plane] = jnp.where(depth > k, error_ref[f, k], 0.0)
+    slots = corner_ref.shape[-1]
+    cells = PLANES * ROWS
+    corner = corner_ref[0, 0]
+    row = (corner >> 7).astype(F32)
+    column = (corner & (COLS - 1)).astype(F32)
+    stacked = jnp.concatenate(
+        [weight_ref[0, 0, 0], value_ref[0, 0], precision_ref[0, 0], row, column], axis=0
+    )
+    tall = jnp.transpose(stacked)
+    wide_row = lax.broadcasted_iota(jnp.int32, (slots, cells), 1).astype(F32)
+    tall_row = lax.broadcasted_iota(jnp.int32, (cells, slots), 0).astype(F32)
+    for step in range(2):
+        here = slice(step * slots, (step + 1) * slots)
+        pick_ref[here, :] = jnp.where(wide_row == tall[:, 6:7] + step, 1.0, 0.0).astype(jnp.bfloat16)
+        back_ref[:, here] = jnp.where(tall_row == row + step, 1.0, 0.0).astype(jnp.bfloat16)
+    lane = lanes(slots).astype(F32)
+    at, beside = lane == tall[:, 7:8], lane == tall[:, 7:8] + 1.0
+    lower_ref[...] = jnp.where(at, tall[:, 0:1], jnp.where(beside, tall[:, 1:2], 0.0))
+    upper_ref[...] = jnp.where(at, tall[:, 2:3], jnp.where(beside, tall[:, 3:4], 0.0))
+    live = lax.broadcasted_iota(jnp.int32, (slots, 8), 0) < count_ref[0]
+    want_ref[...] = jnp.where(live, tall, 0.0)
+
+
 def observe_kernel(
-    count_ref,
     smooth_ref,
-    error_ref,
-    bottom_ref,
+    scale_ref,
     keep_ref,
     other_ref,
-    corner_ref,
-    weight_ref,
-    value_ref,
-    precision_ref,
+    pick_ref,
+    back_ref,
+    lower_ref,
+    upper_ref,
+    want_ref,
     field_ref,
     first_ref,
     second_ref,
@@ -511,47 +563,22 @@
     high_ref,
 ):
     group = lax.axis_index("grp")
-    slots = corner_ref.shape[-1]
-    depth = bottom_ref[...]
+    slots = want_ref.shape[0]
     for plane in range(PLANES):
         f, k = divmod(plane, LEVELS)
-        scale = jnp.where(depth > k, error_ref[f, k], 0.0)
         held = group == k // HALF
         prior = jnp.where(held, keep_ref[f, k % HALF], other_ref[f, k % HALF])
-        total_ref[plane * ROWS : (plane + 1) * ROWS, :] = scale * smooth_ref[plane] + prior
-    corner = corner_ref[0, 0]
-    row = (corner >> 7).astype(F32)
-    column = (corner & (COLS - 1)).astype(F32)
-    stacked = jnp.concatenate(
-        [weight_ref[0, 0, 0], value_ref[0, 0], precision_ref[0, 0], row, column], axis=0
-    )
-    tall = jnp.transpose(stacked)
-    row_tall = jnp.concatenate([tall[:, 6:7], tall[:, 6:7] + 1.0], axis=0)
-    cells = PLANES * ROWS
-    wide_row = lax.broadcasted_iota(jnp.int32, (2 * slots, cells), 1).astype(F32)
-    pick = jnp.where(wide_row == row_tall, 1.0, 0.0).astype(jnp.bfloat16)
-    seen = join(jnp.dot(pick, split(total_ref[...]), preferred_element_type=F32))
-    lane = lanes(slots).astype(F32)
-    at, beside = lane == tall[:, 7:8], lane == tall[:, 7:8] + 1.0
-    lower = jnp.where(at, tall[:, 0:1], jnp.where(beside, tall[:, 1:2], 0.0))
-    upper = jnp.where(at, tall[:, 2:3], jnp.where(beside, tall[:, 3:4], 0.0))
+        total_ref[plane * ROWS : (plane + 1) * ROWS, :] = (
+            scale_ref[plane] * smooth_ref[plane] + prior
+        )
+    seen = join(jnp.dot(pick_ref[...], split(total_ref[...]), preferred_element_type=F32))
+    lower, upper = lower_ref[...], upper_ref[...]
     observed = jnp.sum(lower * seen[:slots] + upper * seen[slots:], axis=1, keepdims=True)
-    live = lax.broadcasted_iota(jnp.int32, (slots, 1), 0) < count_ref[0, 0, 0]
-    misfit = jnp.where(live, tall[:, 5:6] * (observed - tall[:, 4:5]), 0.0)
+    misfit = want_ref[:, 5:6] * (observed - want_ref[:, 4:5])
     spread = jnp.concatenate([lower * misfit, upper * misfit], axis=0)
-    tall_row = lax.broadcasted_iota(jnp.int32, (cells, slots), 0).astype(F32)
-    back = jnp.concatenate(
-        [
-            jnp.where(tall_row == row, 1.0, 0.0).astype(jnp.bfloat16),
-            jnp.where(tall_row == row + 1.0, 1.0, 0.0).astype(jnp.bfloat16),
-        ],
-        axis=1,
-    )
-    total_ref[...] = join(jnp.dot(back, split(spread), preferred_element_type=F32))
-    for plane in range(PLANES):
-        f, k = divmod(plane, LEVELS)
-        scale = jnp.where(depth > k, error_ref[f, k], 0.0)
-        field_ref[plane] = scale * total_ref[plane * ROWS : (plane + 1) * ROWS, :]
+    total_ref[...] = join(jnp.dot(back_ref[...], split(spread), preferred_element_type=F32))
+    for plane in range(PLANES):
+        field_ref[plane] = scale_ref[plane] * total_ref[plane * ROWS : (plane + 1) * ROWS, :]
     stage(
         low_ref,
         high_ref,
@@ -564,20 +591,19 @@
     send_rows(low_ref, high_ref, first_ref, second_ref)
 
 
-def call(kernel, outs, scratch=(), scalars=0, remote=False, work=0):
-    space = pltpu.HBM if remote else VMEM
+def call(kernel, outs, scratch=(), remote=0, work=0):
+    space = pl.ANY if remote else VMEM
 
     def run(*args):
         return pl.pallas_call(
             kernel,
             out_shape=[jax.ShapeDtypeStruct(shape, kind) for shape, kind in outs],
-            in_specs=[
-                pl.BlockSpec(memory_space=pltpu.SMEM if i < scalars else space)
-                for i in range(len(args))
-            ],
+            in_specs=[pl.BlockSpec(memory_space=space) for _ in args],
             out_specs=[pl.BlockSpec(memory_space=VMEM) for _ in outs],
             scratch_shapes=list(scratch),
-            compiler_params=pltpu.CompilerParams(vmem_limit_bytes=24 * 2**20),
+            compiler_params=pltpu.CompilerParams(
+                vmem_limit_bytes=int((remote or GRANT) * 2**20)
+            ),
             cost_estimate=pl.CostEstimate(
                 flops=work, bytes_accessed=work // 10, transcendentals=0
             )
@@ -589,18 +615,17 @@
     return run
 
 
-def swap(value, axis, shift, wrap):
+def swap(value, axis, shift):
     size = lax.axis_size(axis)
     pairs = []
-    for i in range(shift, size + shift - 1, 2):
-        j = i + 1
-        if j < size or wrap:
-            pairs += [(i, j % size), (j % size, i)]
+    for i in range(shift, size, 2):
+        j = (i + 1) % size
+        pairs += [(i, j), (j, i)]
     return lax.ppermute(value, axis, pairs)
 
 
-def exchange(first, second, axis, wrap):
-    return swap(first, axis, 0, wrap), swap(second, axis, 1, wrap)
+def exchange(first, second, axis):
+    return swap(first, axis, 0), swap(second, axis, 1)
 
 
 FULL = ((PLANES, ROWS, COLS), F32)
@@ -640,15 +665,37 @@
         + [VMEM((FIELDS, HALF, 8, COLS), F32)] * 2
         + [VMEM((EDGE, COLS), jnp.int32)] * 2
         + [long, long, dma((6,))],
-        remote=True,
+        remote=GRANT_MOST,
     )(model_state, control, bottom_level)
-    mer = exchange(first, second, "mer", False)
+    mer = exchange(first, second, "mer")
+    slots = obs_corner.shape[-1]
+    inputs = (
+        obs_count,
+        model_state,
+        error_std,
+        bottom_level,
+        obs_corner,
+        obs_weight,
+        obs_value,
+        obs_precision,
+    )
+    model_east, model_west, scale, *operators = call(
+        prepare_kernel,
+        [((ROWS, COLS), F32)] * 2
+        + [FULL]
+        + [((2 * slots, PLANES * ROWS), jnp.bfloat16), ((PLANES * ROWS, 2 * slots), jnp.bfloat16)]
+        + [((slots, COLS), F32)] * 2
+        + [((slots, 8), F32)],
+        [VMEM(value.shape, value.dtype) for value in inputs] + [dma((len(inputs),))],
+        remote=GRANT_MORE,
+        work=10**7,
+    )(*inputs)
     tall, depth, west, east, first, second = call(
         first_columns_kernel,
         [RAISED, ((TALL, COLS), F32), SIDE, SIDE, columns_of(2), columns_of(2)],
         [long, long],
-    )(model_state, control, bottom_level, *mer)
-    zon = exchange(first, second, "zon", True)
+    )(control, bottom_level, model_east, model_west, *mer)
+    zon = exchange(first, second, "zon")
     inner, keep_coef, give_coef, base = call(
         first_interior_kernel,
         [FULL, MASKS, MASKS, STEP],
@@ -666,24 +713,12 @@
         observe_kernel,
         [FULL, rows_of(SHORT), rows_of(SHORT)],
         [VMEM((PLANES * ROWS, COLS), F32), short, short],
-        scalars=1,
-    )(
-        obs_count,
-        smoothed,
-        error_std,
-        bottom_level,
-        keep,
-        other,
-        obs_corner,
-        obs_weight,
-        obs_value,
-        obs_precision,
-    )
-    mer = exchange(first, second, "mer", False)
+    )(smoothed, scale, keep, other, *operators)
+    mer = exchange(first, second, "mer")
     tall, west, east, first, second = call(
         next_columns_kernel, [RAISED, SIDE, SIDE, columns_of(1), columns_of(1)], [short, short]
     )(field, *mer)
-    zon = exchange(first, second, "zon", True)
+    zon = exchange(first, second, "zon")
     (inner,) = call(
         next_interior_kernel, [FULL], [VMEM((PLANES, DEEP, COLS), F32)] * 2, work=10**7
     )(tall, keep_coef, give_coef)

time: 50.2 us -> 44.6 us (0.89)
  the two profiles are of different devices: /device:TPU:10 before, /device:TPU:1 now
where the time goes in v3:
time: 44.6 us; the launch traced here: 44.5 us
  starting transfers between devices  23.7 us (53%)
  Pallas kernels  16.2 us (36%)
  waiting for transfers between devices  2.89 us (6%)
  between operations  0.85 us (2%)
  local copies, waits for them, and re-layouts  0.84 us (2%)
    ppermute x8, starting transfers between devices, swap(): return lax.ppermute(value, axis, pairs)  20.9 us
    pallas_call x10, Pallas kernels, run(): pl.pallas_call(kernel, out_shape=[jax.ShapeDtypeStruct(shape, kind) for s...  16.2 us
    ppermute x8, waiting for transfers between devices, swap(): return lax.ppermute(value, axis, pairs)  2.88 us
    ppermute x1, starting transfers between devices, body(): other = lax.ppermute(send, 'grp', [(0, 1), (1, 0)])  2.75 us
  transfers between devices with their start and end apart: 9, of which 3 were waited for; matrix products, arithmetic and copies ran while one was open for 0% of the time, Pallas kernels for 23%

profile of v3, /device:TPU:1, one launch (start us, length us, event | category | flops | bytes accessed | tf_op | source)
XLA Modules:
  0.0 44.5 jit_solution(956659620646811304)
XLA Ops:
  0.0 0.0 copy-start
  0.0 0.0 copy-start.3
  0.0 0.8 %copy-done.3 = s32[64,128]{1,0:T(8,128)S(1)} copy-done((s32[64,128]{1,0:T(8,128)S(1)}, s32[64,128]{1,0:T(8,128)}, u32[]{:S(2)}) %copy-start.3) | copy-done | bytes 32792
  0.8 0.0 copy-start.2
  0.8 0.0 copy-start.6
  0.8 0.0 copy-start.7
  0.8 1.1 %start.1 = (bf16[160,128]{1,0:T(8,128)(2,1)S(1)}, bf16[160,128]{1,0:T(8,128)(2,1)S(1)}) custom-call(f32[4,3,64,128]{3,2,1,0:T(8,128)} %model_ref.5, f32[2,6,64,128]{3,2,1,0:T(8,128)} %control_ref.5, s32[64,128]{1,0:T(8,128)S(1)} %copy-done.3), custom_call_target="tpu_custom_call" | custom-call | tf_op jit(solution)/shard_map/start/pallas_call | solution.py:598
  1.9 0.0 copy-start.4
  1.9 2.2 %collective-permute-start = (bf16[160,128]{1,0:T(8,128)(2,1)S(1)}, bf16[160,128]{1,0:T(8,128)(2,1)S(1)}, u32[]{:S(2)}, u32[]{:S(2)}) collective-permute-start(bf16[160,128]{1,0:T(8,128)(2,1)S(1)} %get-tuple-element.40), channel_id=1, source_target_pairs={{0,1},{1,0},{2,3},{3,2},{4,5},{5,4},{6,7},{7,6},{8,9},{9,8},{10,11... | collective-permute-start | bytes 122888 | tf_op jit(solution)/shard_map/ppermute | solution.py:624
  4.1 0.0 copy-start.5
  4.1 2.4 %collective-permute-start.1 = (bf16[160,128]{1,0:T(8,128)(2,1)S(1)}, bf16[160,128]{1,0:T(8,128)(2,1)S(1)}, u32[]{:S(2)}, u32[]{:S(2)}) collective-permute-start(bf16[160,128]{1,0:T(8,128)(2,1)S(1)} %get-tuple-element.41), channel_id=1, source_target_pairs={{1,2},{2,1},{3,4},{4,3},{5,6},{6,5},{7,0},{0,7},{9,10},{10,9},{11,... | collective-permute-start | bytes 122888 | tf_op jit(solution)/shard_map/ppermute | solution.py:624
  7.2 0.0 copy-done
  7.2 0.0 copy-done.2
  7.2 0.0 copy-done.6
  7.2 0.0 copy-done.7
  7.2 0.0 copy-done.4
  7.2 0.0 copy-done.5
  7.2 0.0 copy-start.1
  7.2 1.5 %prepare.1 = (f32[64,128]{1,0:T(8,128)S(1)}, f32[64,128]{1,0:T(8,128)S(1)}, f32[12,64,128]{2,1,0:T(8,128)S(1)}, bf16[512,768]{1,0:T(8,128)(2,1)S(1)}, bf16[768,5...) custom-call(s32[1,1,1]{2,1,0:T(1,128)S(6)} %copy.10.refs_0_, ...), custom_call_target="tpu_custom_call" | custom-call | flops 10000000 | bytes 1000000 | tf_op jit(solution)/shard_map/prepare/pallas_call | solution.py:598
  8.7 0.0 collective-permute-done.a_ref
  8.7 0.4 collective-permute-done.1.b_ref
  9.1 0.0 copy-done.1
  9.1 0.4 first_columns.1
  9.5 2.7 %collective-permute-start.2 = (bf16[96,256]{1,0:T(8,128)(2,1)S(1)}, bf16[96,256]{1,0:T(8,128)(2,1)S(1)}, u32[]{:S(2)}, u32[]{:S(2)}) collective-permute-start(bf16[96,256]{1,0:T(8,128)(2,1)S(1)} %get-tuple-element.42), channel_id=1, source_target_pairs={{0,8},{8,0},{16,24},{24,16},{32,40},{40,32},{48,56},{56,48},{64,72... | collective-permute-start | bytes 147464 | tf_op jit(solution)/shard_map/ppermute | solution.py:624
  12.2 5.6 %collective-permute-start.3 = (bf16[96,256]{1,0:T(8,128)(2,1)S(1)}, bf16[96,256]{1,0:T(8,128)(2,1)S(1)}, u32[]{:S(2)}, u32[]{:S(2)}) collective-permute-start(bf16[96,256]{1,0:T(8,128)(2,1)S(1)} %get-tuple-element.43), channel_id=1, source_target_pairs={{8,16},{16,8},{24,32},{32,24},{40,48},{48,40},{56,64},{64,56},{72,... | collective-permute-start | bytes 147464 | tf_op jit(solution)/shard_map/ppermute | solution.py:624
  17.9 3.4 %first_interior.1 = (f32[12,64,128]{2,1,0:T(8,128)S(1)}, f32[6,112,128]{2,1,0:T(8,128)S(1)}, f32[6,112,128]{2,1,0:T(8,128)S(1)}, f32[4,3,64,128]{3,2,1,0:T(8,128)S(1)}) custom-call(f32[12,96,128]{2,1,0:T(8,128)S(1)} %get-tuple-element.47.tall_ref, f32[96,128]{1,0:T(8,128)S(1)} %get-tuple-element.46.depth_ref, f32[4,3,64,128]{3,2,1,0:T(8,128)S(1)} %copy-done, ...), custom_call_target="tpu_custom_call" | custom-call | flops 10000000 | bytes 1000000 | tf_op jit(solution)/shard_map/first_interior/pallas_call | solution.py:598
  21.3 0.0 collective-permute-done.2.first_ref
  21.3 0.0 collective-permute-done.3.second_ref
  21.3 0.3 background.1
  21.6 2.8 %collective-permute-start.4 = (f32[2,3,64,128]{3,2,1,0:T(8,128)S(1)}, f32[2,3,64,128]{3,2,1,0:T(8,128)S(1)}, u32[]{:S(2)}, u32[]{:S(2)}) collective-permute-start(f32[2,3,64,128]{3,2,1,0:T(8,128)S(1)} %get-tuple-element.53), channel_id=1, source_target_pairs={{0,128},{128,0},{1,129},{129,1},{2,130},{130,2},{3,131},{131,3},{4... | collective-permute-start | bytes 589832 | tf_op jit(solution)/shard_map/ppermute | solution.py:708
  24.3 2.2 %first_bands.1 = (f32[12,64,128]{2,1,0:T(8,128)S(1)}, f32[6,112,128]{2,1,0:T(8,128)S(1)}, f32[6,112,128]{2,1,0:T(8,128)S(1)}) custom-call(bf16[96,256]{1,0:T(8,128)(2,1)S(1)} %collective-permute-done.2.first_ref, bf16[96,256]{1,0:T(8,128)(2,1)S(1)} %collective-permute-done.3.second_ref, f32[3,96,128]{2,1,0:T(8,128)S(1)} %get-tuple-element.44.west_ref, ...), custom_call_target="tpu_custom_call" | custom-call | flops 10000000 | bytes 1000000 | tf_op jit(solution)/shard_map/first_bands/pallas_call | solution.py:598
  26.5 0.0 collective-permute-done.4.other_ref
  26.5 1.4 %observe.1 = (f32[12,64,128]{2,1,0:T(8,128)S(1)}, bf16[128,128]{1,0:T(8,128)(2,1)S(1)}, bf16[128,128]{1,0:T(8,128)(2,1)S(1)}) custom-call(f32[12,64,128]{2,1,0:T(8,128)S(1)} %get-tuple-element.49.smooth_ref, f32[12,64,128]{2,1,0:T(8,128)S(1)} %get-tuple-element.50.scale_ref, f32[2,3,64,128]{3,2,1,0:T(8,128)S(1)} %get-tuple-element.52.keep_ref, ...), custom_call_target="tpu_custom_call" | custom-call | tf_op jit(solution)/shard_map/observe/pallas_call | solution.py:598
  27.9 0.1 collective-permute-start.5
  28.0 2.5 %collective-permute-start.6 = (bf16[128,128]{1,0:T(8,128)(2,1)S(1)}, bf16[128,128]{1,0:T(8,128)(2,1)S(1)}, u32[]{:S(2)}, u32[]{:S(2)}) collective-permute-start(bf16[128,128]{1,0:T(8,128)(2,1)S(1)} %get-tuple-element.61), channel_id=1, source_target_pairs={{1,2},{2,1},{3,4},{4,3},{5,6},{6,5},{7,0},{0,7},{9,10},{10,9},{11,... | collective-permute-start | bytes 98312 | tf_op jit(solution)/shard_map/ppermute | solution.py:624
  30.5 0.3 collective-permute-done.5.a_ref
  30.8 2.2 %collective-permute-done.6.b_ref = bf16[128,128]{1,0:T(8,128)(2,1)S(1)} collective-permute-done((bf16[128,128]{1,0:T(8,128)(2,1)S(1)}, bf16[128,128]{1,0:T(8,128)(2,1)S(1)}, u32[]{:S(2)}, u32[]{:S(2)}) %collective-permute-start.6) | collective-permute-done | bytes 32800 | tf_op jit(solution)/shard_map/ppermute | solution.py:624
  33.0 0.4 next_columns.1
  33.4 0.1 collective-permute-start.7
  33.5 5.4 %collective-permute-start.8 = (bf16[96,128]{1,0:T(8,128)(2,1)S(1)}, bf16[96,128]{1,0:T(8,128)(2,1)S(1)}, u32[]{:S(2)}, u32[]{:S(2)}) collective-permute-start(bf16[96,128]{1,0:T(8,128)(2,1)S(1)} %get-tuple-element.63), channel_id=1, source_target_pairs={{8,16},{16,8},{24,32},{32,24},{40,48},{48,40},{56,64},{64,56},{72,... | collective-permute-start | bytes 73736 | tf_op jit(solution)/shard_map/ppermute | solution.py:624
  38.9 3.0 %next_interior.1.inner_ref = f32[12,64,128]{2,1,0:T(8,128)S(1)} custom-call(f32[12,96,128]{2,1,0:T(8,128)S(1)} %get-tuple-element.66.tall_ref, f32[6,112,128]{2,1,0:T(8,128)S(1)} %get-tuple-element.67.keep_ref, f32[6,112,128]{2,1,0:T(8,128)S(1)} %get-tuple-element.68.give_ref), custom_call_target="tpu_custom_call" | custom-call | flops 10000000 | bytes 1000000 | tf_op jit(solution)/shard_map/next_interior/pallas_call | solution.py:598
  41.8 0.0 collective-permute-done.7.first_ref
  41.8 0.0 collective-permute-done.8.second_ref
  41.8 2.6 %gradient.1 = f32[2,6,64,128]{3,2,1,0:T(8,128)} custom-call(bf16[96,128]{1,0:T(8,128)(2,1)S(1)} %collective-permute-done.7.first_ref, bf16[96,128]{1,0:T(8,128)(2,1)S(1)} %collective-permute-done.8.second_ref, f32[3,96,128]{2,1,0:T(8,128)S(1)} %get-tuple-element.64.west_ref, f32[3,96,128]{2,1,0:T(8,128)S(1)} %get-tuple-element.65.east_ref, ...), custom_call_target="tpu_custom_call" | custom-call | tf_op jit(solution)/shard_map/gradient/pallas_call | solution.py:598
Async XLA Ops:
  0.0 7.2 %copy-start = (f32[4,3,64,128]{3,2,1,0:T(8,128)S(1)}, f32[4,3,64,128]{3,2,1,0:T(8,128)}, u32[]{:S(2)}) copy-start(f32[4,3,64,128]{3,2,1,0:T(8,128)} %model_ref.5) | copy-start | bytes 1179652
  0.0 0.8 %copy-start.3 = (s32[64,128]{1,0:T(8,128)S(1)}, s32[64,128]{1,0:T(8,128)}, u32[]{:S(2)}) copy-start(s32[64,128]{1,0:T(8,128)} %bottom_ref.3) | copy-start | bytes 98308
  0.8 6.4 %copy-start.2 = (f32[2,6,64,128]{3,2,1,0:T(8,128)S(1)}, f32[2,6,64,128]{3,2,1,0:T(8,128)}, u32[]{:S(2)}) copy-start(f32[2,6,64,128]{3,2,1,0:T(8,128)} %refs_2_.1) | copy-start | bytes 1179652
  0.8 6.4 %copy-start.6 = (f32[1,1,1,256]{3,2,1,0:T(1,128)S(1)}, f32[1,1,1,256]{3,2,1,0:T(1,128)}, u32[]{:S(2)}) copy-start(f32[1,1,1,256]{3,2,1,0:T(1,128)} %refs_6_.1) | copy-start | bytes 3076
  0.8 6.4 %copy-start.7 = (f32[1,1,1,256]{3,2,1,0:T(1,128)S(1)}, f32[1,1,1,256]{3,2,1,0:T(1,128)}, u32[]{:S(2)}) copy-start(f32[1,1,1,256]{3,2,1,0:T(1,128)} %refs_7_.1) | copy-start | bytes 3076
  1.9 5.3 %copy-start.4 = (f32[1,1,1,4,256]{4,3,2,1,0:T(4,128)S(1)}, f32[1,1,1,4,256]{4,3,2,1,0:T(4,128)}, u32[]{:S(2)}) copy-start(f32[1,1,1,4,256]{4,3,2,1,0:T(4,128)} %refs_5_.1) | copy-start | bytes 12292
  1.9 6.8 %collective-permute-start = (bf16[160,128]{1,0:T(8,128)(2,1)S(1)}, bf16[160,128]{1,0:T(8,128)(2,1)S(1)}, u32[]{:S(2)}, u32[]{:S(2)}) collective-permute-start(bf16[160,128]{1,0:T(8,128)(2,1)S(1)} %get-tuple-element.40), channel_id=1, source_target_pairs={{0,1},{1,0},{2,3},{3,2},{4,5},{5,4},{6,7},{7,6},{8,9},{9,8},{10,11... | collective-permute-start | bytes 122888 | tf_op jit(solution)/shard_map/ppermute | solution.py:624
  4.1 3.1 %copy-start.5 = (s32[1,1,1,256]{3,2,1,0:T(1,128)S(1)}, s32[1,1,1,256]{3,2,1,0:T(1,128)}, u32[]{:S(2)}) copy-start(s32[1,1,1,256]{3,2,1,0:T(1,128)} %refs_4_.1) | copy-start | bytes 3076
  4.1 5.0 %collective-permute-start.1 = (bf16[160,128]{1,0:T(8,128)(2,1)S(1)}, bf16[160,128]{1,0:T(8,128)(2,1)S(1)}, u32[]{:S(2)}, u32[]{:S(2)}) collective-permute-start(bf16[160,128]{1,0:T(8,128)(2,1)S(1)} %get-tuple-element.41), channel_id=1, source_target_pairs={{1,2},{2,1},{3,4},{4,3},{5,6},{6,5},{7,0},{0,7},{9,10},{10,9},{11,... | collective-permute-start | bytes 122888 | tf_op jit(solution)/shard_map/ppermute | solution.py:624
  7.2 1.9 %copy-start.1 = (f32[2,6,64,128]{3,2,1,0:T(8,128)S(1)}, f32[2,6,64,128]{3,2,1,0:T(8,128)}, u32[]{:S(2)}) copy-start(f32[2,6,64,128]{3,2,1,0:T(8,128)} %control_ref.5) | copy-start | bytes 1179652
  9.5 11.8 %collective-permute-start.2 = (bf16[96,256]{1,0:T(8,128)(2,1)S(1)}, bf16[96,256]{1,0:T(8,128)(2,1)S(1)}, u32[]{:S(2)}, u32[]{:S(2)}) collective-permute-start(bf16[96,256]{1,0:T(8,128)(2,1)S(1)} %get-tuple-element.42), channel_id=1, source_target_pairs={{0,8},{8,0},{16,24},{24,16},{32,40},{40,32},{48,56},{56,48},{64,72... | collective-permute-start | bytes 147464 | tf_op jit(solution)/shard_map/ppermute | solution.py:624
  12.2 9.1 %collective-permute-start.3 = (bf16[96,256]{1,0:T(8,128)(2,1)S(1)}, bf16[96,256]{1,0:T(8,128)(2,1)S(1)}, u32[]{:S(2)}, u32[]{:S(2)}) collective-permute-start(bf16[96,256]{1,0:T(8,128)(2,1)S(1)} %get-tuple-element.43), channel_id=1, source_target_pairs={{8,16},{16,8},{24,32},{32,24},{40,48},{48,40},{56,64},{64,56},{72,... | collective-permute-start | bytes 147464 | tf_op jit(solution)/shard_map/ppermute | solution.py:624
  21.6 4.9 %collective-permute-start.4 = (f32[2,3,64,128]{3,2,1,0:T(8,128)S(1)}, f32[2,3,64,128]{3,2,1,0:T(8,128)S(1)}, u32[]{:S(2)}, u32[]{:S(2)}) collective-permute-start(f32[2,3,64,128]{3,2,1,0:T(8,128)S(1)} %get-tuple-element.53), channel_id=1, source_target_pairs={{0,128},{128,0},{1,129},{129,1},{2,130},{130,2},{3,131},{131,3},{4... | collective-permute-start | bytes 589832 | tf_op jit(solution)/shard_map/ppermute | solution.py:708
  27.9 2.8 %collective-permute-start.5 = (bf16[128,128]{1,0:T(8,128)(2,1)S(1)}, bf16[128,128]{1,0:T(8,128)(2,1)S(1)}, u32[]{:S(2)}, u32[]{:S(2)}) collective-permute-start(bf16[128,128]{1,0:T(8,128)(2,1)S(1)} %get-tuple-element.60), channel_id=1, source_target_pairs={{0,1},{1,0},{2,3},{3,2},{4,5},{5,4},{6,7},{7,6},{8,9},{9,8},{10,11... | collective-permute-start | bytes 98312 | tf_op jit(solution)/shard_map/ppermute | solution.py:624
  28.0 5.0 %collective-permute-start.6 = (bf16[128,128]{1,0:T(8,128)(2,1)S(1)}, bf16[128,128]{1,0:T(8,128)(2,1)S(1)}, u32[]{:S(2)}, u32[]{:S(2)}) collective-permute-start(bf16[128,128]{1,0:T(8,128)(2,1)S(1)} %get-tuple-element.61), channel_id=1, source_target_pairs={{1,2},{2,1},{3,4},{4,3},{5,6},{6,5},{7,0},{0,7},{9,10},{10,9},{11,... | collective-permute-start | bytes 98312 | tf_op jit(solution)/shard_map/ppermute | solution.py:624
  33.4 8.4 %collective-permute-start.7 = (bf16[96,128]{1,0:T(8,128)(2,1)S(1)}, bf16[96,128]{1,0:T(8,128)(2,1)S(1)}, u32[]{:S(2)}, u32[]{:S(2)}) collective-permute-start(bf16[96,128]{1,0:T(8,128)(2,1)S(1)} %get-tuple-element.62), channel_id=1, source_target_pairs={{0,8},{8,0},{16,24},{24,16},{32,40},{40,32},{48,56},{56,48},{64,72... | collective-permute-start | bytes 73736 | tf_op jit(solution)/shard_map/ppermute | solution.py:624
  33.5 8.3 %collective-permute-start.8 = (bf16[96,128]{1,0:T(8,128)(2,1)S(1)}, bf16[96,128]{1,0:T(8,128)(2,1)S(1)}, u32[]{:S(2)}, u32[]{:S(2)}) collective-permute-start(bf16[96,128]{1,0:T(8,128)(2,1)S(1)} %get-tuple-element.63), channel_id=1, source_target_pairs={{8,16},{16,8},{24,32},{32,24},{40,48},{48,40},{56,64},{64,56},{72,... | collective-permute-start | bytes 73736 | tf_op jit(solution)/shard_map/ppermute | solution.py:624

commit v4 on v3

--- a/solution.py
+++ b/solution.py
@@ -34,7 +34,7 @@
 TRAVEL = jnp.bfloat16
 F32 = jnp.float32
 VMEM = pltpu.VMEM
-GRANT, GRANT_MORE, GRANT_MOST = 24, 40, 53.7
+GRANT, GRANT_MOST = 24, 53.6
 
 
 def lanes(rows):
@@ -66,7 +66,7 @@
 
 def sides(first, second, even):
     first, second = first.astype(F32), second.astype(F32)
-    return jnp.where(even, second, first), jnp.where(even, first, second)
+    return jnp.where(even, first, second), jnp.where(even, second, first)
 
 
 def turn(plane):
@@ -87,20 +87,15 @@
     second_ref[...] = jnp.where(even, low, high).astype(TRAVEL)
 
 
-def start_kernel(
+def rows_kernel(
     model_ref,
     control_ref,
-    bottom_ref,
-    first_ref,
-    second_ref,
+    low_ref,
+    high_ref,
     control_low,
     control_high,
     model_low,
     model_high,
-    bottom_low,
-    bottom_high,
-    low_ref,
-    high_ref,
     sems,
 ):
     ends = pl.ds(0, EDGE), pl.ds(ROWS - EDGE, EDGE)
@@ -110,8 +105,6 @@
         pltpu.make_async_copy(control_ref.at[:, :, ends[1], :], control_high, sems.at[1]),
         pltpu.make_async_copy(model_ref.at[:, :, tips[0], :], model_low, sems.at[2]),
         pltpu.make_async_copy(model_ref.at[:, :, tips[1], :], model_high, sems.at[3]),
-        pltpu.make_async_copy(bottom_ref.at[ends[0], :], bottom_low, sems.at[4]),
-        pltpu.make_async_copy(bottom_ref.at[ends[1], :], bottom_high, sems.at[5]),
     ]
     for copy in copies:
         copy.start()
@@ -123,8 +116,6 @@
         lambda p: control_low[p // LEVELS, p % LEVELS, :HALO, :],
         lambda p: control_high[p // LEVELS, p % LEVELS, EDGE - HALO :, :],
     )
-    low_ref[DEPTH_ROW:MODEL_ROW, :] = bottom_low[:HALO, :].astype(F32)
-    high_ref[DEPTH_ROW:MODEL_ROW, :] = bottom_high[EDGE - HALO :, :].astype(F32)
     for q in range(STEPPED):
         for ref, value in (
             (low_ref, model_low[q // HALF, q % HALF, :1, :]),
@@ -137,6 +128,13 @@
     rest = MODEL_ROW + 2 * STEPPED
     low_ref[rest:, :] = jnp.zeros((LONG - rest, COLS), F32)
     high_ref[rest:, :] = jnp.zeros((LONG - rest, COLS), F32)
+
+
+def start_kernel(bottom_ref, first_low, first_high, first_ref, second_ref, low_ref, high_ref):
+    low_ref[...] = first_low[...]
+    high_ref[...] = first_high[...]
+    low_ref[DEPTH_ROW:MODEL_ROW, :] = bottom_ref[:HALO, :].astype(F32)
+    high_ref[DEPTH_ROW:MODEL_ROW, :] = bottom_ref[ROWS - HALO :, :].astype(F32)
     send_rows(low_ref, high_ref, first_ref, second_ref)
 
 
@@ -505,18 +503,9 @@
 
 
 def prepare_kernel(*refs):
-    here_refs, out_refs, (*held_refs, sems) = refs[:8], refs[8:16], refs[16:]
-    copies = [
-        pltpu.make_async_copy(source, target, sems.at[i])
-        for i, (source, target) in enumerate(zip(here_refs, held_refs))
-    ]
-    for copy in copies:
-        copy.start()
-    for copy in copies:
-        copy.wait()
-    count_ref, model_ref, error_ref, bottom_ref = held_refs[:4]
-    corner_ref, weight_ref, value_ref, precision_ref = held_refs[4:]
-    east_ref, west_ref, scale_ref, pick_ref, back_ref, lower_ref, upper_ref, want_ref = out_refs
+    count_ref, model_ref, error_ref, bottom_ref, *observed_refs = refs[:8]
+    corner_ref, weight_ref, value_ref, precision_ref = observed_refs
+    east_ref, west_ref, scale_ref, pick_ref, back_ref, lower_ref, upper_ref, want_ref = refs[8:]
     model_columns(model_ref, east_ref, west_ref)
     depth = bottom_ref[...]
     for plane in range(PLANES):
@@ -625,7 +614,7 @@
 
 
 def exchange(first, second, axis):
-    return swap(first, axis, 0), swap(second, axis, 1)
+    return swap(second, axis, 1), swap(first, axis, 0)
 
 
 FULL = ((PLANES, ROWS, COLS), F32)
@@ -658,15 +647,15 @@
 ):
     dma = pltpu.SemaphoreType.DMA
     long, short = VMEM((LONG, COLS), F32), VMEM((SHORT, COLS), F32)
-    first, second = call(
-        start_kernel,
-        [rows_of(LONG)] * 2,
+    low, high = call(
+        rows_kernel,
+        [((LONG, COLS), F32)] * 2,
         [VMEM((PAIR, LEVELS, EDGE, COLS), F32)] * 2
         + [VMEM((FIELDS, HALF, 8, COLS), F32)] * 2
-        + [VMEM((EDGE, COLS), jnp.int32)] * 2
-        + [long, long, dma((6,))],
+        + [dma((4,))],
         remote=GRANT_MOST,
-    )(model_state, control, bottom_level)
+    )(model_state, control)
+    first, second = call(start_kernel, [rows_of(LONG)] * 2, [long, long])(bottom_level, low, high)
     mer = exchange(first, second, "mer")
     slots = obs_corner.shape[-1]
     inputs = (
@@ -686,8 +675,6 @@
         + [((2 * slots, PLANES * ROWS), jnp.bfloat16), ((PLANES * ROWS, 2 * slots), jnp.bfloat16)]
         + [((slots, COLS), F32)] * 2
         + [((slots, 8), F32)],
-        [VMEM(value.shape, value.dtype) for value in inputs] + [dma((len(inputs),))],
-        remote=GRANT_MORE,
         work=10**7,
     )(*inputs)
     tall, depth, west, east, first, second = call(

time: 44.6 us -> 43.4 us (0.973)
  waiting for transfers between devices: 2.89 us -> 7.41 us
  starting transfers between devices: 23.7 us -> 19.2 us
  local copies, waits for them, and re-layouts: 0.84 us -> 0.04 us
  Pallas kernels: 16.2 us -> 15.7 us
    ppermute x8, starting transfers between devices: 20.9 us -> 16.1 us  [swap(): return lax.ppermute(value, axis, pairs)]
    ppermute x8, waiting for transfers between devices: 2.88 us -> 7.4 us  [swap(): return lax.ppermute(value, axis, pairs)]
    unnamed x16, local copies, waits for them, and re-layouts: 0.84 us -> 0.04 us
    pallas_call x10 -> x11, Pallas kernels: 16.2 us -> 15.7 us  [run(): pl.pallas_call(kernel, out_shape=[jax.ShapeDtypeStruct(shape, kind) for s...]
  transfers between devices with their start and end apart: 9 -> 9, of which waited for: 3 -> 4; matrix products, arithmetic and copies ran while one was open for 0% -> 0% of each run, Pallas kernels for 23% -> 22%
where the time goes in v4:
time: 43.4 us; the launch traced here: 43.3 us
  starting transfers between devices  19.2 us (44%)
  Pallas kernels  15.7 us (36%)
  waiting for transfers between devices  7.41 us (17%)
  between operations  0.86 us (2%)
    ppermute x8, starting transfers between devices, swap(): return lax.ppermute(value, axis, pairs)  16.1 us
    pallas_call x11, Pallas kernels, run(): pl.pallas_call(kernel, out_shape=[jax.ShapeDtypeStruct(shape, kind) for s...  15.7 us
    ppermute x8, waiting for transfers between devices, swap(): return lax.ppermute(value, axis, pairs)  7.4 us
    ppermute x1, starting transfers between devices, body(): other = lax.ppermute(send, 'grp', [(0, 1), (1, 0)])  3.18 us
  transfers between devices with their start and end apart: 9, of which 4 were waited for; matrix products, arithmetic and copies ran while one was open for 0% of the time, Pallas kernels for 22%

profile of v4, /device:TPU:1, one launch (start us, length us, event | category | flops | bytes accessed | tf_op | source)
XLA Modules:
  0.0 43.3 jit_solution(3282639506949142547)
XLA Ops:
  0.0 0.0 copy-start
  0.0 0.0 copy-start.3
  0.0 0.0 copy-start.2
  0.0 1.1 %rows.1 = (f32[160,128]{1,0:T(8,128)S(1)}, f32[160,128]{1,0:T(8,128)S(1)}) custom-call(f32[4,3,64,128]{3,2,1,0:T(8,128)} %model_ref.5, f32[2,6,64,128]{3,2,1,0:T(8,128)} %control_ref.5), custom_call_target="tpu_custom_call" | custom-call | tf_op jit(solution)/shard_map/rows/pallas_call | solution.py:587
  1.1 0.0 copy-done.3
  1.1 0.0 copy-start.6
  1.1 0.0 copy-start.7
  1.2 0.0 copy-start.4
  1.2 4.4 %collective-permute-start = (bf16[160,128]{1,0:T(8,128)(2,1)S(1)}, bf16[160,128]{1,0:T(8,128)(2,1)S(1)}, u32[]{:S(2)}, u32[]{:S(2)}) collective-permute-start(bf16[160,128]{1,0:T(8,128)(2,1)S(1)} %get-tuple-element.44), channel_id=1, source_target_pairs={{1,2},{2,1},{3,4},{4,3},{5,6},{6,5},{7,0},{0,7},{9,10},{10,9},{11,... | collective-permute-start | bytes 122888 | tf_op jit(solution)/shard_map/ppermute | solution.py:613
  5.6 0.0 copy-start.5
  5.6 0.0 collective-permute-start.1
  6.3 0.0 copy-done
  6.3 0.0 copy-done.2
  6.3 0.0 copy-done.6
  6.3 0.0 copy-done.7
  6.3 0.0 copy-done.4
  6.3 0.0 copy-done.5
  6.3 0.0 copy-start.1
  6.3 1.0 %prepare.1 = (f32[64,128]{1,0:T(8,128)S(1)}, f32[64,128]{1,0:T(8,128)S(1)}, f32[12,64,128]{2,1,0:T(8,128)S(1)}, bf16[512,768]{1,0:T(8,128)(2,1)S(1)}, bf16[768,5...) custom-call(s32[1,1,1]{2,1,0:T(1,128)S(6)} %copy.10.refs_0_, ...), custom_call_target="tpu_custom_call" | custom-call | flops 10000000 | bytes 1000000 | tf_op jit(solution)/shard_map/prepare/pallas_call | solution.py:587
  7.3 0.0 collective-permute-done.a_ref
  7.3 1.1 %collective-permute-done.1.b_ref = bf16[160,128]{1,0:T(8,128)(2,1)S(1)} collective-permute-done((bf16[160,128]{1,0:T(8,128)(2,1)S(1)}, bf16[160,128]{1,0:T(8,128)(2,1)S(1)}, u32[]{:S(2)}, u32[]{:S(2)}) %collective-permute-start.1) | collective-permute-done | bytes 40992 | tf_op jit(solution)/shard_map/ppermute | solution.py:613
  8.4 0.0 copy-done.1
  8.4 0.4 first_columns.1
  8.9 8.4 %collective-permute-start.2 = (bf16[96,256]{1,0:T(8,128)(2,1)S(1)}, bf16[96,256]{1,0:T(8,128)(2,1)S(1)}, u32[]{:S(2)}, u32[]{:S(2)}) collective-permute-start(bf16[96,256]{1,0:T(8,128)(2,1)S(1)} %get-tuple-element.46), channel_id=1, source_target_pairs={{8,16},{16,8},{24,32},{32,24},{40,48},{48,40},{56,64},{64,56},{72,... | collective-permute-start | bytes 147464 | tf_op jit(solution)/shard_map/ppermute | solution.py:613
  17.3 0.0 collective-permute-start.3
  17.3 3.4 %first_interior.1 = (f32[12,64,128]{2,1,0:T(8,128)S(1)}, f32[6,112,128]{2,1,0:T(8,128)S(1)}, f32[6,112,128]{2,1,0:T(8,128)S(1)}, f32[4,3,64,128]{3,2,1,0:T(8,128)S(1)}) custom-call(f32[12,96,128]{2,1,0:T(8,128)S(1)} %get-tuple-element.51.tall_ref, f32[96,128]{1,0:T(8,128)S(1)} %get-tuple-element.50.depth_ref, f32[4,3,64,128]{3,2,1,0:T(8,128)S(1)} %copy-done, ...), custom_call_target="tpu_custom_call" | custom-call | flops 10000000 | bytes 1000000 | tf_op jit(solution)/shard_map/first_interior/pallas_call | solution.py:587
  20.7 0.0 collective-permute-done.2.first_ref
  20.7 1.0 %collective-permute-done.3.second_ref = bf16[96,256]{1,0:T(8,128)(2,1)S(1)} collective-permute-done((bf16[96,256]{1,0:T(8,128)(2,1)S(1)}, bf16[96,256]{1,0:T(8,128)(2,1)S(1)}, u32[]{:S(2)}, u32[]{:S(2)}) %collective-permute-start.3) | collective-permute-done | bytes 49184 | tf_op jit(solution)/shard_map/ppermute | solution.py:613
  21.7 0.3 background.1
  22.0 3.2 %collective-permute-start.4 = (f32[2,3,64,128]{3,2,1,0:T(8,128)S(1)}, f32[2,3,64,128]{3,2,1,0:T(8,128)S(1)}, u32[]{:S(2)}, u32[]{:S(2)}) collective-permute-start(f32[2,3,64,128]{3,2,1,0:T(8,128)S(1)} %get-tuple-element.57), channel_id=1, source_target_pairs={{0,128},{128,0},{1,129},{129,1},{2,130},{130,2},{3,131},{131,3},{4... | collective-permute-start | bytes 589832 | tf_op jit(solution)/shard_map/ppermute | solution.py:695
  25.2 2.2 %first_bands.1 = (f32[12,64,128]{2,1,0:T(8,128)S(1)}, f32[6,112,128]{2,1,0:T(8,128)S(1)}, f32[6,112,128]{2,1,0:T(8,128)S(1)}) custom-call(bf16[96,256]{1,0:T(8,128)(2,1)S(1)} %collective-permute-done.2.first_ref, bf16[96,256]{1,0:T(8,128)(2,1)S(1)} %collective-permute-done.3.second_ref, f32[3,96,128]{2,1,0:T(8,128)S(1)} %get-tuple-element.48.west_ref, ...), custom_call_target="tpu_custom_call" | custom-call | flops 10000000 | bytes 1000000 | tf_op jit(solution)/shard_map/first_bands/pallas_call | solution.py:587
  27.4 0.0 collective-permute-done.4.other_ref
  27.4 1.4 %observe.1 = (f32[12,64,128]{2,1,0:T(8,128)S(1)}, bf16[128,128]{1,0:T(8,128)(2,1)S(1)}, bf16[128,128]{1,0:T(8,128)(2,1)S(1)}) custom-call(f32[12,64,128]{2,1,0:T(8,128)S(1)} %get-tuple-element.53.smooth_ref, f32[12,64,128]{2,1,0:T(8,128)S(1)} %get-tuple-element.54.scale_ref, f32[2,3,64,128]{3,2,1,0:T(8,128)S(1)} %get-tuple-element.56.keep_ref, ...), custom_call_target="tpu_custom_call" | custom-call | tf_op jit(solution)/shard_map/observe/pallas_call | solution.py:587
  28.8 1.3 %collective-permute-start.5 = (bf16[128,128]{1,0:T(8,128)(2,1)S(1)}, bf16[128,128]{1,0:T(8,128)(2,1)S(1)}, u32[]{:S(2)}, u32[]{:S(2)}) collective-permute-start(bf16[128,128]{1,0:T(8,128)(2,1)S(1)} %get-tuple-element.64), channel_id=1, source_target_pairs={{1,2},{2,1},{3,4},{4,3},{5,6},{6,5},{7,0},{0,7},{9,10},{10,9},{11,... | collective-permute-start | bytes 98312 | tf_op jit(solution)/shard_map/ppermute | solution.py:613
  30.1 0.0 collective-permute-start.6
  30.1 3.8 %collective-permute-done.5.a_ref = bf16[128,128]{1,0:T(8,128)(2,1)S(1)} collective-permute-done((bf16[128,128]{1,0:T(8,128)(2,1)S(1)}, bf16[128,128]{1,0:T(8,128)(2,1)S(1)}, u32[]{:S(2)}, u32[]{:S(2)}) %collective-permute-start.5) | collective-permute-done | bytes 32800 | tf_op jit(solution)/shard_map/ppermute | solution.py:613
  33.8 0.0 collective-permute-done.6.b_ref
  33.8 0.4 next_columns.1
  34.3 1.9 %collective-permute-start.7 = (bf16[96,128]{1,0:T(8,128)(2,1)S(1)}, bf16[96,128]{1,0:T(8,128)(2,1)S(1)}, u32[]{:S(2)}, u32[]{:S(2)}) collective-permute-start(bf16[96,128]{1,0:T(8,128)(2,1)S(1)} %get-tuple-element.66), channel_id=1, source_target_pairs={{8,16},{16,8},{24,32},{32,24},{40,48},{48,40},{56,64},{64,56},{72,... | collective-permute-start | bytes 73736 | tf_op jit(solution)/shard_map/ppermute | solution.py:613
  36.1 0.0 collective-permute-start.8
  36.1 3.0 %next_interior.1.inner_ref = f32[12,64,128]{2,1,0:T(8,128)S(1)} custom-call(f32[12,96,128]{2,1,0:T(8,128)S(1)} %get-tuple-element.70.tall_ref, f32[6,112,128]{2,1,0:T(8,128)S(1)} %get-tuple-element.71.keep_ref, f32[6,112,128]{2,1,0:T(8,128)S(1)} %get-tuple-element.72.give_ref), custom_call_target="tpu_custom_call" | custom-call | flops 10000000 | bytes 1000000 | tf_op jit(solution)/shard_map/next_interior/pallas_call | solution.py:587
  39.1 1.5 %collective-permute-done.7.first_ref = bf16[96,128]{1,0:T(8,128)(2,1)S(1)} collective-permute-done((bf16[96,128]{1,0:T(8,128)(2,1)S(1)}, bf16[96,128]{1,0:T(8,128)(2,1)S(1)}, u32[]{:S(2)}, u32[]{:S(2)}) %collective-permute-start.7) | collective-permute-done | bytes 24608 | tf_op jit(solution)/shard_map/ppermute | solution.py:613
  40.6 0.0 collective-permute-done.8.second_ref
  40.6 2.6 %gradient.1 = f32[2,6,64,128]{3,2,1,0:T(8,128)} custom-call(bf16[96,128]{1,0:T(8,128)(2,1)S(1)} %collective-permute-done.7.first_ref, bf16[96,128]{1,0:T(8,128)(2,1)S(1)} %collective-permute-done.8.second_ref, f32[3,96,128]{2,1,0:T(8,128)S(1)} %get-tuple-element.68.west_ref, f32[3,96,128]{2,1,0:T(8,128)S(1)} %get-tuple-element.69.east_ref, ...), custom_call_target="tpu_custom_call" | custom-call | tf_op jit(solution)/shard_map/gradient/pallas_call | solution.py:587
  (1 shorter events, 0.0 us)
Async XLA Ops:
  0.0 6.3 %copy-start = (f32[4,3,64,128]{3,2,1,0:T(8,128)S(1)}, f32[4,3,64,128]{3,2,1,0:T(8,128)}, u32[]{:S(2)}) copy-start(f32[4,3,64,128]{3,2,1,0:T(8,128)} %model_ref.5) | copy-start | bytes 1179652
  0.0 1.1 %copy-start.3 = (s32[64,128]{1,0:T(8,128)S(1)}, s32[64,128]{1,0:T(8,128)}, u32[]{:S(2)}) copy-start(s32[64,128]{1,0:T(8,128)} %bottom_ref.3) | copy-start | bytes 98308
  0.0 6.3 %copy-start.2 = (f32[2,6,64,128]{3,2,1,0:T(8,128)S(1)}, f32[2,6,64,128]{3,2,1,0:T(8,128)}, u32[]{:S(2)}) copy-start(f32[2,6,64,128]{3,2,1,0:T(8,128)} %refs_2_.1) | copy-start | bytes 1179652
  1.1 5.2 %copy-start.6 = (f32[1,1,1,256]{3,2,1,0:T(1,128)S(1)}, f32[1,1,1,256]{3,2,1,0:T(1,128)}, u32[]{:S(2)}) copy-start(f32[1,1,1,256]{3,2,1,0:T(1,128)} %refs_6_.1) | copy-start | bytes 3076
  1.1 5.2 %copy-start.7 = (f32[1,1,1,256]{3,2,1,0:T(1,128)S(1)}, f32[1,1,1,256]{3,2,1,0:T(1,128)}, u32[]{:S(2)}) copy-start(f32[1,1,1,256]{3,2,1,0:T(1,128)} %refs_7_.1) | copy-start | bytes 3076
  1.2 5.1 %copy-start.4 = (f32[1,1,1,4,256]{4,3,2,1,0:T(4,128)S(1)}, f32[1,1,1,4,256]{4,3,2,1,0:T(4,128)}, u32[]{:S(2)}) copy-start(f32[1,1,1,4,256]{4,3,2,1,0:T(4,128)} %refs_5_.1) | copy-start | bytes 12292
  1.2 6.1 %collective-permute-start = (bf16[160,128]{1,0:T(8,128)(2,1)S(1)}, bf16[160,128]{1,0:T(8,128)(2,1)S(1)}, u32[]{:S(2)}, u32[]{:S(2)}) collective-permute-start(bf16[160,128]{1,0:T(8,128)(2,1)S(1)} %get-tuple-element.44), channel_id=1, source_target_pairs={{1,2},{2,1},{3,4},{4,3},{5,6},{6,5},{7,0},{0,7},{9,10},{10,9},{11,... | collective-permute-start | bytes 122888 | tf_op jit(solution)/shard_map/ppermute | solution.py:613
  5.6 0.7 %copy-start.5 = (s32[1,1,1,256]{3,2,1,0:T(1,128)S(1)}, s32[1,1,1,256]{3,2,1,0:T(1,128)}, u32[]{:S(2)}) copy-start(s32[1,1,1,256]{3,2,1,0:T(1,128)} %refs_4_.1) | copy-start | bytes 3076
  5.6 2.9 %collective-permute-start.1 = (bf16[160,128]{1,0:T(8,128)(2,1)S(1)}, bf16[160,128]{1,0:T(8,128)(2,1)S(1)}, u32[]{:S(2)}, u32[]{:S(2)}) collective-permute-start(bf16[160,128]{1,0:T(8,128)(2,1)S(1)} %get-tuple-element.45), channel_id=1, source_target_pairs={{0,1},{1,0},{2,3},{3,2},{4,5},{5,4},{6,7},{7,6},{8,9},{9,8},{10,11... | collective-permute-start | bytes 122888 | tf_op jit(solution)/shard_map/ppermute | solution.py:613
  6.3 2.1 %copy-start.1 = (f32[2,6,64,128]{3,2,1,0:T(8,128)S(1)}, f32[2,6,64,128]{3,2,1,0:T(8,128)}, u32[]{:S(2)}) copy-start(f32[2,6,64,128]{3,2,1,0:T(8,128)} %control_ref.5) | copy-start | bytes 1179652
  8.9 11.9 %collective-permute-start.2 = (bf16[96,256]{1,0:T(8,128)(2,1)S(1)}, bf16[96,256]{1,0:T(8,128)(2,1)S(1)}, u32[]{:S(2)}, u32[]{:S(2)}) collective-permute-start(bf16[96,256]{1,0:T(8,128)(2,1)S(1)} %get-tuple-element.46), channel_id=1, source_target_pairs={{8,16},{16,8},{24,32},{32,24},{40,48},{48,40},{56,64},{64,56},{72,... | collective-permute-start | bytes 147464 | tf_op jit(solution)/shard_map/ppermute | solution.py:613
  17.3 4.4 %collective-permute-start.3 = (bf16[96,256]{1,0:T(8,128)(2,1)S(1)}, bf16[96,256]{1,0:T(8,128)(2,1)S(1)}, u32[]{:S(2)}, u32[]{:S(2)}) collective-permute-start(bf16[96,256]{1,0:T(8,128)(2,1)S(1)} %get-tuple-element.47), channel_id=1, source_target_pairs={{0,8},{8,0},{16,24},{24,16},{32,40},{40,32},{48,56},{56,48},{64,72... | collective-permute-start | bytes 147464 | tf_op jit(solution)/shard_map/ppermute | solution.py:613
  22.0 5.4 %collective-permute-start.4 = (f32[2,3,64,128]{3,2,1,0:T(8,128)S(1)}, f32[2,3,64,128]{3,2,1,0:T(8,128)S(1)}, u32[]{:S(2)}, u32[]{:S(2)}) collective-permute-start(f32[2,3,64,128]{3,2,1,0:T(8,128)S(1)} %get-tuple-element.57), channel_id=1, source_target_pairs={{0,128},{128,0},{1,129},{129,1},{2,130},{130,2},{3,131},{131,3},{4... | collective-permute-start | bytes 589832 | tf_op jit(solution)/shard_map/ppermute | solution.py:695
  28.8 5.1 %collective-permute-start.5 = (bf16[128,128]{1,0:T(8,128)(2,1)S(1)}, bf16[128,128]{1,0:T(8,128)(2,1)S(1)}, u32[]{:S(2)}, u32[]{:S(2)}) collective-permute-start(bf16[128,128]{1,0:T(8,128)(2,1)S(1)} %get-tuple-element.64), channel_id=1, source_target_pairs={{1,2},{2,1},{3,4},{4,3},{5,6},{6,5},{7,0},{0,7},{9,10},{10,9},{11,... | collective-permute-start | bytes 98312 | tf_op jit(solution)/shard_map/ppermute | solution.py:613
  30.1 3.8 %collective-permute-start.6 = (bf16[128,128]{1,0:T(8,128)(2,1)S(1)}, bf16[128,128]{1,0:T(8,128)(2,1)S(1)}, u32[]{:S(2)}, u32[]{:S(2)}) collective-permute-start(bf16[128,128]{1,0:T(8,128)(2,1)S(1)} %get-tuple-element.65), channel_id=1, source_target_pairs={{0,1},{1,0},{2,3},{3,2},{4,5},{5,4},{6,7},{7,6},{8,9},{9,8},{10,11... | collective-permute-start | bytes 98312 | tf_op jit(solution)/shard_map/ppermute | solution.py:613
  34.3 6.4 %collective-permute-start.7 = (bf16[96,128]{1,0:T(8,128)(2,1)S(1)}, bf16[96,128]{1,0:T(8,128)(2,1)S(1)}, u32[]{:S(2)}, u32[]{:S(2)}) collective-permute-start(bf16[96,128]{1,0:T(8,128)(2,1)S(1)} %get-tuple-element.66), channel_id=1, source_target_pairs={{8,16},{16,8},{24,32},{32,24},{40,48},{48,40},{56,64},{64,56},{72,... | collective-permute-start | bytes 73736 | tf_op jit(solution)/shard_map/ppermute | solution.py:613
  36.1 4.5 %collective-permute-start.8 = (bf16[96,128]{1,0:T(8,128)(2,1)S(1)}, bf16[96,128]{1,0:T(8,128)(2,1)S(1)}, u32[]{:S(2)}, u32[]{:S(2)}) collective-permute-start(bf16[96,128]{1,0:T(8,128)(2,1)S(1)} %get-tuple-element.67), channel_id=1, source_target_pairs={{0,8},{8,0},{16,24},{24,16},{32,40},{40,32},{48,56},{56,48},{64,72... | collective-permute-start | bytes 73736 | tf_op jit(solution)/shard_map/ppermute | solution.py:613

commit v5 on v4

--- a/solution.py
+++ b/solution.py
@@ -23,9 +23,8 @@
 TALL = ROWS + 2 * EDGE
 PAD = 8
 DEEP = TALL + 2 * PAD
-BAND = 3 * HALO
-LANES = COLS // BAND
-BANDS = PLANES // LANES
+BAND = 2 * HALO + 1
+BANDS = 2 * PAIR
 DEPTH_ROW = PLANES * HALO
 MODEL_ROW = DEPTH_ROW + HALO
 LONG = 160
@@ -69,8 +68,8 @@
     return jnp.where(even, first, second), jnp.where(even, second, first)
 
 
-def turn(plane):
-    return BAND * (plane % LANES) + 2 * HALO
+def turn(level):
+    return BAND * level + HALO + 1
 
 
 def stage(low_ref, high_ref, low, high):
@@ -180,25 +179,20 @@
         tall_ref[plane, EDGE + ROWS + HALO :, :] = blank
 
 
-def cut_bands(tall_ref, west_ref, east_ref):
+def turn_planes(tall_ref, turned_ref):
     lane = lanes(TALL)
-    blank = jnp.zeros((TALL, COLS), F32)
-    to_east, to_west = blank, blank
-    for group in range(BANDS):
-        west = east = go_east = go_west = blank
-        for j in range(LANES):
-            plane = group * LANES + j
-            turned = roll(tall_ref[plane], turn(plane))
-            at = BAND * j
-            west = jnp.where(window(lane, at + 2 * HALO, 2 * HALO), turned, west)
-            east = jnp.where(window(lane, at, 2 * HALO), turned, east)
-            go_east = jnp.where(window(lane, at + HALO, HALO), turned, go_east)
-            go_west = jnp.where(window(lane, at + 2 * HALO, HALO), turned, go_west)
-        west_ref[group] = west
-        east_ref[group] = east
-        to_east = to_east + roll(go_east, HALO * group)
-        to_west = to_west + roll(go_west, HALO * group)
-    return to_east, to_west
+    to_east, to_west = [], []
+    for f in range(PAIR):
+        go_east = go_west = jnp.zeros((TALL, COLS), F32)
+        for k in range(LEVELS):
+            turned = roll(tall_ref[f * LEVELS + k], turn(k))
+            turned_ref[f * LEVELS + k] = turned
+            at = BAND * k
+            go_east = jnp.where(window(lane, at + 1, HALO), turned, go_east)
+            go_west = jnp.where(window(lane, at + 1 + HALO, HALO), turned, go_west)
+        to_east.append(go_east)
+        to_west.append(go_west)
+    return to_east[0] + roll(to_east[1], HALO), to_west[0] + roll(to_west[1], -HALO)
 
 
 def send_columns(part, to_east, to_west, first_ref, second_ref):
@@ -215,19 +209,18 @@
     model_west_ref,
     a_ref,
     b_ref,
-    tall_ref,
+    turned_ref,
     depth_ref,
-    west_ref,
-    east_ref,
     first_ref,
     second_ref,
     low_ref,
     high_ref,
+    tall_ref,
 ):
     raise_planes(
         lambda p: control_ref[p // LEVELS, p % LEVELS], a_ref, b_ref, low_ref, high_ref, tall_ref
     )
-    send_columns(0, *cut_bands(tall_ref, west_ref, east_ref), first_ref, second_ref)
+    send_columns(0, *turn_planes(tall_ref, turned_ref), first_ref, second_ref)
     depth = stand(
         bottom_ref[...].astype(F32),
         low_ref[DEPTH_ROW:MODEL_ROW, :],
@@ -245,10 +238,10 @@
 
 
 def next_columns_kernel(
-    field_ref, a_ref, b_ref, tall_ref, west_ref, east_ref, first_ref, second_ref, low_ref, high_ref
+    field_ref, a_ref, b_ref, turned_ref, first_ref, second_ref, low_ref, high_ref, tall_ref
 ):
     raise_planes(lambda p: field_ref[p], a_ref, b_ref, low_ref, high_ref, tall_ref)
-    send_columns(0, *cut_bands(tall_ref, west_ref, east_ref), first_ref, second_ref)
+    send_columns(0, *turn_planes(tall_ref, turned_ref), first_ref, second_ref)
 
 
 def base_step(model_ref, depth_ref, a_ref, b_ref, base_ref, low_ref, high_ref, tall_ref):
@@ -330,24 +323,51 @@
         give_ref[index, PAD : PAD + TALL, :] = SMOOTHING * wet
 
 
-def sweep_all(count, masks, keep_ref, give_ref, one_ref, two_ref):
-    def sweep(source_ref, target_ref, start, rows):
-        for index in range(count):
-            here, total = neighbour_sum(source_ref, index, start, rows)
-            at = pl.ds(start, rows)
-            target_ref[index, at, :] = (
-                keep_ref[index % masks, at, :] * here + give_ref[index % masks, at, :] * total
+def sweep_all(sweep):
+    sweep(0, 0, PAD, TALL)
+    sweep(1, 1, 2 * PAD, TALL - 2 * PAD)
+
+    def pair(step, carry):
+        sweep(2 * step + 2, 0, 2 * PAD, TALL - 2 * PAD)
+        sweep(2 * step + 3, 1, 2 * PAD, TALL - 2 * PAD)
+        return carry
+
+    lax.fori_loop(0, SWEEPS // 2 - 1, pair, 0)
+
+
+def sweep_planes(keep_ref, give_ref, one_ref, two_ref, record_refs):
+    def sweep(index, odd, start, rows):
+        source_ref, target_ref = (two_ref, one_ref) if odd else (one_ref, two_ref)
+        at = pl.ds(start, rows)
+        lane = lanes(rows)
+        for f in range(PAIR):
+            west = east = jnp.zeros((rows, COLS), F32)
+            for k in range(LEVELS):
+                plane = f * LEVELS + k
+                here, total = neighbour_sum(source_ref, plane, start, rows)
+                target_ref[plane, at, :] = keep_ref[k, at, :] * here + give_ref[k, at, :] * total
+                west = jnp.where(lane == BAND * (k + 1), here, west)
+                east = jnp.where(lane == BAND * k, here, east)
+            record_refs[f][index, at, :] = west
+            record_refs[PAIR + f][index, at, :] = east
+
+    sweep_all(sweep)
+
+
+def sweep_bands(keep_ref, give_ref, one_ref, two_ref, record_refs):
+    def sweep(index, odd, start, rows):
+        source_ref, target_ref = (two_ref, one_ref) if odd else (one_ref, two_ref)
+        at = pl.ds(start, rows)
+        for tile in range(BANDS):
+            here = source_ref[tile, at, :] + record_refs[tile][index, at, :]
+            total = (roll(here, -1) + roll(here, 1)) + (
+                source_ref[tile, pl.ds(start - 1, rows), :]
+                + source_ref[tile, pl.ds(start + 1, rows), :]
             )
-
-    sweep(one_ref, two_ref, PAD, TALL)
-    sweep(two_ref, one_ref, 2 * PAD, TALL - 2 * PAD)
-
-    def step(index, carry):
-        sweep(one_ref, two_ref, 2 * PAD, TALL - 2 * PAD)
-        sweep(two_ref, one_ref, 2 * PAD, TALL - 2 * PAD)
-        return carry
-
-    lax.fori_loop(0, SWEEPS // 2 - 1, step, 0)
+            side = tile // PAIR
+            target_ref[tile, at, :] = keep_ref[side, at, :] * here + give_ref[side, at, :] * total
+
+    sweep_all(sweep)
 
 
 def clear_pads(ref, count):
@@ -360,17 +380,34 @@
 BODY = slice(PAD, PAD + TALL)
 
 
+def bands_of(one_ref, bands_ref):
+    lane = lanes(TALL)
+    for f in range(PAIR):
+        west = east = jnp.zeros((TALL, COLS), F32)
+        for k in range(LEVELS):
+            value = one_ref[f * LEVELS + k, BODY, :]
+            west = jnp.where(window(lane, BAND * k + 1 + HALO, HALO), value, west)
+            east = jnp.where(window(lane, BAND * k + 1, HALO), value, east)
+        bands_ref[f] = west
+        bands_ref[PAIR + f] = east
+
+
 def first_interior_kernel(
-    tall_ref,
+    turned_ref,
     depth_ref,
     model_ref,
     a_ref,
     b_ref,
     inner_ref,
+    bands_ref,
+    record_0,
+    record_1,
+    record_2,
+    record_3,
+    mask_ref,
     keep_ref,
     give_ref,
     base_ref,
-    mask_ref,
     one_ref,
     two_ref,
     low_ref,
@@ -382,58 +419,60 @@
     clear_pads(one_ref, PLANES)
     depth = depth_ref[...]
     for level in range(LEVELS):
-        wet = jnp.where(depth > level, 1.0, 0.0)
+        wet = roll(jnp.where(depth > level, 1.0, 0.0), turn(level))
         mask_ref[level, BODY, :] = wet
         for field in range(PAIR):
             plane = field * LEVELS + level
-            one_ref[plane, BODY, :] = wet * tall_ref[plane]
+            one_ref[plane, BODY, :] = wet * turned_ref[plane]
     coefficients(mask_ref, LEVELS, keep_ref, give_ref)
-    sweep_all(PLANES, LEVELS, keep_ref, give_ref, one_ref, two_ref)
+    bands_of(one_ref, bands_ref)
+    sweep_planes(keep_ref, give_ref, one_ref, two_ref, (record_0, record_1, record_2, record_3))
     for plane in range(PLANES):
         inner_ref[plane] = one_ref[plane, CORE, :]
 
 
-def next_interior_kernel(tall_ref, keep_ref, give_ref, inner_ref, one_ref, two_ref):
+def next_interior_kernel(
+    turned_ref, keep_ref, give_ref, inner_ref, bands_ref, record_0, record_1, record_2, record_3, one_ref, two_ref
+):
     clear_pads(one_ref, PLANES)
     for plane in range(PLANES):
-        one_ref[plane, BODY, :] = tall_ref[plane]
-    sweep_all(PLANES, LEVELS, keep_ref, give_ref, one_ref, two_ref)
+        one_ref[plane, BODY, :] = turned_ref[plane]
+    bands_of(one_ref, bands_ref)
+    sweep_planes(keep_ref, give_ref, one_ref, two_ref, (record_0, record_1, record_2, record_3))
     for plane in range(PLANES):
         inner_ref[plane] = one_ref[plane, CORE, :]
 
 
-def fill_bands(first_ref, second_ref, west_ref, east_ref, one_ref, mask_ref):
-    lane = lanes(TALL)
+def fill_bands(first_ref, second_ref, bands_ref, one_ref, mask_ref):
+    inside = lanes(TALL) % BAND
+    near, far = (inside >= 1) & (inside <= HALO), inside > HALO
     before, after = sides(first_ref[:, :COLS], second_ref[:, :COLS], even_on("zon"))
-    clear_pads(one_ref, 2 * BANDS)
-    in_west = (lane >= HALO) & ((lane - HALO) % BAND < HALO)
-    in_east = (lane >= 2 * HALO) & ((lane - 2 * HALO) % BAND < HALO)
-    for group in range(BANDS):
-        west = jnp.where(in_west, roll(before, -HALO * group), west_ref[group])
-        east = jnp.where(in_east, roll(after, -HALO * group), east_ref[group])
-        for index, value in ((group, west), (BANDS + group, east)):
-            if mask_ref is not None:
-                value = value * mask_ref[index, BODY, :]
-            one_ref[index, BODY, :] = value
+    clear_pads(one_ref, BANDS)
+    for f in range(PAIR):
+        west, east = (before, after) if f == 0 else (roll(before, -HALO), roll(after, HALO))
+        if mask_ref is not None:
+            west, east = west * mask_ref[0, BODY, :], east * mask_ref[1, BODY, :]
+        one_ref[f, BODY, :] = jnp.where(near, west, bands_ref[f])
+        one_ref[PAIR + f, BODY, :] = jnp.where(far, east, bands_ref[PAIR + f])
 
 
 def join_bands(one_ref, plane, inner, lane):
-    group, j = divmod(plane, LANES)
-    value = jnp.where(
-        window(lane, BAND * j + 2 * HALO, HALO),
-        one_ref[group, CORE, :],
-        one_ref[BANDS + group, CORE, :],
-    )
-    edge = (lane < HALO) | (lane >= COLS - HALO)
-    return jnp.where(edge, roll(value, -turn(plane)), inner)
+    f, k = divmod(plane, LEVELS)
+    at = BAND * k + 1
+    value = jnp.where(window(lane, at, HALO), one_ref[PAIR + f, CORE, :], inner)
+    value = jnp.where(window(lane, at + HALO, HALO), one_ref[f, CORE, :], value)
+    return roll(value, -turn(k))
 
 
 def first_bands_kernel(
     first_ref,
     second_ref,
-    west_ref,
-    east_ref,
-    depth_ref,
+    bands_ref,
+    record_0,
+    record_1,
+    record_2,
+    record_3,
+    wet_ref,
     inner_ref,
     out_ref,
     keep_ref,
@@ -443,30 +482,27 @@
     two_ref,
 ):
     tall_lane = lanes(TALL)
-    clear_pads(mask_ref, 2 * BANDS)
+    clear_pads(mask_ref, 2)
     before, after = sides(first_ref[:, COLS:], second_ref[:, COLS:], even_on("zon"))
-    depth = depth_ref[...]
-    blank = jnp.zeros((TALL, COLS), F32)
-    west, east = [blank] * BANDS, [blank] * BANDS
-    for j in range(LANES):
-        at = BAND * j
-        turned = roll(depth, turn(j))
-        low = jnp.where(window(tall_lane, at + HALO, HALO), roll(before, at + HALO), turned)
-        high = jnp.where(window(tall_lane, at + 2 * HALO, HALO), roll(after, at + 2 * HALO), turned)
-        for group in range(BANDS):
-            level = (group * LANES + j) % LEVELS
-            west[group] = jnp.where(
-                window(tall_lane, at + HALO, BAND), jnp.where(low > level, 1.0, 0.0), west[group]
-            )
-            east[group] = jnp.where(
-                window(tall_lane, at, BAND), jnp.where(high > level, 1.0, 0.0), east[group]
-            )
-    for group in range(BANDS):
-        mask_ref[group, BODY, :] = west[group]
-        mask_ref[BANDS + group, BODY, :] = east[group]
-    coefficients(mask_ref, 2 * BANDS, keep_ref, give_ref)
-    fill_bands(first_ref, second_ref, west_ref, east_ref, one_ref, mask_ref)
-    sweep_all(2 * BANDS, 2 * BANDS, keep_ref, give_ref, one_ref, two_ref)
+    west = east = jnp.zeros((TALL, COLS), F32)
+    for k in range(LEVELS):
+        at = BAND * k
+        wet = wet_ref[k, BODY, :]
+        low = jnp.where(roll(before, at + 1) > k, 1.0, 0.0)
+        high = jnp.where(roll(after, at + 1 + HALO) > k, 1.0, 0.0)
+        west = jnp.where(window(tall_lane, at + 1, HALO), low, west)
+        west = jnp.where(window(tall_lane, at + 1 + HALO, HALO + 1), wet, west)
+        east = jnp.where(window(tall_lane, at, HALO + 1), wet, east)
+        east = jnp.where(window(tall_lane, at + 1 + HALO, HALO), high, east)
+    mask_ref[0, BODY, :] = west
+    mask_ref[1, BODY, :] = east
+    inside = jnp.where(tall_lane % BAND == 0, 0.0, 1.0)
+    for side in range(2):
+        wet, total = neighbour_sum(mask_ref, side, PAD, TALL)
+        keep_ref[side, BODY, :] = inside * (wet * (1.0 - SMOOTHING * total))
+        give_ref[side, BODY, :] = inside * (SMOOTHING * wet)
+    fill_bands(first_ref, second_ref, bands_ref, one_ref, mask_ref)
+    sweep_bands(keep_ref, give_ref, one_ref, two_ref, (record_0, record_1, record_2, record_3))
     lane = lanes(ROWS)
     for plane in range(PLANES):
         out_ref[plane] = join_bands(one_ref, plane, inner_ref[plane], lane)
@@ -475,8 +511,11 @@
 def gradient_kernel(
     first_ref,
     second_ref,
-    west_ref,
-    east_ref,
+    bands_ref,
+    record_0,
+    record_1,
+    record_2,
+    record_3,
     inner_ref,
     keep_ref,
     give_ref,
@@ -485,8 +524,8 @@
     one_ref,
     two_ref,
 ):
-    fill_bands(first_ref, second_ref, west_ref, east_ref, one_ref, None)
-    sweep_all(2 * BANDS, 2 * BANDS, keep_ref, give_ref, one_ref, two_ref)
+    fill_bands(first_ref, second_ref, bands_ref, one_ref, None)
+    sweep_bands(keep_ref, give_ref, one_ref, two_ref, (record_0, record_1, record_2, record_3))
     lane = lanes(ROWS)
     for plane in range(PLANES):
         f, k = divmod(plane, LEVELS)
@@ -505,7 +544,9 @@
 def prepare_kernel(*refs):
     count_ref, model_ref, error_ref, bottom_ref, *observed_refs = refs[:8]
     corner_ref, weight_ref, value_ref, precision_ref = observed_refs
-    east_ref, west_ref, scale_ref, pick_ref, back_ref, lower_ref, upper_ref, want_ref = refs[8:]
+    east_ref, west_ref, copy_ref, scale_ref, pick_ref, back_ref = refs[8:14]
+    lower_ref, upper_ref, want_ref = refs[14:]
+    copy_ref[...] = model_ref[...]
     model_columns(model_ref, east_ref, west_ref)
     depth = bottom_ref[...]
     for plane in range(PLANES):
@@ -619,11 +660,13 @@
 
 FULL = ((PLANES, ROWS, COLS), F32)
 RAISED = ((PLANES, TALL, COLS), F32)
-SIDE = ((BANDS, TALL, COLS), F32)
+CUT = ((BANDS, TALL, COLS), F32)
+RECORD = ((SWEEPS, DEEP, COLS), F32)
 STEP = ((FIELDS, HALF, ROWS, COLS), F32)
 PART = ((PAIR, HALF, ROWS, COLS), F32)
 MASKS = ((LEVELS, DEEP, COLS), F32)
-STRIP = ((2 * BANDS, DEEP, COLS), F32)
+STRIP = ((BANDS, DEEP, COLS), F32)
+SIDES = ((2, DEEP, COLS), F32)
 
 
 def rows_of(count):
@@ -668,49 +711,50 @@
         obs_value,
         obs_precision,
     )
-    model_east, model_west, scale, *operators = call(
+    model_east, model_west, model, scale, *operators = call(
         prepare_kernel,
         [((ROWS, COLS), F32)] * 2
-        + [FULL]
+        + [STEP, FULL]
         + [((2 * slots, PLANES * ROWS), jnp.bfloat16), ((PLANES * ROWS, 2 * slots), jnp.bfloat16)]
         + [((slots, COLS), F32)] * 2
         + [((slots, 8), F32)],
         work=10**7,
     )(*inputs)
-    tall, depth, west, east, first, second = call(
+    turned, depth, first, second = call(
         first_columns_kernel,
-        [RAISED, ((TALL, COLS), F32), SIDE, SIDE, columns_of(2), columns_of(2)],
-        [long, long],
+        [RAISED, ((TALL, COLS), F32), columns_of(2), columns_of(2)],
+        [long, long, VMEM(*RAISED)],
     )(control, bottom_level, model_east, model_west, *mer)
     zon = exchange(first, second, "zon")
-    inner, keep_coef, give_coef, base = call(
+    deep = [VMEM((PLANES, DEEP, COLS), F32)] * 2
+    inner, bands, *record, wet, keep_coef, give_coef, base = call(
         first_interior_kernel,
-        [FULL, MASKS, MASKS, STEP],
-        [VMEM(*MASKS)]
-        + [VMEM((PLANES, DEEP, COLS), F32)] * 2
-        + [long, long, VMEM((ROWS + 16, COLS), F32)],
+        [FULL, CUT] + [RECORD] * BANDS + [MASKS, MASKS, MASKS, STEP],
+        deep + [long, long, VMEM((ROWS + 16, COLS), F32)],
         work=10**7,
-    )(tall, depth, model_state, *mer)
-    keep, send = call(background_kernel, [PART, PART])(model_state, depth, base, *zon)
+    )(turned, depth, model, *mer)
+    keep, send = call(background_kernel, [PART, PART])(model, depth, base, *zon)
     other = lax.ppermute(send, "grp", [(0, 1), (1, 0)])
     smoothed, keep_band, give_band = call(
-        first_bands_kernel, [FULL, STRIP, STRIP], [VMEM(*STRIP)] * 3, work=10**7
-    )(*zon, west, east, depth, inner)
+        first_bands_kernel, [FULL, SIDES, SIDES], [VMEM(*SIDES)] + [VMEM(*STRIP)] * 2, work=10**7
+    )(*zon, bands, *record, wet, inner)
     field, first, second = call(
         observe_kernel,
         [FULL, rows_of(SHORT), rows_of(SHORT)],
         [VMEM((PLANES * ROWS, COLS), F32), short, short],
     )(smoothed, scale, keep, other, *operators)
     mer = exchange(first, second, "mer")
-    tall, west, east, first, second = call(
-        next_columns_kernel, [RAISED, SIDE, SIDE, columns_of(1), columns_of(1)], [short, short]
+    turned, first, second = call(
+        next_columns_kernel,
+        [RAISED, columns_of(1), columns_of(1)],
+        [short, short, VMEM(*RAISED)],
     )(field, *mer)
     zon = exchange(first, second, "zon")
-    (inner,) = call(
-        next_interior_kernel, [FULL], [VMEM((PLANES, DEEP, COLS), F32)] * 2, work=10**7
-    )(tall, keep_coef, give_coef)
+    inner, bands, *record = call(
+        next_interior_kernel, [FULL, CUT] + [RECORD] * BANDS, deep, work=10**7
+    )(turned, keep_coef, give_coef)
     return call(gradient_kernel, [(control.shape, F32)], [VMEM(*STRIP)] * 2)(
-        *zon, west, east, inner, keep_band, give_band, control
+        *zon, bands, *record, inner, keep_band, give_band, control
     )[0]
 
 

time: 43.4 us -> 42.4 us (0.977)
  waiting for transfers between devices: 7.41 us -> 6.85 us
  Pallas kernels: 15.7 us -> 15.2 us
    ppermute x8, waiting for transfers between devices: 7.4 us -> 6.85 us  [swap(): return lax.ppermute(value, axis, pairs)]
    pallas_call x11, Pallas kernels: 15.7 us -> 15.2 us  [run(): pl.pallas_call(kernel, out_shape=[jax.ShapeDtypeStruct(shape, kind) for s...]
  transfers between devices with their start and end apart: 9 -> 9, of which waited for: 4 -> 4; matrix products, arithmetic and copies ran while one was open for 0% -> 0% of each run, Pallas kernels for 22% -> 23%
where the time goes in v5:
time: 42.4 us; the launch traced here: 42.2 us
  starting transfers between devices  19.2 us (45%)
  Pallas kernels  15.2 us (36%)
  waiting for transfers between devices  6.85 us (16%)
  between operations  0.85 us (2%)
    ppermute x8, starting transfers between devices, swap(): return lax.ppermute(value, axis, pairs)  16.1 us
    pallas_call x11, Pallas kernels, run(): pl.pallas_call(kernel, out_shape=[jax.ShapeDtypeStruct(shape, kind) for s...  15.2 us
    ppermute x8, waiting for transfers between devices, swap(): return lax.ppermute(value, axis, pairs)  6.85 us
    ppermute x1, starting transfers between devices, body(): other = lax.ppermute(send, 'grp', [(0, 1), (1, 0)])  3.18 us
  transfers between devices with their start and end apart: 9, of which 4 were waited for; matrix products, arithmetic and copies ran while one was open for 0% of the time, Pallas kernels for 23%

profile of v5, /device:TPU:1, one launch (start us, length us, event | category | flops | bytes accessed | tf_op | source)
XLA Modules:
  0.0 42.2 jit_solution(8347789197842724797)
XLA Ops:
  0.0 0.0 copy-start.1
  0.0 0.0 copy-start.3
  0.0 0.0 copy-start.2
  0.0 1.1 %rows.1 = (f32[160,128]{1,0:T(8,128)S(1)}, f32[160,128]{1,0:T(8,128)S(1)}) custom-call(f32[4,3,64,128]{3,2,1,0:T(8,128)} %model_ref.1, f32[2,6,64,128]{3,2,1,0:T(8,128)} %control_ref.5), custom_call_target="tpu_custom_call" | custom-call | tf_op jit(solution)/shard_map/rows/pallas_call | solution.py:628
  1.1 0.0 copy-done.3
  1.1 0.0 copy-start.6
  1.1 0.0 copy-start.7
  1.2 0.0 copy-start.4
  1.2 4.4 %collective-permute-start = (bf16[160,128]{1,0:T(8,128)(2,1)S(1)}, bf16[160,128]{1,0:T(8,128)(2,1)S(1)}, u32[]{:S(2)}, u32[]{:S(2)}) collective-permute-start(bf16[160,128]{1,0:T(8,128)(2,1)S(1)} %get-tuple-element.53), channel_id=1, source_target_pairs={{1,2},{2,1},{3,4},{4,3},{5,6},{6,5},{7,0},{0,7},{9,10},{10,9},{11,... | collective-permute-start | bytes 122888 | tf_op jit(solution)/shard_map/ppermute | solution.py:654
  5.6 0.0 copy-start.5
  5.6 0.0 collective-permute-start.1
  6.3 0.0 copy-done.1
  6.3 0.0 copy-done.2
  6.3 0.0 copy-done.6
  6.3 0.0 copy-done.7
  6.3 0.0 copy-done.4
  6.3 0.0 copy-done.5
  6.3 0.0 copy-start
  6.3 1.0 %prepare.1 = (f32[64,128]{1,0:T(8,128)S(1)}, f32[64,128]{1,0:T(8,128)S(1)}, f32[4,3,64,128]{3,2,1,0:T(8,128)S(1)}, f32[12,64,128]{2,1,0:T(8,128)S(1)}, bf16[512,...) custom-call(s32[1,1,1]{2,1,0:T(1,128)S(6)} %copy.10.refs_0_, ...), custom_call_target="tpu_custom_call" | custom-call | flops 10000000 | bytes 1000000 | tf_op jit(solution)/shard_map/prepare/pallas_call | solution.py:628
  7.3 0.0 collective-permute-done.a_ref
  7.4 1.1 %collective-permute-done.1.b_ref = bf16[160,128]{1,0:T(8,128)(2,1)S(1)} collective-permute-done((bf16[160,128]{1,0:T(8,128)(2,1)S(1)}, bf16[160,128]{1,0:T(8,128)(2,1)S(1)}, u32[]{:S(2)}, u32[]{:S(2)}) %collective-permute-start.1) | collective-permute-done | bytes 40992 | tf_op jit(solution)/shard_map/ppermute | solution.py:654
  8.4 0.0 copy-done
  8.4 0.3 first_columns.1
  8.8 8.4 %collective-permute-start.2 = (bf16[96,256]{1,0:T(8,128)(2,1)S(1)}, bf16[96,256]{1,0:T(8,128)(2,1)S(1)}, u32[]{:S(2)}, u32[]{:S(2)}) collective-permute-start(bf16[96,256]{1,0:T(8,128)(2,1)S(1)} %get-tuple-element.55), channel_id=1, source_target_pairs={{8,16},{16,8},{24,32},{32,24},{40,48},{48,40},{56,64},{64,56},{72,... | collective-permute-start | bytes 147464 | tf_op jit(solution)/shard_map/ppermute | solution.py:654
  17.2 0.0 collective-permute-start.3
  17.2 3.6 %first_interior.1 = (f32[12,64,128]{2,1,0:T(8,128)S(1)}, f32[4,96,128]{2,1,0:T(8,128)S(1)}, f32[10,112,128]{2,1,0:T(8,128)S(1)}, f32[10,112,128]{2,1,0:T(8,128)S...) custom-call(f32[12,96,128]{2,1,0:T(8,128)S(1)} %get-tuple-element.57, ...), custom_call_target="tpu_custom_call" | custom-call | flops 10000000 | bytes 1000000 | tf_op jit(solution)/shard_map/first_interior/pallas_call | solution.py:628
  20.8 0.0 collective-permute-done.2.first_ref
  20.8 0.8 %collective-permute-done.3.second_ref = bf16[96,256]{1,0:T(8,128)(2,1)S(1)} collective-permute-done((bf16[96,256]{1,0:T(8,128)(2,1)S(1)}, bf16[96,256]{1,0:T(8,128)(2,1)S(1)}, u32[]{:S(2)}, u32[]{:S(2)}) %collective-permute-start.3) | collective-permute-done | bytes 49184 | tf_op jit(solution)/shard_map/ppermute | solution.py:654
  21.7 0.3 background.1
  21.9 3.2 %collective-permute-start.4 = (f32[2,3,64,128]{3,2,1,0:T(8,128)S(1)}, f32[2,3,64,128]{3,2,1,0:T(8,128)S(1)}, u32[]{:S(2)}, u32[]{:S(2)}) collective-permute-start(f32[2,3,64,128]{3,2,1,0:T(8,128)S(1)} %get-tuple-element.71), channel_id=1, source_target_pairs={{0,128},{128,0},{1,129},{129,1},{2,130},{130,2},{3,131},{131,3},{4... | collective-permute-start | bytes 589832 | tf_op jit(solution)/shard_map/ppermute | solution.py:737
  25.1 1.7 %first_bands.1 = (f32[12,64,128]{2,1,0:T(8,128)S(1)}, f32[2,112,128]{2,1,0:T(8,128)S(1)}, f32[2,112,128]{2,1,0:T(8,128)S(1)}) custom-call(bf16[96,256]{1,0:T(8,128)(2,1)S(1)} %collective-permute-done.2.first_ref, bf16[96,256]{1,0:T(8,128)(2,1)S(1)} %collective-permute-done.3.second_ref, f32[4,96,128]{2,1,0:T(8,128)S(1)} %get-tuple-element.60.bands_ref, ...), custom_call_target="tpu_custom_call" | custom-call | flops 10000000 | bytes 1000000 | tf_op jit(solution)/shard_map/first_bands/pallas_call | solution.py:628
  26.8 0.0 collective-permute-done.4.other_ref
  26.8 1.4 %observe.1 = (f32[12,64,128]{2,1,0:T(8,128)S(1)}, bf16[128,128]{1,0:T(8,128)(2,1)S(1)}, bf16[128,128]{1,0:T(8,128)(2,1)S(1)}) custom-call(f32[12,64,128]{2,1,0:T(8,128)S(1)} %get-tuple-element.67.smooth_ref, f32[12,64,128]{2,1,0:T(8,128)S(1)} %get-tuple-element.68.scale_ref, f32[2,3,64,128]{3,2,1,0:T(8,128)S(1)} %get-tuple-element.70.keep_ref, ...), custom_call_target="tpu_custom_call" | custom-call | tf_op jit(solution)/shard_map/observe/pallas_call | solution.py:628
  28.2 1.3 %collective-permute-start.5 = (bf16[128,128]{1,0:T(8,128)(2,1)S(1)}, bf16[128,128]{1,0:T(8,128)(2,1)S(1)}, u32[]{:S(2)}, u32[]{:S(2)}) collective-permute-start(bf16[128,128]{1,0:T(8,128)(2,1)S(1)} %get-tuple-element.78), channel_id=1, source_target_pairs={{1,2},{2,1},{3,4},{4,3},{5,6},{6,5},{7,0},{0,7},{9,10},{10,9},{11,... | collective-permute-start | bytes 98312 | tf_op jit(solution)/shard_map/ppermute | solution.py:654
  29.5 0.0 collective-permute-start.6
  29.5 3.8 %collective-permute-done.5.a_ref = bf16[128,128]{1,0:T(8,128)(2,1)S(1)} collective-permute-done((bf16[128,128]{1,0:T(8,128)(2,1)S(1)}, bf16[128,128]{1,0:T(8,128)(2,1)S(1)}, u32[]{:S(2)}, u32[]{:S(2)}) %collective-permute-start.5) | collective-permute-done | bytes 32800 | tf_op jit(solution)/shard_map/ppermute | solution.py:654
  33.3 0.0 collective-permute-done.6.b_ref
  33.3 0.3 next_columns.1
  33.6 1.9 %collective-permute-start.7 = (bf16[96,128]{1,0:T(8,128)(2,1)S(1)}, bf16[96,128]{1,0:T(8,128)(2,1)S(1)}, u32[]{:S(2)}, u32[]{:S(2)}) collective-permute-start(bf16[96,128]{1,0:T(8,128)(2,1)S(1)} %get-tuple-element.80), channel_id=1, source_target_pairs={{8,16},{16,8},{24,32},{32,24},{40,48},{48,40},{56,64},{64,56},{72,... | collective-permute-start | bytes 73736 | tf_op jit(solution)/shard_map/ppermute | solution.py:654
  35.5 0.0 collective-permute-start.8
  35.5 3.3 %next_interior.1 = (f32[12,64,128]{2,1,0:T(8,128)S(1)}, f32[4,96,128]{2,1,0:T(8,128)S(1)}, f32[10,112,128]{2,1,0:T(8,128)S(1)}, f32[10,112,128]{2,1,0:T(8,128)S(...) custom-call(f32[12,96,128]{2,1,0:T(8,128)S(1)} %get-tuple-element.82.turned_ref, ...), custom_call_target="tpu_custom_call" | custom-call | flops 10000000 | bytes 1000000 | tf_op jit(solution)/shard_map/next_interior/pallas_call | solution.py:628
  38.8 1.2 %collective-permute-done.7.first_ref = bf16[96,128]{1,0:T(8,128)(2,1)S(1)} collective-permute-done((bf16[96,128]{1,0:T(8,128)(2,1)S(1)}, bf16[96,128]{1,0:T(8,128)(2,1)S(1)}, u32[]{:S(2)}, u32[]{:S(2)}) %collective-permute-start.7) | collective-permute-done | bytes 24608 | tf_op jit(solution)/shard_map/ppermute | solution.py:654
  40.0 0.0 collective-permute-done.8.second_ref
  40.0 2.2 %gradient.1 = f32[2,6,64,128]{3,2,1,0:T(8,128)} custom-call(bf16[96,128]{1,0:T(8,128)(2,1)S(1)} %collective-permute-done.7.first_ref, bf16[96,128]{1,0:T(8,128)(2,1)S(1)} %collective-permute-done.8.second_ref, f32[4,96,128]{2,1,0:T(8,128)S(1)} %get-tuple-element.85.bands_ref, f32[10,112,128]{2,1,0:T(8,128)S(1)} %get-tuple-element.86.record_0, ...), custom_call_target="tpu_custom_call" | custom-call | tf_op jit(solution)/shard_map/gradient/pallas_call | solution.py:628
  (1 shorter events, 0.0 us)
Async XLA Ops:
  0.0 6.3 %copy-start.1 = (f32[4,3,64,128]{3,2,1,0:T(8,128)S(1)}, f32[4,3,64,128]{3,2,1,0:T(8,128)}, u32[]{:S(2)}) copy-start(f32[4,3,64,128]{3,2,1,0:T(8,128)} %model_ref.1) | copy-start | bytes 1179652
  0.0 1.1 %copy-start.3 = (s32[64,128]{1,0:T(8,128)S(1)}, s32[64,128]{1,0:T(8,128)}, u32[]{:S(2)}) copy-start(s32[64,128]{1,0:T(8,128)} %bottom_ref.3) | copy-start | bytes 98308
  0.0 6.3 %copy-start.2 = (f32[2,6,64,128]{3,2,1,0:T(8,128)S(1)}, f32[2,6,64,128]{3,2,1,0:T(8,128)}, u32[]{:S(2)}) copy-start(f32[2,6,64,128]{3,2,1,0:T(8,128)} %refs_2_.1) | copy-start | bytes 1179652
  1.1 5.2 %copy-start.6 = (f32[1,1,1,256]{3,2,1,0:T(1,128)S(1)}, f32[1,1,1,256]{3,2,1,0:T(1,128)}, u32[]{:S(2)}) copy-start(f32[1,1,1,256]{3,2,1,0:T(1,128)} %refs_6_.1) | copy-start | bytes 3076
  1.1 5.2 %copy-start.7 = (f32[1,1,1,256]{3,2,1,0:T(1,128)S(1)}, f32[1,1,1,256]{3,2,1,0:T(1,128)}, u32[]{:S(2)}) copy-start(f32[1,1,1,256]{3,2,1,0:T(1,128)} %refs_7_.1) | copy-start | bytes 3076
  1.2 5.1 %copy-start.4 = (f32[1,1,1,4,256]{4,3,2,1,0:T(4,128)S(1)}, f32[1,1,1,4,256]{4,3,2,1,0:T(4,128)}, u32[]{:S(2)}) copy-start(f32[1,1,1,4,256]{4,3,2,1,0:T(4,128)} %refs_5_.1) | copy-start | bytes 12292
  1.2 6.2 %collective-permute-start = (bf16[160,128]{1,0:T(8,128)(2,1)S(1)}, bf16[160,128]{1,0:T(8,128)(2,1)S(1)}, u32[]{:S(2)}, u32[]{:S(2)}) collective-permute-start(bf16[160,128]{1,0:T(8,128)(2,1)S(1)} %get-tuple-element.53), channel_id=1, source_target_pairs={{1,2},{2,1},{3,4},{4,3},{5,6},{6,5},{7,0},{0,7},{9,10},{10,9},{11,... | collective-permute-start | bytes 122888 | tf_op jit(solution)/shard_map/ppermute | solution.py:654
  5.6 0.7 %copy-start.5 = (s32[1,1,1,256]{3,2,1,0:T(1,128)S(1)}, s32[1,1,1,256]{3,2,1,0:T(1,128)}, u32[]{:S(2)}) copy-start(s32[1,1,1,256]{3,2,1,0:T(1,128)} %refs_4_.1) | copy-start | bytes 3076
  5.6 2.9 %collective-permute-start.1 = (bf16[160,128]{1,0:T(8,128)(2,1)S(1)}, bf16[160,128]{1,0:T(8,128)(2,1)S(1)}, u32[]{:S(2)}, u32[]{:S(2)}) collective-permute-start(bf16[160,128]{1,0:T(8,128)(2,1)S(1)} %get-tuple-element.54), channel_id=1, source_target_pairs={{0,1},{1,0},{2,3},{3,2},{4,5},{5,4},{6,7},{7,6},{8,9},{9,8},{10,11... | collective-permute-start | bytes 122888 | tf_op jit(solution)/shard_map/ppermute | solution.py:654
  6.3 2.1 %copy-start = (f32[2,6,64,128]{3,2,1,0:T(8,128)S(1)}, f32[2,6,64,128]{3,2,1,0:T(8,128)}, u32[]{:S(2)}) copy-start(f32[2,6,64,128]{3,2,1,0:T(8,128)} %control_ref.5) | copy-start | bytes 1179652
  8.8 12.0 %collective-permute-start.2 = (bf16[96,256]{1,0:T(8,128)(2,1)S(1)}, bf16[96,256]{1,0:T(8,128)(2,1)S(1)}, u32[]{:S(2)}, u32[]{:S(2)}) collective-permute-start(bf16[96,256]{1,0:T(8,128)(2,1)S(1)} %get-tuple-element.55), channel_id=1, source_target_pairs={{8,16},{16,8},{24,32},{32,24},{40,48},{48,40},{56,64},{64,56},{72,... | collective-permute-start | bytes 147464 | tf_op jit(solution)/shard_map/ppermute | solution.py:654
  17.2 4.4 %collective-permute-start.3 = (bf16[96,256]{1,0:T(8,128)(2,1)S(1)}, bf16[96,256]{1,0:T(8,128)(2,1)S(1)}, u32[]{:S(2)}, u32[]{:S(2)}) collective-permute-start(bf16[96,256]{1,0:T(8,128)(2,1)S(1)} %get-tuple-element.56), channel_id=1, source_target_pairs={{0,8},{8,0},{16,24},{24,16},{32,40},{40,32},{48,56},{56,48},{64,72... | collective-permute-start | bytes 147464 | tf_op jit(solution)/shard_map/ppermute | solution.py:654
  21.9 4.9 %collective-permute-start.4 = (f32[2,3,64,128]{3,2,1,0:T(8,128)S(1)}, f32[2,3,64,128]{3,2,1,0:T(8,128)S(1)}, u32[]{:S(2)}, u32[]{:S(2)}) collective-permute-start(f32[2,3,64,128]{3,2,1,0:T(8,128)S(1)} %get-tuple-element.71), channel_id=1, source_target_pairs={{0,128},{128,0},{1,129},{129,1},{2,130},{130,2},{3,131},{131,3},{4... | collective-permute-start | bytes 589832 | tf_op jit(solution)/shard_map/ppermute | solution.py:737
  28.2 5.1 %collective-permute-start.5 = (bf16[128,128]{1,0:T(8,128)(2,1)S(1)}, bf16[128,128]{1,0:T(8,128)(2,1)S(1)}, u32[]{:S(2)}, u32[]{:S(2)}) collective-permute-start(bf16[128,128]{1,0:T(8,128)(2,1)S(1)} %get-tuple-element.78), channel_id=1, source_target_pairs={{1,2},{2,1},{3,4},{4,3},{5,6},{6,5},{7,0},{0,7},{9,10},{10,9},{11,... | collective-permute-start | bytes 98312 | tf_op jit(solution)/shard_map/ppermute | solution.py:654
  29.5 3.8 %collective-permute-start.6 = (bf16[128,128]{1,0:T(8,128)(2,1)S(1)}, bf16[128,128]{1,0:T(8,128)(2,1)S(1)}, u32[]{:S(2)}, u32[]{:S(2)}) collective-permute-start(bf16[128,128]{1,0:T(8,128)(2,1)S(1)} %get-tuple-element.79), channel_id=1, source_target_pairs={{0,1},{1,0},{2,3},{3,2},{4,5},{5,4},{6,7},{7,6},{8,9},{9,8},{10,11... | collective-permute-start | bytes 98312 | tf_op jit(solution)/shard_map/ppermute | solution.py:654
  33.6 6.4 %collective-permute-start.7 = (bf16[96,128]{1,0:T(8,128)(2,1)S(1)}, bf16[96,128]{1,0:T(8,128)(2,1)S(1)}, u32[]{:S(2)}, u32[]{:S(2)}) collective-permute-start(bf16[96,128]{1,0:T(8,128)(2,1)S(1)} %get-tuple-element.80), channel_id=1, source_target_pairs={{8,16},{16,8},{24,32},{32,24},{40,48},{48,40},{56,64},{64,56},{72,... | collective-permute-start | bytes 73736 | tf_op jit(solution)/shard_map/ppermute | solution.py:654
  35.5 4.5 %collective-permute-start.8 = (bf16[96,128]{1,0:T(8,128)(2,1)S(1)}, bf16[96,128]{1,0:T(8,128)(2,1)S(1)}, u32[]{:S(2)}, u32[]{:S(2)}) collective-permute-start(bf16[96,128]{1,0:T(8,128)(2,1)S(1)} %get-tuple-element.81), channel_id=1, source_target_pairs={{0,8},{8,0},{16,24},{24,16},{32,40},{40,32},{48,56},{56,48},{64,72... | collective-permute-start | bytes 73736 | tf_op jit(solution)/shard_map/ppermute | solution.py:654

commit v6 on v5

--- a/solution.py
+++ b/solution.py
@@ -185,8 +185,10 @@
     for f in range(PAIR):
         go_east = go_west = jnp.zeros((TALL, COLS), F32)
         for k in range(LEVELS):
-            turned = roll(tall_ref[f * LEVELS + k], turn(k))
-            turned_ref[f * LEVELS + k] = turned
+            turned = tall_ref[f * LEVELS + k]
+            if turned_ref is not None:
+                turned = roll(turned, turn(k))
+                turned_ref[f * LEVELS + k] = turned
             at = BAND * k
             go_east = jnp.where(window(lane, at + 1, HALO), turned, go_east)
             go_west = jnp.where(window(lane, at + 1 + HALO, HALO), turned, go_west)
@@ -238,10 +240,10 @@
 
 
 def next_columns_kernel(
-    field_ref, a_ref, b_ref, turned_ref, first_ref, second_ref, low_ref, high_ref, tall_ref
+    field_ref, a_ref, b_ref, turned_ref, first_ref, second_ref, low_ref, high_ref
 ):
-    raise_planes(lambda p: field_ref[p], a_ref, b_ref, low_ref, high_ref, tall_ref)
-    send_columns(0, *turn_planes(tall_ref, turned_ref), first_ref, second_ref)
+    raise_planes(lambda p: field_ref[p], a_ref, b_ref, low_ref, high_ref, turned_ref)
+    send_columns(0, *turn_planes(turned_ref, None), first_ref, second_ref)
 
 
 def base_step(model_ref, depth_ref, a_ref, b_ref, base_ref, low_ref, high_ref, tall_ref):
@@ -523,13 +525,25 @@
     out_ref,
     one_ref,
     two_ref,
+    whole_ref,
+    sems,
 ):
     fill_bands(first_ref, second_ref, bands_ref, one_ref, None)
     sweep_bands(keep_ref, give_ref, one_ref, two_ref, (record_0, record_1, record_2, record_3))
     lane = lanes(ROWS)
+    copies = []
     for plane in range(PLANES):
         f, k = divmod(plane, LEVELS)
-        out_ref[f, k] = control_ref[f, k] + join_bands(one_ref, plane, inner_ref[plane], lane)
+        whole_ref[f, k] = control_ref[f, k] + join_bands(one_ref, plane, inner_ref[plane], lane)
+        part, last = divmod(plane, 3)
+        if last == 2:
+            here = pl.ds(k - 2, 3)
+            copies.append(
+                pltpu.make_async_copy(whole_ref.at[f, here], out_ref.at[f, here], sems.at[part])
+            )
+            copies[-1].start()
+    for copy in copies:
+        copy.wait()
 
 
 def split(value):
@@ -544,14 +558,16 @@
 def prepare_kernel(*refs):
     count_ref, model_ref, error_ref, bottom_ref, *observed_refs = refs[:8]
     corner_ref, weight_ref, value_ref, precision_ref = observed_refs
-    east_ref, west_ref, copy_ref, scale_ref, pick_ref, back_ref = refs[8:14]
-    lower_ref, upper_ref, want_ref = refs[14:]
+    east_ref, west_ref, copy_ref, scale_ref, turned_ref, pick_ref, back_ref = refs[8:15]
+    lower_ref, upper_ref, lower_turned, upper_turned, value_out, gain_out = refs[15:]
     copy_ref[...] = model_ref[...]
     model_columns(model_ref, east_ref, west_ref)
     depth = bottom_ref[...]
     for plane in range(PLANES):
         f, k = divmod(plane, LEVELS)
-        scale_ref[plane] = jnp.where(depth > k, error_ref[f, k], 0.0)
+        scale = jnp.where(depth > k, error_ref[f, k], 0.0)
+        scale_ref[plane] = scale
+        turned_ref[plane] = roll(scale, turn(k))
     slots = corner_ref.shape[-1]
     cells = PLANES * ROWS
     corner = corner_ref[0, 0]
@@ -568,11 +584,19 @@
         pick_ref[here, :] = jnp.where(wide_row == tall[:, 6:7] + step, 1.0, 0.0).astype(jnp.bfloat16)
         back_ref[:, here] = jnp.where(tall_row == row + step, 1.0, 0.0).astype(jnp.bfloat16)
     lane = lanes(slots).astype(F32)
-    at, beside = lane == tall[:, 7:8], lane == tall[:, 7:8] + 1.0
-    lower_ref[...] = jnp.where(at, tall[:, 0:1], jnp.where(beside, tall[:, 1:2], 0.0))
-    upper_ref[...] = jnp.where(at, tall[:, 2:3], jnp.where(beside, tall[:, 3:4], 0.0))
-    live = lax.broadcasted_iota(jnp.int32, (slots, 8), 0) < count_ref[0]
-    want_ref[...] = jnp.where(live, tall, 0.0)
+    level = (tall[:, 6:7].astype(jnp.int32) // ROWS) % LEVELS
+    column_turned = (tall[:, 7:8].astype(jnp.int32) + turn(level)) % COLS
+    for left, low_out, high_out in (
+        (tall[:, 7:8].astype(jnp.int32), lower_ref, upper_ref),
+        (column_turned, lower_turned, upper_turned),
+    ):
+        at = lane == left.astype(F32)
+        beside = lane == ((left + 1) % COLS).astype(F32)
+        low_out[...] = jnp.where(at, tall[:, 0:1], jnp.where(beside, tall[:, 1:2], 0.0))
+        high_out[...] = jnp.where(at, tall[:, 2:3], jnp.where(beside, tall[:, 3:4], 0.0))
+    live = lax.broadcasted_iota(jnp.int32, (slots, COLS), 0) < count_ref[0]
+    value_out[...] = jnp.broadcast_to(tall[:, 4:5], (slots, COLS))
+    gain_out[...] = jnp.where(live, jnp.broadcast_to(tall[:, 5:6], (slots, COLS)), 0.0)
 
 
 def observe_kernel(
@@ -580,11 +604,15 @@
     scale_ref,
     keep_ref,
     other_ref,
+    turned_ref,
     pick_ref,
     back_ref,
     lower_ref,
     upper_ref,
-    want_ref,
+    lower_turned,
+    upper_turned,
+    value_ref,
+    gain_ref,
     field_ref,
     first_ref,
     second_ref,
@@ -593,7 +621,7 @@
     high_ref,
 ):
     group = lax.axis_index("grp")
-    slots = want_ref.shape[0]
+    slots = value_ref.shape[0]
     for plane in range(PLANES):
         f, k = divmod(plane, LEVELS)
         held = group == k // HALF
@@ -603,12 +631,14 @@
         )
     seen = join(jnp.dot(pick_ref[...], split(total_ref[...]), preferred_element_type=F32))
     lower, upper = lower_ref[...], upper_ref[...]
-    observed = jnp.sum(lower * seen[:slots] + upper * seen[slots:], axis=1, keepdims=True)
-    misfit = want_ref[:, 5:6] * (observed - want_ref[:, 4:5])
-    spread = jnp.concatenate([lower * misfit, upper * misfit], axis=0)
+    weighted = split(lower * seen[:slots] + upper * seen[slots:])
+    ones = jnp.ones((2 * COLS, COLS), jnp.bfloat16)
+    observed = jnp.dot(weighted, ones, preferred_element_type=F32)
+    misfit = gain_ref[...] * (observed - value_ref[...])
+    spread = jnp.concatenate([lower_turned[...] * misfit, upper_turned[...] * misfit], axis=0)
     total_ref[...] = join(jnp.dot(back_ref[...], split(spread), preferred_element_type=F32))
     for plane in range(PLANES):
-        field_ref[plane] = scale_ref[plane] * total_ref[plane * ROWS : (plane + 1) * ROWS, :]
+        field_ref[plane] = turned_ref[plane] * total_ref[plane * ROWS : (plane + 1) * ROWS, :]
     stage(
         low_ref,
         high_ref,
@@ -621,7 +651,7 @@
     send_rows(low_ref, high_ref, first_ref, second_ref)
 
 
-def call(kernel, outs, scratch=(), remote=0, work=0):
+def call(kernel, outs, scratch=(), remote=0, work=0, out_space=VMEM):
     space = pl.ANY if remote else VMEM
 
     def run(*args):
@@ -629,7 +659,7 @@
             kernel,
             out_shape=[jax.ShapeDtypeStruct(shape, kind) for shape, kind in outs],
             in_specs=[pl.BlockSpec(memory_space=space) for _ in args],
-            out_specs=[pl.BlockSpec(memory_space=VMEM) for _ in outs],
+            out_specs=[pl.BlockSpec(memory_space=out_space) for _ in outs],
             scratch_shapes=list(scratch),
             compiler_params=pltpu.CompilerParams(
                 vmem_limit_bytes=int((remote or GRANT) * 2**20)
@@ -714,10 +744,9 @@
     model_east, model_west, model, scale, *operators = call(
         prepare_kernel,
         [((ROWS, COLS), F32)] * 2
-        + [STEP, FULL]
+        + [STEP, FULL, FULL]
         + [((2 * slots, PLANES * ROWS), jnp.bfloat16), ((PLANES * ROWS, 2 * slots), jnp.bfloat16)]
-        + [((slots, COLS), F32)] * 2
-        + [((slots, 8), F32)],
+        + [((slots, COLS), F32)] * 6,
         work=10**7,
     )(*inputs)
     turned, depth, first, second = call(
@@ -747,13 +776,16 @@
     turned, first, second = call(
         next_columns_kernel,
         [RAISED, columns_of(1), columns_of(1)],
-        [short, short, VMEM(*RAISED)],
+        [short, short],
     )(field, *mer)
     zon = exchange(first, second, "zon")
     inner, bands, *record = call(
         next_interior_kernel, [FULL, CUT] + [RECORD] * BANDS, deep, work=10**7
     )(turned, keep_coef, give_coef)
-    return call(gradient_kernel, [(control.shape, F32)], [VMEM(*STRIP)] * 2)(
+    whole = [VMEM(control.shape, F32), dma((4,))]
+    return call(
+        gradient_kernel, [(control.shape, F32)], [VMEM(*STRIP)] * 2 + whole, out_space=pl.ANY
+    )(
         *zon, bands, *record, inner, keep_band, give_band, control
     )[0]
 

time: 42.4 us -> 42 us (level)
  transfers between devices with their start and end apart: 9 -> 9, of which waited for: 4 -> 4; matrix products, arithmetic and copies ran while one was open for 0% -> 0% of each run, Pallas kernels for 23% -> 24%
where the time goes in v6:
time: 42 us; the launch traced here: 41.9 us
  starting transfers between devices  19.2 us (46%)
  Pallas kernels  15.2 us (36%)
  waiting for transfers between devices  6.61 us (16%)
  between operations  0.84 us (2%)
    ppermute x8, starting transfers between devices, swap(): return lax.ppermute(value, axis, pairs)  16 us
    pallas_call x11, Pallas kernels, run(): pl.pallas_call(kernel, out_shape=[jax.ShapeDtypeStruct(shape, kind) for s...  15.2 us
    ppermute x8, waiting for transfers between devices, swap(): return lax.ppermute(value, axis, pairs)  6.61 us
    ppermute x1, starting transfers between devices, body(): other = lax.ppermute(send, 'grp', [(0, 1), (1, 0)])  3.18 us
  transfers between devices with their start and end apart: 9, of which 4 were waited for; matrix products, arithmetic and copies ran while one was open for 0% of the time, Pallas kernels for 24%

profile of v6, /device:TPU:1, one launch (start us, length us, event | category | flops | bytes accessed | tf_op | source)
XLA Modules:
  0.0 41.9 jit_solution(9487089864631071371)
XLA Ops:
  0.0 0.0 copy-start.1
  0.0 0.0 copy-start.3
  0.0 0.0 copy-start.2
  0.0 1.1 %rows.1 = (f32[160,128]{1,0:T(8,128)S(1)}, f32[160,128]{1,0:T(8,128)S(1)}) custom-call(f32[4,3,64,128]{3,2,1,0:T(8,128)} %model_ref.1, f32[2,6,64,128]{3,2,1,0:T(8,128)} %control_ref.5), custom_call_target="tpu_custom_call" | custom-call | tf_op jit(solution)/shard_map/rows/pallas_call | solution.py:658
  1.1 0.0 copy-done.3
  1.1 0.0 copy-start.6
  1.1 0.0 copy-start.7
  1.2 0.0 copy-start.4
  1.2 4.4 %collective-permute-start = (bf16[160,128]{1,0:T(8,128)(2,1)S(1)}, bf16[160,128]{1,0:T(8,128)(2,1)S(1)}, u32[]{:S(2)}, u32[]{:S(2)}) collective-permute-start(bf16[160,128]{1,0:T(8,128)(2,1)S(1)} %get-tuple-element.57), channel_id=1, source_target_pairs={{1,2},{2,1},{3,4},{4,3},{5,6},{6,5},{7,0},{0,7},{9,10},{10,9},{11,... | collective-permute-start | bytes 122888 | tf_op jit(solution)/shard_map/ppermute | solution.py:684
  5.6 0.0 copy-start.5
  5.6 0.0 collective-permute-start.1
  6.3 0.0 copy-done.1
  6.3 0.0 copy-done.2
  6.3 0.0 copy-done.6
  6.3 0.0 copy-done.7
  6.3 0.0 copy-done.4
  6.3 0.0 copy-done.5
  6.3 0.0 copy-start
  6.3 1.3 %prepare.1 = (f32[64,128]{1,0:T(8,128)S(1)}, f32[64,128]{1,0:T(8,128)S(1)}, f32[4,3,64,128]{3,2,1,0:T(8,128)S(1)}, f32[12,64,128]{2,1,0:T(8,128)S(1)}, f32[12,64...) custom-call(s32[1,1,1]{2,1,0:T(1,128)S(6)} %copy.10.refs_0_, ...), custom_call_target="tpu_custom_call" | custom-call | flops 10000000 | bytes 1000000 | tf_op jit(solution)/shard_map/prepare/pallas_call | solution.py:658
  7.6 0.0 collective-permute-done.a_ref
  7.6 0.8 %collective-permute-done.1.b_ref = bf16[160,128]{1,0:T(8,128)(2,1)S(1)} collective-permute-done((bf16[160,128]{1,0:T(8,128)(2,1)S(1)}, bf16[160,128]{1,0:T(8,128)(2,1)S(1)}, u32[]{:S(2)}, u32[]{:S(2)}) %collective-permute-start.1) | collective-permute-done | bytes 40992 | tf_op jit(solution)/shard_map/ppermute | solution.py:684
  8.4 0.0 copy-done
  8.4 0.3 first_columns.1
  8.8 8.4 %collective-permute-start.2 = (bf16[96,256]{1,0:T(8,128)(2,1)S(1)}, bf16[96,256]{1,0:T(8,128)(2,1)S(1)}, u32[]{:S(2)}, u32[]{:S(2)}) collective-permute-start(bf16[96,256]{1,0:T(8,128)(2,1)S(1)} %get-tuple-element.59), channel_id=1, source_target_pairs={{8,16},{16,8},{24,32},{32,24},{40,48},{48,40},{56,64},{64,56},{72,... | collective-permute-start | bytes 147464 | tf_op jit(solution)/shard_map/ppermute | solution.py:684
  17.2 0.0 collective-permute-start.3
  17.2 3.6 %first_interior.1 = (f32[12,64,128]{2,1,0:T(8,128)S(1)}, f32[4,96,128]{2,1,0:T(8,128)S(1)}, f32[10,112,128]{2,1,0:T(8,128)S(1)}, f32[10,112,128]{2,1,0:T(8,128)S...) custom-call(f32[12,96,128]{2,1,0:T(8,128)S(1)} %get-tuple-element.61, ...), custom_call_target="tpu_custom_call" | custom-call | flops 10000000 | bytes 1000000 | tf_op jit(solution)/shard_map/first_interior/pallas_call | solution.py:658
  20.8 0.0 collective-permute-done.2.first_ref
  20.8 0.8 %collective-permute-done.3.second_ref = bf16[96,256]{1,0:T(8,128)(2,1)S(1)} collective-permute-done((bf16[96,256]{1,0:T(8,128)(2,1)S(1)}, bf16[96,256]{1,0:T(8,128)(2,1)S(1)}, u32[]{:S(2)}, u32[]{:S(2)}) %collective-permute-start.3) | collective-permute-done | bytes 49184 | tf_op jit(solution)/shard_map/ppermute | solution.py:684
  21.7 0.3 background.1
  21.9 3.2 %collective-permute-start.4 = (f32[2,3,64,128]{3,2,1,0:T(8,128)S(1)}, f32[2,3,64,128]{3,2,1,0:T(8,128)S(1)}, u32[]{:S(2)}, u32[]{:S(2)}) collective-permute-start(f32[2,3,64,128]{3,2,1,0:T(8,128)S(1)} %get-tuple-element.75), channel_id=1, source_target_pairs={{0,128},{128,0},{1,129},{129,1},{2,130},{130,2},{3,131},{131,3},{4... | collective-permute-start | bytes 589832 | tf_op jit(solution)/shard_map/ppermute | solution.py:766
  25.1 1.7 %first_bands.1 = (f32[12,64,128]{2,1,0:T(8,128)S(1)}, f32[2,112,128]{2,1,0:T(8,128)S(1)}, f32[2,112,128]{2,1,0:T(8,128)S(1)}) custom-call(bf16[96,256]{1,0:T(8,128)(2,1)S(1)} %collective-permute-done.2.first_ref, bf16[96,256]{1,0:T(8,128)(2,1)S(1)} %collective-permute-done.3.second_ref, f32[4,96,128]{2,1,0:T(8,128)S(1)} %get-tuple-element.64.bands_ref, ...), custom_call_target="tpu_custom_call" | custom-call | flops 10000000 | bytes 1000000 | tf_op jit(solution)/shard_map/first_bands/pallas_call | solution.py:658
  26.8 0.0 collective-permute-done.4.other_ref
  26.8 1.3 %observe.1 = (f32[12,64,128]{2,1,0:T(8,128)S(1)}, bf16[128,128]{1,0:T(8,128)(2,1)S(1)}, bf16[128,128]{1,0:T(8,128)(2,1)S(1)}) custom-call(f32[12,64,128]{2,1,0:T(8,128)S(1)} %get-tuple-element.71.smooth_ref, f32[12,64,128]{2,1,0:T(8,128)S(1)} %get-tuple-element.72.scale_ref, f32[2,3,64,128]{3,2,1,0:T(8,128)S(1)} %get-tuple-element.74.keep_ref, ...), custom_call_target="tpu_custom_call" | custom-call | tf_op jit(solution)/shard_map/observe/pallas_call | solution.py:658
  28.1 1.3 %collective-permute-start.5 = (bf16[128,128]{1,0:T(8,128)(2,1)S(1)}, bf16[128,128]{1,0:T(8,128)(2,1)S(1)}, u32[]{:S(2)}, u32[]{:S(2)}) collective-permute-start(bf16[128,128]{1,0:T(8,128)(2,1)S(1)} %get-tuple-element.86), channel_id=1, source_target_pairs={{1,2},{2,1},{3,4},{4,3},{5,6},{6,5},{7,0},{0,7},{9,10},{10,9},{11,... | collective-permute-start | bytes 98312 | tf_op jit(solution)/shard_map/ppermute | solution.py:684
  29.4 0.0 collective-permute-start.6
  29.4 3.8 %collective-permute-done.5.a_ref = bf16[128,128]{1,0:T(8,128)(2,1)S(1)} collective-permute-done((bf16[128,128]{1,0:T(8,128)(2,1)S(1)}, bf16[128,128]{1,0:T(8,128)(2,1)S(1)}, u32[]{:S(2)}, u32[]{:S(2)}) %collective-permute-start.5) | collective-permute-done | bytes 32800 | tf_op jit(solution)/shard_map/ppermute | solution.py:684
  33.2 0.0 collective-permute-done.6.b_ref
  33.2 0.1 next_columns.1
  33.3 1.9 %collective-permute-start.7 = (bf16[96,128]{1,0:T(8,128)(2,1)S(1)}, bf16[96,128]{1,0:T(8,128)(2,1)S(1)}, u32[]{:S(2)}, u32[]{:S(2)}) collective-permute-start(bf16[96,128]{1,0:T(8,128)(2,1)S(1)} %get-tuple-element.88), channel_id=1, source_target_pairs={{8,16},{16,8},{24,32},{32,24},{40,48},{48,40},{56,64},{64,56},{72,... | collective-permute-start | bytes 73736 | tf_op jit(solution)/shard_map/ppermute | solution.py:684
  35.2 0.0 collective-permute-start.8
  35.2 3.3 %next_interior.1 = (f32[12,64,128]{2,1,0:T(8,128)S(1)}, f32[4,96,128]{2,1,0:T(8,128)S(1)}, f32[10,112,128]{2,1,0:T(8,128)S(1)}, f32[10,112,128]{2,1,0:T(8,128)S(...) custom-call(f32[12,96,128]{2,1,0:T(8,128)S(1)} %get-tuple-element.90.turned_ref, ...), custom_call_target="tpu_custom_call" | custom-call | flops 10000000 | bytes 1000000 | tf_op jit(solution)/shard_map/next_interior/pallas_call | solution.py:658
  38.5 1.2 %collective-permute-done.7.first_ref = bf16[96,128]{1,0:T(8,128)(2,1)S(1)} collective-permute-done((bf16[96,128]{1,0:T(8,128)(2,1)S(1)}, bf16[96,128]{1,0:T(8,128)(2,1)S(1)}, u32[]{:S(2)}, u32[]{:S(2)}) %collective-permute-start.7) | collective-permute-done | bytes 24608 | tf_op jit(solution)/shard_map/ppermute | solution.py:684
  39.7 0.0 collective-permute-done.8.second_ref
  39.7 2.2 %gradient.1 = f32[2,6,64,128]{3,2,1,0:T(8,128)} custom-call(bf16[96,128]{1,0:T(8,128)(2,1)S(1)} %collective-permute-done.7.first_ref, bf16[96,128]{1,0:T(8,128)(2,1)S(1)} %collective-permute-done.8.second_ref, f32[4,96,128]{2,1,0:T(8,128)S(1)} %get-tuple-element.93.bands_ref, f32[10,112,128]{2,1,0:T(8,128)S(1)} %get-tuple-element.94.record_0, ...), custom_call_target="tpu_custom_call" | custom-call | tf_op jit(solution)/shard_map/gradient/pallas_call | solution.py:658
  (1 shorter events, 0.0 us)
Async XLA Ops:
  0.0 6.3 %copy-start.1 = (f32[4,3,64,128]{3,2,1,0:T(8,128)S(1)}, f32[4,3,64,128]{3,2,1,0:T(8,128)}, u32[]{:S(2)}) copy-start(f32[4,3,64,128]{3,2,1,0:T(8,128)} %model_ref.1) | copy-start | bytes 1179652
  0.0 1.1 %copy-start.3 = (s32[64,128]{1,0:T(8,128)S(1)}, s32[64,128]{1,0:T(8,128)}, u32[]{:S(2)}) copy-start(s32[64,128]{1,0:T(8,128)} %bottom_ref.3) | copy-start | bytes 98308
  0.0 6.3 %copy-start.2 = (f32[2,6,64,128]{3,2,1,0:T(8,128)S(1)}, f32[2,6,64,128]{3,2,1,0:T(8,128)}, u32[]{:S(2)}) copy-start(f32[2,6,64,128]{3,2,1,0:T(8,128)} %refs_2_.1) | copy-start | bytes 1179652
  1.1 5.2 %copy-start.6 = (f32[1,1,1,256]{3,2,1,0:T(1,128)S(1)}, f32[1,1,1,256]{3,2,1,0:T(1,128)}, u32[]{:S(2)}) copy-start(f32[1,1,1,256]{3,2,1,0:T(1,128)} %refs_6_.1) | copy-start | bytes 3076
  1.1 5.2 %copy-start.7 = (f32[1,1,1,256]{3,2,1,0:T(1,128)S(1)}, f32[1,1,1,256]{3,2,1,0:T(1,128)}, u32[]{:S(2)}) copy-start(f32[1,1,1,256]{3,2,1,0:T(1,128)} %refs_7_.1) | copy-start | bytes 3076
  1.2 5.1 %copy-start.4 = (f32[1,1,1,4,256]{4,3,2,1,0:T(4,128)S(1)}, f32[1,1,1,4,256]{4,3,2,1,0:T(4,128)}, u32[]{:S(2)}) copy-start(f32[1,1,1,4,256]{4,3,2,1,0:T(4,128)} %refs_5_.1) | copy-start | bytes 12292
  1.2 6.4 %collective-permute-start = (bf16[160,128]{1,0:T(8,128)(2,1)S(1)}, bf16[160,128]{1,0:T(8,128)(2,1)S(1)}, u32[]{:S(2)}, u32[]{:S(2)}) collective-permute-start(bf16[160,128]{1,0:T(8,128)(2,1)S(1)} %get-tuple-element.57), channel_id=1, source_target_pairs={{1,2},{2,1},{3,4},{4,3},{5,6},{6,5},{7,0},{0,7},{9,10},{10,9},{11,... | collective-permute-start | bytes 122888 | tf_op jit(solution)/shard_map/ppermute | solution.py:684
  5.6 0.7 %copy-start.5 = (s32[1,1,1,256]{3,2,1,0:T(1,128)S(1)}, s32[1,1,1,256]{3,2,1,0:T(1,128)}, u32[]{:S(2)}) copy-start(s32[1,1,1,256]{3,2,1,0:T(1,128)} %refs_4_.1) | copy-start | bytes 3076
  5.6 2.9 %collective-permute-start.1 = (bf16[160,128]{1,0:T(8,128)(2,1)S(1)}, bf16[160,128]{1,0:T(8,128)(2,1)S(1)}, u32[]{:S(2)}, u32[]{:S(2)}) collective-permute-start(bf16[160,128]{1,0:T(8,128)(2,1)S(1)} %get-tuple-element.58), channel_id=1, source_target_pairs={{0,1},{1,0},{2,3},{3,2},{4,5},{5,4},{6,7},{7,6},{8,9},{9,8},{10,11... | collective-permute-start | bytes 122888 | tf_op jit(solution)/shard_map/ppermute | solution.py:684
  6.3 2.1 %copy-start = (f32[2,6,64,128]{3,2,1,0:T(8,128)S(1)}, f32[2,6,64,128]{3,2,1,0:T(8,128)}, u32[]{:S(2)}) copy-start(f32[2,6,64,128]{3,2,1,0:T(8,128)} %control_ref.5) | copy-start | bytes 1179652
  8.8 12.0 %collective-permute-start.2 = (bf16[96,256]{1,0:T(8,128)(2,1)S(1)}, bf16[96,256]{1,0:T(8,128)(2,1)S(1)}, u32[]{:S(2)}, u32[]{:S(2)}) collective-permute-start(bf16[96,256]{1,0:T(8,128)(2,1)S(1)} %get-tuple-element.59), channel_id=1, source_target_pairs={{8,16},{16,8},{24,32},{32,24},{40,48},{48,40},{56,64},{64,56},{72,... | collective-permute-start | bytes 147464 | tf_op jit(solution)/shard_map/ppermute | solution.py:684
  17.2 4.4 %collective-permute-start.3 = (bf16[96,256]{1,0:T(8,128)(2,1)S(1)}, bf16[96,256]{1,0:T(8,128)(2,1)S(1)}, u32[]{:S(2)}, u32[]{:S(2)}) collective-permute-start(bf16[96,256]{1,0:T(8,128)(2,1)S(1)} %get-tuple-element.60), channel_id=1, source_target_pairs={{0,8},{8,0},{16,24},{24,16},{32,40},{40,32},{48,56},{56,48},{64,72... | collective-permute-start | bytes 147464 | tf_op jit(solution)/shard_map/ppermute | solution.py:684
  21.9 4.9 %collective-permute-start.4 = (f32[2,3,64,128]{3,2,1,0:T(8,128)S(1)}, f32[2,3,64,128]{3,2,1,0:T(8,128)S(1)}, u32[]{:S(2)}, u32[]{:S(2)}) collective-permute-start(f32[2,3,64,128]{3,2,1,0:T(8,128)S(1)} %get-tuple-element.75), channel_id=1, source_target_pairs={{0,128},{128,0},{1,129},{129,1},{2,130},{130,2},{3,131},{131,3},{4... | collective-permute-start | bytes 589832 | tf_op jit(solution)/shard_map/ppermute | solution.py:766
  28.1 5.1 %collective-permute-start.5 = (bf16[128,128]{1,0:T(8,128)(2,1)S(1)}, bf16[128,128]{1,0:T(8,128)(2,1)S(1)}, u32[]{:S(2)}, u32[]{:S(2)}) collective-permute-start(bf16[128,128]{1,0:T(8,128)(2,1)S(1)} %get-tuple-element.86), channel_id=1, source_target_pairs={{1,2},{2,1},{3,4},{4,3},{5,6},{6,5},{7,0},{0,7},{9,10},{10,9},{11,... | collective-permute-start | bytes 98312 | tf_op jit(solution)/shard_map/ppermute | solution.py:684
  29.4 3.8 %collective-permute-start.6 = (bf16[128,128]{1,0:T(8,128)(2,1)S(1)}, bf16[128,128]{1,0:T(8,128)(2,1)S(1)}, u32[]{:S(2)}, u32[]{:S(2)}) collective-permute-start(bf16[128,128]{1,0:T(8,128)(2,1)S(1)} %get-tuple-element.87), channel_id=1, source_target_pairs={{0,1},{1,0},{2,3},{3,2},{4,5},{5,4},{6,7},{7,6},{8,9},{9,8},{10,11... | collective-permute-start | bytes 98312 | tf_op jit(solution)/shard_map/ppermute | solution.py:684
  33.3 6.4 %collective-permute-start.7 = (bf16[96,128]{1,0:T(8,128)(2,1)S(1)}, bf16[96,128]{1,0:T(8,128)(2,1)S(1)}, u32[]{:S(2)}, u32[]{:S(2)}) collective-permute-start(bf16[96,128]{1,0:T(8,128)(2,1)S(1)} %get-tuple-element.88), channel_id=1, source_target_pairs={{8,16},{16,8},{24,32},{32,24},{40,48},{48,40},{56,64},{64,56},{72,... | collective-permute-start | bytes 73736 | tf_op jit(solution)/shard_map/ppermute | solution.py:684
  35.2 4.5 %collective-permute-start.8 = (bf16[96,128]{1,0:T(8,128)(2,1)S(1)}, bf16[96,128]{1,0:T(8,128)(2,1)S(1)}, u32[]{:S(2)}, u32[]{:S(2)}) collective-permute-start(bf16[96,128]{1,0:T(8,128)(2,1)S(1)} %get-tuple-element.89), channel_id=1, source_target_pairs={{0,8},{8,0},{16,24},{24,16},{32,40},{40,32},{48,56},{56,48},{64,72... | collective-permute-start | bytes 73736 | tf_op jit(solution)/shard_map/ppermute | solution.py:684

commit v7 on v6

--- a/solution.py
+++ b/solution.py
@@ -334,7 +334,9 @@
         sweep(2 * step + 3, 1, 2 * PAD, TALL - 2 * PAD)
         return carry
 
-    lax.fori_loop(0, SWEEPS // 2 - 1, pair, 0)
+    lax.fori_loop(0, SWEEPS // 2 - 2, pair, 0)
+    sweep(SWEEPS - 2, 0, 2 * PAD, TALL - 2 * PAD)
+    sweep(SWEEPS - 1, 1, PAD + EDGE, ROWS)
 
 
 def sweep_planes(keep_ref, give_ref, one_ref, two_ref, record_refs):

time: 42 us -> 42.1 us (level)
  transfers between devices with their start and end apart: 9 -> 9, of which waited for: 4 -> 4; matrix products, arithmetic and copies ran while one was open for 0% -> 0% of each run, Pallas kernels for 24% -> 23%
where the time goes in v7:
time: 42.1 us; the launch traced here: 42 us
  starting transfers between devices  19.2 us (46%)
  Pallas kernels  14.9 us (35%)
  waiting for transfers between devices  6.78 us (16%)
  between operations  1 us (2%)
    ppermute x8, starting transfers between devices, swap(): return lax.ppermute(value, axis, pairs)  16 us
    pallas_call x11, Pallas kernels, run(): pl.pallas_call(kernel, out_shape=[jax.ShapeDtypeStruct(shape, kind) for s...  14.9 us
    ppermute x8, waiting for transfers between devices, swap(): return lax.ppermute(value, axis, pairs)  6.78 us
    ppermute x1, starting transfers between devices, body(): other = lax.ppermute(send, 'grp', [(0, 1), (1, 0)])  3.18 us
  transfers between devices with their start and end apart: 9, of which 4 were waited for; matrix products, arithmetic and copies ran while one was open for 0% of the time, Pallas kernels for 23%

profile of v7, /device:TPU:1, one launch (start us, length us, event | category | flops | bytes accessed | tf_op | source)
XLA Modules:
  0.0 42.0 jit_solution(15668977497249731557)
XLA Ops:
  0.0 0.0 copy-start.1
  0.0 0.0 copy-start.3
  0.0 0.0 copy-start.2
  0.0 1.1 %rows.1 = (f32[160,128]{1,0:T(8,128)S(1)}, f32[160,128]{1,0:T(8,128)S(1)}) custom-call(f32[4,3,64,128]{3,2,1,0:T(8,128)} %model_ref.1, f32[2,6,64,128]{3,2,1,0:T(8,128)} %control_ref.5), custom_call_target="tpu_custom_call" | custom-call | tf_op jit(solution)/shard_map/rows/pallas_call | solution.py:660
  1.1 0.0 copy-done.3
  1.1 0.0 copy-start.6
  1.1 0.0 copy-start.7
  1.2 0.0 copy-start.4
  1.2 4.4 %collective-permute-start = (bf16[160,128]{1,0:T(8,128)(2,1)S(1)}, bf16[160,128]{1,0:T(8,128)(2,1)S(1)}, u32[]{:S(2)}, u32[]{:S(2)}) collective-permute-start(bf16[160,128]{1,0:T(8,128)(2,1)S(1)} %get-tuple-element.57), channel_id=1, source_target_pairs={{1,2},{2,1},{3,4},{4,3},{5,6},{6,5},{7,0},{0,7},{9,10},{10,9},{11,... | collective-permute-start | bytes 122888 | tf_op jit(solution)/shard_map/ppermute | solution.py:686
  5.6 0.0 copy-start.5
  5.6 0.0 collective-permute-start.1
  6.3 0.0 copy-done.1
  6.3 0.0 copy-done.2
  6.3 0.0 copy-done.6
  6.3 0.0 copy-done.7
  6.3 0.0 copy-done.4
  6.3 0.0 copy-done.5
  6.3 0.0 copy-start
  6.3 1.3 %prepare.1 = (f32[64,128]{1,0:T(8,128)S(1)}, f32[64,128]{1,0:T(8,128)S(1)}, f32[4,3,64,128]{3,2,1,0:T(8,128)S(1)}, f32[12,64,128]{2,1,0:T(8,128)S(1)}, f32[12,64...) custom-call(s32[1,1,1]{2,1,0:T(1,128)S(6)} %copy.10.refs_0_, ...), custom_call_target="tpu_custom_call" | custom-call | flops 10000000 | bytes 1000000 | tf_op jit(solution)/shard_map/prepare/pallas_call | solution.py:660
  7.6 0.0 collective-permute-done.a_ref
  7.6 0.8 %collective-permute-done.1.b_ref = bf16[160,128]{1,0:T(8,128)(2,1)S(1)} collective-permute-done((bf16[160,128]{1,0:T(8,128)(2,1)S(1)}, bf16[160,128]{1,0:T(8,128)(2,1)S(1)}, u32[]{:S(2)}, u32[]{:S(2)}) %collective-permute-start.1) | collective-permute-done | bytes 40992 | tf_op jit(solution)/shard_map/ppermute | solution.py:686
  8.4 0.0 copy-done
  8.4 0.3 first_columns.1
  8.8 8.4 %collective-permute-start.2 = (bf16[96,256]{1,0:T(8,128)(2,1)S(1)}, bf16[96,256]{1,0:T(8,128)(2,1)S(1)}, u32[]{:S(2)}, u32[]{:S(2)}) collective-permute-start(bf16[96,256]{1,0:T(8,128)(2,1)S(1)} %get-tuple-element.59), channel_id=1, source_target_pairs={{8,16},{16,8},{24,32},{32,24},{40,48},{48,40},{56,64},{64,56},{72,... | collective-permute-start | bytes 147464 | tf_op jit(solution)/shard_map/ppermute | solution.py:686
  17.2 0.0 collective-permute-start.3
  17.2 3.5 %first_interior.1 = (f32[12,64,128]{2,1,0:T(8,128)S(1)}, f32[4,96,128]{2,1,0:T(8,128)S(1)}, f32[10,112,128]{2,1,0:T(8,128)S(1)}, f32[10,112,128]{2,1,0:T(8,128)S...) custom-call(f32[12,96,128]{2,1,0:T(8,128)S(1)} %get-tuple-element.61, ...), custom_call_target="tpu_custom_call" | custom-call | flops 10000000 | bytes 1000000 | tf_op jit(solution)/shard_map/first_interior/pallas_call | solution.py:660
  20.7 0.0 collective-permute-done.2.first_ref
  20.7 0.9 %collective-permute-done.3.second_ref = bf16[96,256]{1,0:T(8,128)(2,1)S(1)} collective-permute-done((bf16[96,256]{1,0:T(8,128)(2,1)S(1)}, bf16[96,256]{1,0:T(8,128)(2,1)S(1)}, u32[]{:S(2)}, u32[]{:S(2)}) %collective-permute-start.3) | collective-permute-done | bytes 49184 | tf_op jit(solution)/shard_map/ppermute | solution.py:686
  21.7 0.3 background.1
  21.9 3.2 %collective-permute-start.4 = (f32[2,3,64,128]{3,2,1,0:T(8,128)S(1)}, f32[2,3,64,128]{3,2,1,0:T(8,128)S(1)}, u32[]{:S(2)}, u32[]{:S(2)}) collective-permute-start(f32[2,3,64,128]{3,2,1,0:T(8,128)S(1)} %get-tuple-element.75), channel_id=1, source_target_pairs={{0,128},{128,0},{1,129},{129,1},{2,130},{130,2},{3,131},{131,3},{4... | collective-permute-start | bytes 589832 | tf_op jit(solution)/shard_map/ppermute | solution.py:768
  25.1 1.7 %first_bands.1 = (f32[12,64,128]{2,1,0:T(8,128)S(1)}, f32[2,112,128]{2,1,0:T(8,128)S(1)}, f32[2,112,128]{2,1,0:T(8,128)S(1)}) custom-call(bf16[96,256]{1,0:T(8,128)(2,1)S(1)} %collective-permute-done.2.first_ref, bf16[96,256]{1,0:T(8,128)(2,1)S(1)} %collective-permute-done.3.second_ref, f32[4,96,128]{2,1,0:T(8,128)S(1)} %get-tuple-element.64.bands_ref, ...), custom_call_target="tpu_custom_call" | custom-call | flops 10000000 | bytes 1000000 | tf_op jit(solution)/shard_map/first_bands/pallas_call | solution.py:660
  26.8 0.0 collective-permute-done.4.other_ref
  26.8 1.3 %observe.1 = (f32[12,64,128]{2,1,0:T(8,128)S(1)}, bf16[128,128]{1,0:T(8,128)(2,1)S(1)}, bf16[128,128]{1,0:T(8,128)(2,1)S(1)}) custom-call(f32[12,64,128]{2,1,0:T(8,128)S(1)} %get-tuple-element.71.smooth_ref, f32[12,64,128]{2,1,0:T(8,128)S(1)} %get-tuple-element.72.scale_ref, f32[2,3,64,128]{3,2,1,0:T(8,128)S(1)} %get-tuple-element.74.keep_ref, ...), custom_call_target="tpu_custom_call" | custom-call | tf_op jit(solution)/shard_map/observe/pallas_call | solution.py:660
  28.1 1.3 %collective-permute-start.5 = (bf16[128,128]{1,0:T(8,128)(2,1)S(1)}, bf16[128,128]{1,0:T(8,128)(2,1)S(1)}, u32[]{:S(2)}, u32[]{:S(2)}) collective-permute-start(bf16[128,128]{1,0:T(8,128)(2,1)S(1)} %get-tuple-element.86), channel_id=1, source_target_pairs={{1,2},{2,1},{3,4},{4,3},{5,6},{6,5},{7,0},{0,7},{9,10},{10,9},{11,... | collective-permute-start | bytes 98312 | tf_op jit(solution)/shard_map/ppermute | solution.py:686
  29.4 0.0 collective-permute-start.6
  29.4 3.8 %collective-permute-done.5.a_ref = bf16[128,128]{1,0:T(8,128)(2,1)S(1)} collective-permute-done((bf16[128,128]{1,0:T(8,128)(2,1)S(1)}, bf16[128,128]{1,0:T(8,128)(2,1)S(1)}, u32[]{:S(2)}, u32[]{:S(2)}) %collective-permute-start.5) | collective-permute-done | bytes 32800 | tf_op jit(solution)/shard_map/ppermute | solution.py:686
  33.1 0.0 collective-permute-done.6.b_ref
  33.1 0.1 next_columns.1
  33.3 1.9 %collective-permute-start.7 = (bf16[96,128]{1,0:T(8,128)(2,1)S(1)}, bf16[96,128]{1,0:T(8,128)(2,1)S(1)}, u32[]{:S(2)}, u32[]{:S(2)}) collective-permute-start(bf16[96,128]{1,0:T(8,128)(2,1)S(1)} %get-tuple-element.88), channel_id=1, source_target_pairs={{8,16},{16,8},{24,32},{32,24},{40,48},{48,40},{56,64},{64,56},{72,... | collective-permute-start | bytes 73736 | tf_op jit(solution)/shard_map/ppermute | solution.py:686
  35.2 0.0 collective-permute-start.8
  35.2 3.2 %next_interior.1 = (f32[12,64,128]{2,1,0:T(8,128)S(1)}, f32[4,96,128]{2,1,0:T(8,128)S(1)}, f32[10,112,128]{2,1,0:T(8,128)S(1)}, f32[10,112,128]{2,1,0:T(8,128)S(...) custom-call(f32[12,96,128]{2,1,0:T(8,128)S(1)} %get-tuple-element.90.turned_ref, ...), custom_call_target="tpu_custom_call" | custom-call | flops 10000000 | bytes 1000000 | tf_op jit(solution)/shard_map/next_interior/pallas_call | solution.py:660
  38.4 1.3 %collective-permute-done.7.first_ref = bf16[96,128]{1,0:T(8,128)(2,1)S(1)} collective-permute-done((bf16[96,128]{1,0:T(8,128)(2,1)S(1)}, bf16[96,128]{1,0:T(8,128)(2,1)S(1)}, u32[]{:S(2)}, u32[]{:S(2)}) %collective-permute-start.7) | collective-permute-done | bytes 24608 | tf_op jit(solution)/shard_map/ppermute | solution.py:686
  39.7 0.0 collective-permute-done.8.second_ref
  39.7 2.2 %gradient.1 = f32[2,6,64,128]{3,2,1,0:T(8,128)} custom-call(bf16[96,128]{1,0:T(8,128)(2,1)S(1)} %collective-permute-done.7.first_ref, bf16[96,128]{1,0:T(8,128)(2,1)S(1)} %collective-permute-done.8.second_ref, f32[4,96,128]{2,1,0:T(8,128)S(1)} %get-tuple-element.93.bands_ref, f32[10,112,128]{2,1,0:T(8,128)S(1)} %get-tuple-element.94.record_0, ...), custom_call_target="tpu_custom_call" | custom-call | tf_op jit(solution)/shard_map/gradient/pallas_call | solution.py:660
  (1 shorter events, 0.0 us)
Async XLA Ops:
  0.0 6.3 %copy-start.1 = (f32[4,3,64,128]{3,2,1,0:T(8,128)S(1)}, f32[4,3,64,128]{3,2,1,0:T(8,128)}, u32[]{:S(2)}) copy-start(f32[4,3,64,128]{3,2,1,0:T(8,128)} %model_ref.1) | copy-start | bytes 1179652
  0.0 1.1 %copy-start.3 = (s32[64,128]{1,0:T(8,128)S(1)}, s32[64,128]{1,0:T(8,128)}, u32[]{:S(2)}) copy-start(s32[64,128]{1,0:T(8,128)} %bottom_ref.3) | copy-start | bytes 98308
  0.0 6.3 %copy-start.2 = (f32[2,6,64,128]{3,2,1,0:T(8,128)S(1)}, f32[2,6,64,128]{3,2,1,0:T(8,128)}, u32[]{:S(2)}) copy-start(f32[2,6,64,128]{3,2,1,0:T(8,128)} %refs_2_.1) | copy-start | bytes 1179652
  1.1 5.2 %copy-start.6 = (f32[1,1,1,256]{3,2,1,0:T(1,128)S(1)}, f32[1,1,1,256]{3,2,1,0:T(1,128)}, u32[]{:S(2)}) copy-start(f32[1,1,1,256]{3,2,1,0:T(1,128)} %refs_6_.1) | copy-start | bytes 3076
  1.1 5.2 %copy-start.7 = (f32[1,1,1,256]{3,2,1,0:T(1,128)S(1)}, f32[1,1,1,256]{3,2,1,0:T(1,128)}, u32[]{:S(2)}) copy-start(f32[1,1,1,256]{3,2,1,0:T(1,128)} %refs_7_.1) | copy-start | bytes 3076
  1.2 5.1 %copy-start.4 = (f32[1,1,1,4,256]{4,3,2,1,0:T(4,128)S(1)}, f32[1,1,1,4,256]{4,3,2,1,0:T(4,128)}, u32[]{:S(2)}) copy-start(f32[1,1,1,4,256]{4,3,2,1,0:T(4,128)} %refs_5_.1) | copy-start | bytes 12292
  1.2 6.4 %collective-permute-start = (bf16[160,128]{1,0:T(8,128)(2,1)S(1)}, bf16[160,128]{1,0:T(8,128)(2,1)S(1)}, u32[]{:S(2)}, u32[]{:S(2)}) collective-permute-start(bf16[160,128]{1,0:T(8,128)(2,1)S(1)} %get-tuple-element.57), channel_id=1, source_target_pairs={{1,2},{2,1},{3,4},{4,3},{5,6},{6,5},{7,0},{0,7},{9,10},{10,9},{11,... | collective-permute-start | bytes 122888 | tf_op jit(solution)/shard_map/ppermute | solution.py:686
  5.6 0.7 %copy-start.5 = (s32[1,1,1,256]{3,2,1,0:T(1,128)S(1)}, s32[1,1,1,256]{3,2,1,0:T(1,128)}, u32[]{:S(2)}) copy-start(s32[1,1,1,256]{3,2,1,0:T(1,128)} %refs_4_.1) | copy-start | bytes 3076
  5.6 2.9 %collective-permute-start.1 = (bf16[160,128]{1,0:T(8,128)(2,1)S(1)}, bf16[160,128]{1,0:T(8,128)(2,1)S(1)}, u32[]{:S(2)}, u32[]{:S(2)}) collective-permute-start(bf16[160,128]{1,0:T(8,128)(2,1)S(1)} %get-tuple-element.58), channel_id=1, source_target_pairs={{0,1},{1,0},{2,3},{3,2},{4,5},{5,4},{6,7},{7,6},{8,9},{9,8},{10,11... | collective-permute-start | bytes 122888 | tf_op jit(solution)/shard_map/ppermute | solution.py:686
  6.3 2.1 %copy-start = (f32[2,6,64,128]{3,2,1,0:T(8,128)S(1)}, f32[2,6,64,128]{3,2,1,0:T(8,128)}, u32[]{:S(2)}) copy-start(f32[2,6,64,128]{3,2,1,0:T(8,128)} %control_ref.5) | copy-start | bytes 1179652
  8.8 12.0 %collective-permute-start.2 = (bf16[96,256]{1,0:T(8,128)(2,1)S(1)}, bf16[96,256]{1,0:T(8,128)(2,1)S(1)}, u32[]{:S(2)}, u32[]{:S(2)}) collective-permute-start(bf16[96,256]{1,0:T(8,128)(2,1)S(1)} %get-tuple-element.59), channel_id=1, source_target_pairs={{8,16},{16,8},{24,32},{32,24},{40,48},{48,40},{56,64},{64,56},{72,... | collective-permute-start | bytes 147464 | tf_op jit(solution)/shard_map/ppermute | solution.py:686
  17.2 4.4 %collective-permute-start.3 = (bf16[96,256]{1,0:T(8,128)(2,1)S(1)}, bf16[96,256]{1,0:T(8,128)(2,1)S(1)}, u32[]{:S(2)}, u32[]{:S(2)}) collective-permute-start(bf16[96,256]{1,0:T(8,128)(2,1)S(1)} %get-tuple-element.60), channel_id=1, source_target_pairs={{0,8},{8,0},{16,24},{24,16},{32,40},{40,32},{48,56},{56,48},{64,72... | collective-permute-start | bytes 147464 | tf_op jit(solution)/shard_map/ppermute | solution.py:686
  21.9 4.9 %collective-permute-start.4 = (f32[2,3,64,128]{3,2,1,0:T(8,128)S(1)}, f32[2,3,64,128]{3,2,1,0:T(8,128)S(1)}, u32[]{:S(2)}, u32[]{:S(2)}) collective-permute-start(f32[2,3,64,128]{3,2,1,0:T(8,128)S(1)} %get-tuple-element.75), channel_id=1, source_target_pairs={{0,128},{128,0},{1,129},{129,1},{2,130},{130,2},{3,131},{131,3},{4... | collective-permute-start | bytes 589832 | tf_op jit(solution)/shard_map/ppermute | solution.py:768
  28.1 5.1 %collective-permute-start.5 = (bf16[128,128]{1,0:T(8,128)(2,1)S(1)}, bf16[128,128]{1,0:T(8,128)(2,1)S(1)}, u32[]{:S(2)}, u32[]{:S(2)}) collective-permute-start(bf16[128,128]{1,0:T(8,128)(2,1)S(1)} %get-tuple-element.86), channel_id=1, source_target_pairs={{1,2},{2,1},{3,4},{4,3},{5,6},{6,5},{7,0},{0,7},{9,10},{10,9},{11,... | collective-permute-start | bytes 98312 | tf_op jit(solution)/shard_map/ppermute | solution.py:686
  29.4 3.8 %collective-permute-start.6 = (bf16[128,128]{1,0:T(8,128)(2,1)S(1)}, bf16[128,128]{1,0:T(8,128)(2,1)S(1)}, u32[]{:S(2)}, u32[]{:S(2)}) collective-permute-start(bf16[128,128]{1,0:T(8,128)(2,1)S(1)} %get-tuple-element.87), channel_id=1, source_target_pairs={{0,1},{1,0},{2,3},{3,2},{4,5},{5,4},{6,7},{7,6},{8,9},{9,8},{10,11... | collective-permute-start | bytes 98312 | tf_op jit(solution)/shard_map/ppermute | solution.py:686
  33.3 6.4 %collective-permute-start.7 = (bf16[96,128]{1,0:T(8,128)(2,1)S(1)}, bf16[96,128]{1,0:T(8,128)(2,1)S(1)}, u32[]{:S(2)}, u32[]{:S(2)}) collective-permute-start(bf16[96,128]{1,0:T(8,128)(2,1)S(1)} %get-tuple-element.88), channel_id=1, source_target_pairs={{8,16},{16,8},{24,32},{32,24},{40,48},{48,40},{56,64},{64,56},{72,... | collective-permute-start | bytes 73736 | tf_op jit(solution)/shard_map/ppermute | solution.py:686
  35.2 4.5 %collective-permute-start.8 = (bf16[96,128]{1,0:T(8,128)(2,1)S(1)}, bf16[96,128]{1,0:T(8,128)(2,1)S(1)}, u32[]{:S(2)}, u32[]{:S(2)}) collective-permute-start(bf16[96,128]{1,0:T(8,128)(2,1)S(1)} %get-tuple-element.89), channel_id=1, source_target_pairs={{0,8},{8,0},{16,24},{24,16},{32,40},{40,32},{48,56},{56,48},{64,72... | collective-permute-start | bytes 73736 | tf_op jit(solution)/shard_map/ppermute | solution.py:686
